TPU v7x, 128 devices: a whole 4x4x4 slice. The times are simulated.
128 devices in a mesh: seq: 64 (over z, y_hi, x, core), tp: 2 (over y_lo).
Axes of the slice: x: 4, y: 4 (y_hi: 2, y_lo: 2; y = y_hi * 2 + y_lo), z: 4, core: 2. Of those that a mesh axis runs over, the one named last changes fastest.
Arguments:
- hidden_in: float32 [8192, 1536], P(('seq', 'tp')), as said below
- cotangent: float32 [8192, 1536], P(('seq', 'tp')), may hold values from -6 to 6
- needle_mask: int32 [8192], P(('seq', 'tp')), may hold values 0 or 1
- attn_gain: float32 [1536], replicated, as said below
- lambdas: float32 [4, 12, 64], replicated, may hold values from -0.625 to 0.625
- subln_gain: float32 [128], replicated, may hold values from 0.1 to 1.9
- ffn_gain: float32 [1536], replicated, may hold values from 0.1 to 1.9
- weight_query: bfloat16 [1536, 1536], P(None, 'tp'), as said below
- weight_key: bfloat16 [1536, 1536], P(None, 'tp'), as said below
- weight_value: bfloat16 [1536, 1536], P(None, 'tp'), may hold values from -0.15625 to 0.15625
- weight_out: bfloat16 [1536, 1536], P(None, 'tp'), may hold values from -0.75 to 0.75
- weight_gate: bfloat16 [1536, 4096], P(None, 'tp'), may hold values from -0.15625 to 0.15625
- weight_up: bfloat16 [1536, 4096], P(None, 'tp'), may hold values from -0.15625 to 0.15625
- weight_down: bfloat16 [1536, 4096], P(None, 'tp'), may hold values from -0.09375 to 0.09375
Outputs:
- output: float32 [8192, 1536], P(('seq', 'tp'))
- grad_input: float32 [8192, 1536], P(('seq', 'tp'))
- grad_query: float32 [1536, 1536], P('seq', 'tp')
- grad_key: float32 [1536, 1536], P('seq', 'tp')
- grad_value: float32 [1536, 1536], P('seq', 'tp')
- grad_out_proj: float32 [1536, 1536], P('seq', 'tp')
- grad_gate: float32 [1536, 4096], P('seq', 'tp')
- grad_up: float32 [1536, 4096], P('seq', 'tp')
- grad_down: float32 [1536, 4096], P('seq', 'tp')
- grad_attn_gain: float32 [1536], replicated
- grad_lambdas: float32 [4, 12, 64], replicated
- grad_subln_gain: float32 [128], replicated
- grad_ffn_gain: float32 [1536], replicated
Inputs may be any that keep to these rules, and one draw needn't show every extreme that they name: `hidden_in`: entries of order one, independent. `attn_gain`: entries about 1, each within 0.1 to 1.9. `weight_query`: independent entries of deviation about 1 / sqrt(1536). `weight_key`: independent entries of deviation about 1 / sqrt(1536).
All inputs are finite; a program needn't handle non-finite values. No bound on the sum of `needle_mask` on one device may be relied on, other than what follows from the above.
Results may differ from a plain program's by a relative error of at most 0.017.
Values may be sent and summed in bfloat16 or wider, within the bound.
A program may use at most 256 MiB of HBM per device.

v0:
```python
import math

import jax
import jax.numpy as jnp
from jax import lax
from jax.sharding import PartitionSpec as P

eps = 1e-06
lambda_init = 0.8 - 0.6 * math.exp(-3.6)


def from_behind(block, axis, distance):
    devices = range(lax.axis_size(axis))
    route = [((i - distance) % len(devices), i) for i in devices]
    return lax.ppermute(block, axis, route)


def rms_scale(values):
    return lax.rsqrt(jnp.mean(values * values, axis=-1, keepdims=True) + eps)


def norm_back(grad_normed, gain, rms, normed_hat):
    scaled = grad_normed * gain
    return rms * (scaled - normed_hat * jnp.mean(scaled * normed_hat, axis=-1, keepdims=True))


def row_product(left, right):
    return lax.dot_general(
        left, right, (((0,), (0,)), ((), ())), preferred_element_type=jnp.float32
    )


def times_transpose(left, right):
    return lax.dot_general(
        left, right, (((1,), (1,)), ((), ())), preferred_element_type=jnp.float32
    )


def block_scores(query_heads, key_heads, offset, half):
    return jnp.einsum(
        "qhd,khd->hqk",
        query_heads[..., offset : offset + half],
        key_heads[..., offset : offset + half],
        preferred_element_type=jnp.float32,
    ) * half ** (-0.5)


def block_grads(
    query_heads, differ_low, stats, key_heads, value_heads, query_first, key_first, lambda_value
):
    first_total, second_total, first_delta, second_delta = stats
    half = key_heads.shape[-1] // 2
    query_pos = query_first + jnp.arange(query_heads.shape[0], dtype=jnp.int32)
    key_pos = key_first + jnp.arange(key_heads.shape[0], dtype=jnp.int32)
    visible = (key_pos[None, :] <= query_pos[:, None])[None]
    upstream = jnp.einsum(
        "qhd,khd->hqk", differ_low, value_heads, preferred_element_type=jnp.float32
    )
    query_parts = []
    key_parts = []
    value_parts = []
    for offset, log_total, delta, factor in (
        (0, first_total, first_delta, jnp.ones_like(lambda_value)),
        (half, second_total, second_delta, -lambda_value),
    ):
        scores = block_scores(query_heads, key_heads, offset, half)
        probability = jnp.where(visible, jnp.exp(scores - log_total[..., None]), 0.0)
        score_grad = (probability * (factor[:, None, None] * upstream - delta[..., None])).astype(
            jnp.bfloat16
        )
        query_parts.append(
            jnp.einsum(
                "hqk,khd->qhd",
                score_grad,
                key_heads[..., offset : offset + half],
                preferred_element_type=jnp.float32,
            )
        )
        key_parts.append(
            jnp.einsum(
                "hqk,qhd->khd",
                score_grad,
                query_heads[..., offset : offset + half],
                preferred_element_type=jnp.float32,
            )
        )
        value_parts.append(
            jnp.einsum(
                "hqk,qhd->khd",
                probability.astype(jnp.bfloat16),
                differ_low,
                preferred_element_type=jnp.float32,
            )
            * factor[None, :, None]
        )
    return (
        jnp.concatenate(query_parts, axis=-1),
        jnp.concatenate(key_parts, axis=-1),
        value_parts[0] + value_parts[1],
    )


def on_device(
    hidden_in,
    cotangent,
    needle_mask,
    attn_gain,
    lambdas,
    subln_gain,
    ffn_gain,
    weight_query,
    weight_key,
    weight_value,
    weight_out,
    weight_gate,
    weight_up,
    weight_down,
):
    half = lambdas.shape[2]
    head_width = 2 * half
    heads = weight_query.shape[1] // head_width
    cycle_index = lax.axis_index("seq")
    cycle_size = lax.axis_size("seq")
    head_first = lax.axis_index("tp") * heads
    attn_rms = rms_scale(hidden_in)
    attn_hat = hidden_in * attn_rms
    normed = (attn_hat * attn_gain).astype(jnp.bfloat16)
    normed_all = lax.all_gather(normed, "tp", axis=0, tiled=True)
    block_rows = normed_all.shape[0]
    first_row = cycle_index * block_rows
    query = jnp.dot(normed_all, weight_query, preferred_element_type=jnp.float32).astype(
        jnp.bfloat16
    )
    keys = jnp.dot(normed_all, weight_key, preferred_element_type=jnp.float32).astype(jnp.bfloat16)
    values = jnp.dot(normed_all, weight_value, preferred_element_type=jnp.float32).astype(
        jnp.bfloat16
    )
    query_heads = query.reshape(block_rows, heads, head_width)
    local_lambdas = lax.dynamic_slice_in_dim(lambdas, head_first, heads, axis=1)
    first_exp = jnp.exp(jnp.sum(local_lambdas[0] * local_lambdas[1], axis=-1))
    second_exp = jnp.exp(jnp.sum(local_lambdas[2] * local_lambdas[3], axis=-1))
    lambda_value = first_exp - second_exp + lambda_init
    query_pos = first_row + jnp.arange(block_rows, dtype=jnp.int32)
    minus = jnp.full((heads, block_rows), -jnp.inf, jnp.float32)
    zero_total = jnp.zeros((heads, block_rows), jnp.float32)
    piece = lax.all_gather(keys, "seq", axis=0, tiled=True)
    count = piece.shape[0]

    def stat_update(state):
        key_part = piece.reshape(count, heads, head_width)
        key_pos = jnp.arange(count, dtype=jnp.int32)
        visible = (key_pos[None, :] <= query_pos[:, None])[None]
        result = []
        for index, offset in enumerate((0, half)):
            running, total = state[2 * index : 2 * index + 2]
            scores = jnp.where(visible, block_scores(query_heads, key_part, offset, half), -jnp.inf)
            peak = jnp.max(scores, axis=-1)
            safe_peak = jnp.where(jnp.isfinite(peak), peak, 0.0)
            total = total * jnp.exp(running - safe_peak) + jnp.sum(
                jnp.exp(scores - safe_peak[..., None]), axis=-1
            )
            result += [peak, total]
        return tuple(result)

    stats_out = lax.cond(
        jnp.int32(0) <= first_row + block_rows - 1,
        stat_update,
        lambda state: state,
        (minus, zero_total, minus, zero_total),
    )
    first_log = stats_out[0] + jnp.log(stats_out[1])
    second_log = stats_out[2] + jnp.log(stats_out[3])
    zero_accum = jnp.zeros((heads, block_rows, head_width), jnp.float32)
    key_piece = lax.all_gather(keys, "seq", axis=0, tiled=True)
    value_piece = lax.all_gather(values, "seq", axis=0, tiled=True)
    absorb_count = key_piece.shape[0]

    def absorb_update(state):
        key_part = key_piece.reshape(absorb_count, heads, head_width)
        value_part = value_piece.reshape(absorb_count, heads, head_width)
        key_pos = jnp.arange(absorb_count, dtype=jnp.int32)
        visible = (key_pos[None, :] <= query_pos[:, None])[None]
        result = []
        for index, (offset, log_total) in enumerate(((0, first_log), (half, second_log))):
            scores = block_scores(query_heads, key_part, offset, half)
            weights = jnp.where(visible, jnp.exp(scores - log_total[..., None]), 0.0)
            result.append(
                state[index]
                + jnp.einsum(
                    "hqk,khd->hqd",
                    weights.astype(jnp.bfloat16),
                    value_part,
                    preferred_element_type=jnp.float32,
                )
            )
        return tuple(result)

    folded = lax.cond(
        jnp.int32(0) <= first_row + block_rows - 1,
        absorb_update,
        lambda state: state,
        (zero_accum, zero_accum),
    )
    first_part = folded[0]
    second_part = folded[1]
    differ = first_part - lambda_value[:, None, None] * second_part
    group_rms = rms_scale(differ)
    group_hat = differ * group_rms
    out_scale = 1.0 - lambda_init
    mixed = (
        jnp.transpose(group_hat * subln_gain * out_scale, (1, 0, 2))
        .reshape(block_rows, heads * head_width)
        .astype(jnp.bfloat16)
    )
    resid = hidden_in + lax.psum_scatter(
        times_transpose(mixed, weight_out).astype(jnp.bfloat16),
        "tp",
        scatter_dimension=0,
        tiled=True,
    ).astype(jnp.float32)
    ffn_rms = rms_scale(resid)
    ffn_hat = resid * ffn_rms
    ffn_normed = (ffn_hat * ffn_gain).astype(jnp.bfloat16)
    dout = cotangent * needle_mask.astype(jnp.float32)[:, None]
    ffn_all, dout_all = (
        lax.all_gather(ffn_normed, "tp", axis=0, tiled=True),
        lax.all_gather(dout.astype(jnp.bfloat16), "tp", axis=0, tiled=True),
    )
    gate = jnp.dot(ffn_all, weight_gate, preferred_element_type=jnp.float32)
    up_values = jnp.dot(ffn_all, weight_up, preferred_element_type=jnp.float32)
    sigmoid_gate = jax.nn.sigmoid(gate)
    silu_gate = gate * sigmoid_gate
    hidden = (silu_gate * up_values).astype(jnp.bfloat16)
    output = resid + lax.psum_scatter(
        times_transpose(hidden, weight_down).astype(jnp.bfloat16),
        "tp",
        scatter_dimension=0,
        tiled=True,
    ).astype(jnp.float32)
    d_hidden = jnp.dot(dout_all, weight_down, preferred_element_type=jnp.float32)
    grad_down = row_product(dout_all, hidden)
    d_gate = (d_hidden * up_values * sigmoid_gate * (1.0 + gate * (1.0 - sigmoid_gate))).astype(
        jnp.bfloat16
    )
    d_up = (d_hidden * silu_gate).astype(jnp.bfloat16)
    grad_gate = row_product(ffn_all, d_gate)
    grad_up = row_product(ffn_all, d_up)
    d_ffn_normed = lax.psum_scatter(
        times_transpose(d_gate, weight_gate) + times_transpose(d_up, weight_up),
        "tp",
        scatter_dimension=0,
        tiled=True,
    )
    ffn_gain_part = jnp.sum(d_ffn_normed * ffn_hat, axis=0)
    d_resid = dout + norm_back(d_ffn_normed, ffn_gain, ffn_rms, ffn_hat)
    resid_all = lax.all_gather(d_resid.astype(jnp.bfloat16), "tp", axis=0, tiled=True)
    grad_out_proj = row_product(resid_all, mixed)
    d_mixed = jnp.dot(resid_all, weight_out, preferred_element_type=jnp.float32)
    scaled_grad = (
        jnp.transpose(d_mixed.reshape(block_rows, heads, head_width), (1, 0, 2)) * out_scale
    )
    subln_part = jnp.sum(scaled_grad * group_hat, axis=(0, 1))
    d_differ = norm_back(scaled_grad, subln_gain, group_rms, group_hat).astype(jnp.bfloat16)
    differ_grad = d_differ.astype(jnp.float32)
    second_dot = jnp.sum(differ_grad * second_part, axis=-1)
    d_lambda = -jnp.sum(second_dot, axis=-1)
    first_delta = jnp.sum(differ_grad * first_part, axis=-1)
    second_delta = -lambda_value[:, None] * second_dot
    lambda_part = jnp.stack(
        [
            (d_lambda * first_exp)[:, None] * local_lambdas[1],
            (d_lambda * first_exp)[:, None] * local_lambdas[0],
            -(d_lambda * second_exp)[:, None] * local_lambdas[3],
            -(d_lambda * second_exp)[:, None] * local_lambdas[2],
        ]
    )
    lambda_grads = lax.dynamic_update_slice_in_dim(
        jnp.zeros(lambdas.shape, jnp.float32), lambda_part, head_first, axis=1
    )
    differ_low = jnp.transpose(d_differ, (1, 0, 2))
    flat_width = heads * head_width
    zero_grads = jnp.zeros((block_rows, flat_width), jnp.float32)
    stats = (first_log, second_log, first_delta, second_delta)

    def key_turn(turn, carry):
        key_piece, value_piece, key_acc, value_acc, query_acc = carry
        source = (cycle_index - turn) % cycle_size

        def contribute(sums):
            query_c, key_c, value_c = block_grads(
                query_heads,
                differ_low,
                stats,
                key_piece.astype(jnp.bfloat16).reshape(block_rows, heads, head_width),
                value_piece.astype(jnp.bfloat16).reshape(block_rows, heads, head_width),
                first_row,
                source * block_rows,
                lambda_value,
            )
            return (
                sums[0] + query_c.reshape(block_rows, flat_width),
                sums[1] + key_c.reshape(block_rows, flat_width),
                sums[2] + value_c.reshape(block_rows, flat_width),
            )

        query_acc, key_acc, value_acc = lax.cond(
            source <= cycle_index, contribute, lambda sums: sums, (query_acc, key_acc, value_acc)
        )
        key_piece, value_piece, key_acc, value_acc = from_behind(
            (key_piece, value_piece, key_acc, value_acc), "seq", 1
        )
        return (key_piece, value_piece, key_acc, value_acc, query_acc)

    final = lax.fori_loop(
        0,
        cycle_size,
        key_turn,
        (keys.astype(jnp.float32), values.astype(jnp.float32), zero_grads, zero_grads, zero_grads),
    )
    key_sum, value_sum, query_sum = (final[2], final[3], final[4])
    query_grad = (query_sum * half ** (-0.5)).astype(jnp.bfloat16)
    key_grad = (key_sum * half ** (-0.5)).astype(jnp.bfloat16)
    value_grad = value_sum.astype(jnp.bfloat16)
    grad_query = row_product(normed_all, query_grad)
    grad_key = row_product(normed_all, key_grad)
    grad_value = row_product(normed_all, value_grad)
    d_normed = lax.psum_scatter(
        (
            times_transpose(query_grad, weight_query)
            + times_transpose(key_grad, weight_key)
            + times_transpose(value_grad, weight_value)
        ).astype(jnp.bfloat16),
        "tp",
        scatter_dimension=0,
        tiled=True,
    ).astype(jnp.float32)
    attn_gain_part = jnp.sum(d_normed * attn_hat, axis=0)
    grad_input = d_resid + norm_back(d_normed, attn_gain, attn_rms, attn_hat)
    summed = (
        lax.psum_scatter(grad_query, "seq", scatter_dimension=0, tiled=True),
        lax.psum_scatter(grad_key, "seq", scatter_dimension=0, tiled=True),
        lax.psum_scatter(grad_value, "seq", scatter_dimension=0, tiled=True),
        lax.psum_scatter(grad_out_proj, "seq", scatter_dimension=0, tiled=True),
        lax.psum_scatter(grad_gate, "seq", scatter_dimension=0, tiled=True),
        lax.psum_scatter(grad_up, "seq", scatter_dimension=0, tiled=True),
        lax.psum_scatter(grad_down, "seq", scatter_dimension=0, tiled=True),
    )
    gains = lax.psum((attn_gain_part, lambda_grads, subln_part, ffn_gain_part), ("seq", "tp"))
    return (
        output,
        grad_input,
        summed[0],
        summed[1],
        summed[2],
        summed[3],
        summed[4],
        summed[5],
        summed[6],
        gains[0],
        gains[1],
        gains[2],
        gains[3],
    )


def solution(mesh):
    return jax.shard_map(
        on_device,
        mesh=mesh,
        in_specs=(
            P(("seq", "tp"), None),
            P(("seq", "tp"), None),
            P(("seq", "tp")),
            P(),
            P(),
            P(),
            P(),
            P(None, "tp"),
            P(None, "tp"),
            P(None, "tp"),
            P(None, "tp"),
            P(None, "tp"),
            P(None, "tp"),
            P(None, "tp"),
        ),
        out_specs=(
            P(("seq", "tp"), None),
            P(("seq", "tp"), None),
            P("seq", "tp"),
            P("seq", "tp"),
            P("seq", "tp"),
            P("seq", "tp"),
            P("seq", "tp"),
            P("seq", "tp"),
            P("seq", "tp"),
            P(),
            P(),
            P(),
            P(),
        ),
        check_vma=False,
    )
```

profile of v0, /device:TPU:31, one launch (start us, length us, event | category | flops | bytes accessed | tf_op | source)
XLA Modules:
  0.0 3839.6 jit_solution(2859734640996528073)
XLA Ops:
  26.3 89.1 %all-gather.3.cloned.1.call-done = bf16[8192,768]{1,0:T(8,128)(2,1)} async-done(((bf16[128,768]{1,0:T(8,128)(2,1)}), bf16[8192,768]{1,0:T(8,128)(2,1)}) %all-gather.3.cloned.1.call-update) | async-done | bytes 12582928 | tf_op jit(solution)/shard_map/all_gather | solution.py:174
  115.4 78.9 %conditional.3 = (f32[6,128]{1,0:T(8,128)}, f32[6,128]{1,0:T(8,128)}, f32[6,128]{1,0:T(8,128)S(1)}, f32[6,128]{1,0:T(8,128)S(1)}) conditional(s32[]{:T(128)} %convert_element_type.119, () %tuple.58, (s32[128]{0:T(128)S(1)}, bf16[128,6,128]{0,2,1:T(8,128)(2,1)}, bf16[8192,768]{1,0:T(8,128)(2,1)}) %tuple.59), branch_computations={%region_1.0_spmd, %region_2.7_spmd} | conditional | flops 1699749376 | bytes 166969888 | solution.py:165
  115.4 16.2 copy.52
  131.6 14.6 fusion.4
  146.9 23.7 fusion.1
  171.3 21.6 exponential_reduce_fusion
  196.3 14.5 all-gather.5.cloned.1.call-done
  210.7 61.4 %conditional.4 = (f32[6,128,128]{1,2,0:T(8,128)S(1)}, f32[6,128,128]{1,2,0:T(8,128)}) conditional(s32[]{:T(128)} %convert_element_type.119, () %tuple.57, (s32[128]{0:T(128)S(1)}, bf16[128,6,128]{0,2,1:T(8,128)(2,1)}, bf16[8192,768]{1,0:T(8,128)(2,1)}, f32[6,128]{1,0:T(8,128)S(1)}, bf16[8192,768]{1,0:T(8,128)(2,1)}, ...), branch_computations={%region_7.8_spmd, %region_8.9_spmd} | conditional | flops 4883218432 | bytes 93003280 | solution.py:198
  210.7 16.6 copy.54
  227.3 16.8 copy.55
  247.0 13.0 fusion.10
  328.0 12.2 reduce-scatter.16.cloned.1.call-done
  341.9 17.7 reduce-scatter.14.cloned.1.call-done
  374.0 2073.4 %while.23 = (s32[]{:T(128)}, bf16[128,768]{0,1:T(8,128)(2,1)}, bf16[128,768]{0,1:T(8,128)(2,1)}, f32[128,768]{0,1:T(8,128)}, f32[128,768]{0,1:T(8,128)}, /*index...) while((s32[]{:T(128)}, bf16[128,768]{0,1:T(8,128)(2,1)}, ...), condition=%wide.region_23.24_spmd, body=%wide.region_20.0_spmd.sunk | while | flops 153174288 | bytes 20122840 | solution.py:314
  376.6 14.4 conditional.6
  410.3 14.4 conditional.6
  447.7 14.4 conditional.6
  485.1 14.4 conditional.6
  522.6 14.4 conditional.6
  560.0 14.4 conditional.6
  597.5 14.4 conditional.6
  634.9 14.4 conditional.6
  672.3 14.4 conditional.6
  709.8 14.4 conditional.6
  747.2 14.4 conditional.6
  784.7 14.4 conditional.6
  822.1 14.4 conditional.6
  859.5 14.4 conditional.6
  897.0 14.4 conditional.6
  934.4 14.4 conditional.6
  971.9 21.4 collective-permute-start.2
  1101.3 16.8 collective-permute-start.2
  1143.8 15.4 collective-permute-start.3
  1181.4 15.5 collective-permute-start
  1220.4 20.6 collective-permute-start.1
  1269.5 16.9 collective-permute-start.2
  1344.7 14.1 collective-permute-start
  1384.6 20.6 collective-permute-start.1
  1433.7 15.9 collective-permute-start.2
  1478.1 16.3 collective-permute-start.3
  1517.4 12.7 collective-permute-start
  1557.4 20.6 collective-permute-start.1
  1606.4 15.9 collective-permute-start.2
  1766.9 16.3 collective-permute-start.3
  1816.2 13.1 collective-permute-start.1
  1846.1 20.6 collective-permute-start.1
  1939.6 16.3 collective-permute-start.3
  1987.6 14.5 collective-permute-start.1
  2018.9 20.6 collective-permute-start.1
  2078.3 13.0 collective-permute-start.3
  2112.4 16.3 collective-permute-start.3
  2158.9 15.9 collective-permute-start.1
  2191.7 20.6 collective-permute-start.1
  2251.1 13.0 collective-permute-start.3
  2427.6 16.9 collective-permute-start.1
  2494.2 160.5 %reduce-scatter.18.cloned.1.call-done = bf16[64,1536]{1,0:T(8,128)(2,1)} async-done(((bf16[128,1536]{1,0:T(8,128)(2,1)}), bf16[64,1536]{1,0:T(8,128)(2,1)}) %reduce-scatter.18.cloned.1.call-update) | async-done | bytes 196624 | tf_op jit(solution)/shard_map/reduce_scatter | solution.py:327
  2655.9 90.8 %all-reduce = (f32[1536]{0:T(1024)}, f32[4,12,64]{2,0,1:T(4,128)}, f32[128]{0:T(128)}, f32[1536]{0:T(1024)}) all-reduce(f32[1536]{0:T(1024)S(1)} %get-tuple-element.520, f32[4,12,64]{2,0,1:T(4,128)S(1)} %maximum_dynamic-update-slice_fusion, f32[128]{0:T(128)S(1)} %copy-done.36, ...), channel_id=1, replica_groups=mesh['seq'=64,'tp'=2] {'seq','tp'}, use_global_device_ids=true, to_apply=%region_34.35 | all-reduce | flops 6272 | bytes 50176 | tf_op jit(solution)/shard_map/psum | solution.py:348
  2748.6 61.3 %reduce-scatter.20.cloned.1.call-done = f32[24,768]{1,0:T(8,128)} async-done(((f32[1536,768]{1,0:T(8,128)}), f32[24,768]{1,0:T(8,128)}) %reduce-scatter.20.cloned.1.call-update) | async-done | bytes 73744 | tf_op jit(solution)/shard_map/reduce_scatter | solution.py:340
  2809.8 155.2 %reduce-scatter.22.cloned.1.call-done = f32[24,768]{1,0:T(8,128)} async-done(((f32[1536,768]{1,0:T(8,128)}), f32[24,768]{1,0:T(8,128)}) %reduce-scatter.22.cloned.1.call-update) | async-done | bytes 73744 | tf_op jit(solution)/shard_map/reduce_scatter | solution.py:341
  2965.0 155.2 %reduce-scatter.24.cloned.1.call-done = f32[24,768]{1,0:T(8,128)} async-done(((f32[1536,768]{1,0:T(8,128)}), f32[24,768]{1,0:T(8,128)}) %reduce-scatter.24.cloned.1.call-update) | async-done | bytes 73744 | tf_op jit(solution)/shard_map/reduce_scatter | solution.py:342
  3120.3 155.1 %reduce-scatter.26.cloned.1.call-done = f32[24,768]{1,0:T(8,128)} async-done(((f32[1536,768]{1,0:T(8,128)}), f32[24,768]{1,0:T(8,128)}) %reduce-scatter.26.cloned.1.call-update) | async-done | bytes 73744 | tf_op jit(solution)/shard_map/reduce_scatter | solution.py:343
  3275.4 186.1 %reduce-scatter.28.cloned.1.call-done = f32[24,2048]{1,0:T(8,128)} async-done(((f32[1536,2048]{1,0:T(8,128)}), f32[24,2048]{1,0:T(8,128)}) %reduce-scatter.28.cloned.1.call-update) | async-done | bytes 196624 | tf_op jit(solution)/shard_map/reduce_scatter | solution.py:344
  3461.5 186.1 %reduce-scatter.30.cloned.1.call-done = f32[24,2048]{1,0:T(8,128)} async-done(((f32[1536,2048]{1,0:T(8,128)}), f32[24,2048]{1,0:T(8,128)}) %reduce-scatter.30.cloned.1.call-update) | async-done | bytes 196624 | tf_op jit(solution)/shard_map/reduce_scatter | solution.py:345
  3647.6 185.2 %reduce-scatter.32.cloned.1.call-done = f32[24,2048]{1,0:T(8,128)} async-done(((f32[1536,2048]{1,0:T(8,128)}), f32[24,2048]{1,0:T(8,128)}) %reduce-scatter.32.cloned.1.call-update) | async-done | bytes 196624 | tf_op jit(solution)/shard_map/reduce_scatter | solution.py:346
  (1264 shorter events, 1812.2 us)
Async XLA Ops:
  7.2 108.2 %all-gather.3.cloned.1.call-start = ((), (), s32[]{:S(2)}) async-start(), calls=%async_computation.11 | async-start | bytes 12779520 | tf_op jit(solution)/shard_map/all_gather | solution.py:174
  19.7 191.0 %all-gather.5.cloned.1.call-start = ((), (), s32[]{:S(2)}) async-start(), calls=%async_computation.12 | async-start | bytes 12779520 | tf_op jit(solution)/shard_map/all_gather | solution.py:175
  22.6 269.1 %reduce-scatter.12.cloned.1.call-start = ((), (), s32[]{:S(2)}) async-start(), calls=%async_computation.13 | async-start | bytes 589824 | tf_op jit(solution)/shard_map/reduce_scatter | solution.py:215
  276.6 63.6 %reduce-scatter.16.cloned.1.call-start = ((), (), s32[]{:S(2)}) async-start(), calls=%async_computation.15 | async-start | bytes 1179648 | tf_op jit(solution)/shard_map/reduce_scatter | solution.py:248
  319.6 40.1 %reduce-scatter.14.cloned.1.call-start = ((), (), s32[]{:S(2)}) async-start(), calls=%async_computation.14 | async-start | bytes 589824 | tf_op jit(solution)/shard_map/reduce_scatter | solution.py:234
  325.6 2329.1 %reduce-scatter.18.cloned.1.call-start = ((), (), s32[]{:S(2)}) async-start(), calls=%async_computation.16 | async-start | bytes 589824 | tf_op jit(solution)/shard_map/reduce_scatter | solution.py:327
  971.9 26.5 collective-permute-start.2
  1101.3 30.1 collective-permute-start.2
  1136.8 31.1 collective-permute-start.2
  1143.8 24.8 collective-permute-start.3
  1173.4 31.1 collective-permute-start.2
  1180.4 24.8 collective-permute-start.3
  1209.9 31.1 collective-permute-start.2
  1216.9 24.8 collective-permute-start.3
  1217.9 24.6 collective-permute-start
  1269.5 30.2 collective-permute-start.2
  1305.1 25.2 collective-permute-start.2
  1335.8 32.0 collective-permute-start.2
  1342.8 25.7 collective-permute-start.3
  1344.7 24.6 collective-permute-start
  1373.2 32.0 collective-permute-start.2
  1380.2 25.7 collective-permute-start.3
  1382.1 24.6 collective-permute-start
  1433.7 32.0 collective-permute-start.2
  1471.1 32.0 collective-permute-start.2
  1478.1 25.7 collective-permute-start.3
  1508.6 32.0 collective-permute-start.2
  1515.5 25.7 collective-permute-start.3
  1546.0 32.0 collective-permute-start.2
  1553.0 25.7 collective-permute-start.3
  1606.4 32.0 collective-permute-start.2
  1759.9 32.0 collective-permute-start.2
  1766.9 25.7 collective-permute-start.3
  1797.3 32.0 collective-permute-start.2
  1804.3 25.7 collective-permute-start.3
  1806.2 24.6 collective-permute-start
  1834.8 32.0 collective-permute-start.2
  1841.8 25.7 collective-permute-start.3
  1843.7 24.6 collective-permute-start
  1895.2 32.0 collective-permute-start.2
  1932.6 32.0 collective-permute-start.2
  1939.6 25.7 collective-permute-start.3
  1970.1 32.0 collective-permute-start.2
  1977.1 25.7 collective-permute-start.3
  1979.0 24.6 collective-permute-start
  2007.5 32.0 collective-permute-start.2
  2014.5 25.7 collective-permute-start.3
  2016.4 24.6 collective-permute-start
  2068.0 32.0 collective-permute-start.2
  2105.4 32.0 collective-permute-start.2
  2112.4 25.7 collective-permute-start.3
  2142.9 32.0 collective-permute-start.2
  2149.8 25.7 collective-permute-start.3
  2180.3 32.0 collective-permute-start.2
  2187.3 25.7 collective-permute-start.3
  2240.7 32.0 collective-permute-start.2
  2416.2 28.3 collective-permute-start.2
  2455.7 354.2 %reduce-scatter.20.cloned.1.call-start = ((), (), s32[]{:S(2)}) async-start(), calls=%async_computation.17 | async-start | bytes 4792320 | tf_op jit(solution)/shard_map/reduce_scatter | solution.py:340
  2459.7 505.3 %reduce-scatter.22.cloned.1.call-start = ((), (), s32[]{:S(2)}) async-start(), calls=%async_computation.18 | async-start | bytes 4792320 | tf_op jit(solution)/shard_map/reduce_scatter | solution.py:341
  2463.9 656.4 %reduce-scatter.24.cloned.1.call-start = ((), (), s32[]{:S(2)}) async-start(), calls=%async_computation.19 | async-start | bytes 4792320 | tf_op jit(solution)/shard_map/reduce_scatter | solution.py:342
  2467.9 807.5 %reduce-scatter.26.cloned.1.call-start = ((), (), s32[]{:S(2)}) async-start(), calls=%async_computation.20 | async-start | bytes 4792320 | tf_op jit(solution)/shard_map/reduce_scatter | solution.py:343
  2470.9 990.6 %reduce-scatter.28.cloned.1.call-start = ((), (), s32[]{:S(2)}) async-start(), calls=%async_computation.21 | async-start | bytes 12779520 | tf_op jit(solution)/shard_map/reduce_scatter | solution.py:344
  2478.4 1169.2 %reduce-scatter.30.cloned.1.call-start = ((), (), s32[]{:S(2)}) async-start(), calls=%async_computation.22 | async-start | bytes 12779520 | tf_op jit(solution)/shard_map/reduce_scatter | solution.py:345
  2485.8 1347.0 %reduce-scatter.32.cloned.1.call-start = ((), (), s32[]{:S(2)}) async-start(), calls=%async_computation.23 | async-start | bytes 12779520 | tf_op jit(solution)/shard_map/reduce_scatter | solution.py:346
  (248 other events, 4504.9 us)
Sparse Core Ops, SparseCore 0:
  19.8 95.5 all-gather.2
  119.2 91.4 all-gather.4
  276.7 14.9 reduce-scatter.11
  319.7 20.4 reduce-scatter.15
  343.0 16.6 reduce-scatter.13
  2455.8 198.8 reduce-scatter.17
  2660.7 149.0 reduce-scatter.19
  2815.8 149.1 reduce-scatter.21
  2971.0 149.2 reduce-scatter.23
  3126.1 149.2 reduce-scatter.25
  3281.9 179.5 reduce-scatter.27
  3468.8 178.7 reduce-scatter.29
  3654.1 178.6 reduce-scatter.31
where the time goes:
time: 3880 us; the launch traced here: 3840 us
  waiting for transfers between devices  1660 us (43%)
  starting transfers between devices  1300 us (34%)
  local copies, waits for them, and re-layouts  351 us (9%)
  matrix products  265 us (7%)
  other arithmetic  123 us (3%)
  blocking collectives  118 us (3%)
    ppermute x256, starting transfers between devices, from_behind(): return lax.ppermute(block, axis, route)  1300 us
    ppermute x256, waiting for transfers between devices, from_behind(): return lax.ppermute(block, axis, route)  281 us
    another operation x132, local copies, waits for them, and re-layouts  213 us
    reduce_scatter x1, waiting for transfers between devices, on_device(): lax.psum_scatter(grad_up, 'seq', scatter_dimension=0, tiled=True)  186 us
    reduce_scatter x1, waiting for transfers between devices, on_device(): lax.psum_scatter(grad_gate, 'seq', scatter_dimension=0, tiled=True)  186 us
    reduce_scatter x1, waiting for transfers between devices, on_device(): lax.psum_scatter(grad_down, 'seq', scatter_dimension=0, tiled=True)  185 us
    reduce_scatter x1, waiting for transfers between devices, on_device(): lax.psum_scatter((times_transpose(query_grad, weight_query) + times_trans...  160 us
    reduce_scatter x1, waiting for transfers between devices, on_device(): lax.psum_scatter(grad_value, 'seq', scatter_dimension=0, tiled=True)  155 us
  transfers between devices with their start and end apart: 269, of which 135 were waited for; matrix products, arithmetic and copies ran while one was open for 6% of the time, Pallas kernels for 0%

commit v1 on v0

v1 whole, which is shorter than its diff:
```python
import math

import jax
import jax.numpy as jnp
from jax import lax
from jax.experimental import pallas as pl
from jax.experimental.pallas import tpu as pltpu
from jax.sharding import PartitionSpec as P

MESH = pl.DeviceIdType.MESH
BF = jnp.bfloat16
F32 = jnp.float32
EPS = 1e-06
LAMBDA_INIT = 0.8 - 0.6 * math.exp(-3.6)
OUT_SCALE = 1.0 - LAMBDA_INIT
D = 1536
CHIPS = 32
SERVED = 30
PER_HEAD = 5
ROWS = 64
BLOCK = 256
TILE = 128
SLOTS = 7
KB = 512
LOG2E = 1.4426950408889634
SCORE = 0.125 * LOG2E
VMEM_LIMIT = 60 * 2**20


def place():
    s = lax.axis_index("seq")
    return s // 2, s % 2, lax.axis_index("tp")


def owner_of(tile):
    step = (tile - 4) // 10
    pos = (tile - 4) % 10
    slot = jnp.where(step % 2 == 0, pos, 9 - pos)
    early = tile < 4
    return jnp.where(early, tile, slot), jnp.where(early, 0, step + 1)


def tile_of(slot, r):
    if r == 0:
        return slot
    return 4 + 10 * (r - 1) + (slot if (r - 1) % 2 == 0 else 9 - slot)


def matmul(a, b):
    return jnp.dot(a, b, preferred_element_type=F32)


def matmul_t(a, b):
    return lax.dot_general(a, b, (((1,), (1,)), ((), ())), preferred_element_type=F32)


def rms_scale(values, axis=-1):
    return lax.rsqrt(jnp.mean(values * values, axis=axis, keepdims=True) + EPS)


def norm_back(grad_normed, gain, rms, hat, axis=-1):
    scaled = grad_normed * gain
    return rms * (scaled - hat * jnp.mean(scaled * hat, axis=axis, keepdims=True))


def greet_all(chip, core, t):
    barrier = pltpu.get_barrier_semaphore()
    s = 2 * chip + core

    def greet(o, carry):
        pl.semaphore_signal(
            barrier, inc=1, device_id=(lax.rem(s + o, 2 * CHIPS), t), device_id_type=MESH
        )
        return carry

    lax.fori_loop(1, 2 * CHIPS, greet, 0)
    pl.semaphore_signal(barrier, inc=1, device_id=(s, 1 - t), device_id_type=MESH)
    pl.semaphore_wait(barrier, 2 * CHIPS)


def remote(src, dst, send_sem, recv_sem, s, t):
    return pltpu.make_async_remote_copy(
        src_ref=src,
        dst_ref=dst,
        send_sem=send_sem,
        recv_sem=recv_sem,
        device_id=(s, t),
        device_id_type=MESH,
    )


def rows_at(ref, start, count):
    return ref.at[pl.ds(pl.multiple_of(start, ROWS), count)]


class QuadGather:
    def __init__(self, buf, send, recv, chip, core, t):
        self.buf, self.send, self.recv = buf, send, recv
        self.chip, self.core, self.t = chip, core, t
        mine = core * 128 + t * ROWS
        self.mine = mine
        self.near = core * 128 + (1 - t) * ROWS
        sib = (2 * chip + 1 - core, t)
        self.to_near = self.copy(mine, 0, (2 * chip + core, 1 - t))
        self.to_sib = self.copy(mine, 1, sib)
        self.forward = self.copy(self.near, 2, sib)

    def copy(self, row, k, target):
        view = rows_at(self.buf, row, ROWS)
        return remote(view, view, self.send.at[k], self.recv.at[k], *target)

    def start(self):
        self.to_near.start()
        self.to_sib.start()

    def finish(self):
        self.to_near.wait_recv()
        self.forward.start()
        self.to_sib.wait_recv()
        self.forward.wait_recv()

    def drain(self):
        self.to_near.wait_send()
        self.to_sib.wait_send()
        self.forward.wait_send()


GATHER_SEMS = [pltpu.SemaphoreType.DMA((3,)), pltpu.SemaphoreType.DMA((3,))]
CW = 512
NC = D // CW


class QuadReduce:
    def __init__(self, part, dsend, drecv, ysend, yrecv, ds, dr, ys, yr, chip, core, t):
        self.part, self.dsend, self.drecv = part, dsend, drecv
        self.ysend, self.yrecv = ysend, yrecv
        self.core, self.t = core, t
        self.d = [
            remote(dsend.at[k], drecv.at[k], ds.at[k], dr.at[k], 2 * chip + 1 - core, t)
            for k in range(NC)
        ]
        self.y = [
            remote(ysend.at[k], yrecv.at[k], ys.at[k], yr.at[k], 2 * chip + core, 1 - t)
            for k in range(NC)
        ]

    def rows(self, start, count, k):
        return self.part[pl.ds(pl.multiple_of(start, ROWS), count), k * CW : (k + 1) * CW]

    def put(self, k, value):
        self.part[:, k * CW : (k + 1) * CW] = value
        self.dsend[k] = self.rows((1 - self.core) * 128, 128, k).astype(BF)
        self.d[k].start()

    def middle(self, k):
        self.d[k].wait_recv()
        near = (1 - self.t) * ROWS
        far = self.rows(self.core * 128 + near, ROWS, k)
        got = self.drecv[k, pl.ds(pl.multiple_of(near, ROWS), ROWS), :]
        self.ysend[k] = (far + got.astype(F32)).astype(BF)
        self.y[k].start()

    def result(self, k):
        mine = self.t * ROWS
        own = self.rows(self.core * 128 + mine, ROWS, k)
        got = self.drecv[k, pl.ds(pl.multiple_of(mine, ROWS), ROWS), :].astype(F32)
        self.y[k].wait_recv()
        return own + got + self.yrecv[k].astype(F32)

    def run(self, term):
        for k in range(NC):
            self.put(k, term(k))
            if k:
                self.middle(k - 1)
        self.middle(NC - 1)

    def drain(self):
        for k in range(NC):
            self.d[k].wait_send()
            self.y[k].wait_send()


REDUCE_SCRATCH = [
    pltpu.VMEM((BLOCK, D), F32),
    pltpu.VMEM((NC, 128, CW), BF),
    pltpu.VMEM((NC, 128, CW), BF),
    pltpu.VMEM((NC, ROWS, CW), BF),
    pltpu.VMEM((NC, ROWS, CW), BF),
] + [pltpu.SemaphoreType.DMA((NC,))] * 4


def tile_sends(tiles, land, send, recv, chip, core, t, start):
    s = 2 * chip + core
    for j in range(3):
        for u in range(2):
            slot, index = owner_of(2 * chip + u)
            target = (core * 3 + j) * 10 + slot
            k = j * 2 + u

            if start:

                @pl.when(target == s)
                def _():
                    pltpu.make_async_copy(tiles.at[j, u], land.at[index], recv.at[index]).start()

            @pl.when(target != s)
            def _():
                cp = remote(tiles.at[j, u], land.at[index], send.at[k], recv.at[index], target, t)
                if start:
                    cp.start()
                else:
                    cp.wait_send()


def tile_waits(tiles, land, send, recv, chip, core, t):
    slot = (2 * chip + core) % 10
    for r in range(SLOTS):
        here = chip < SERVED
        if r == 0:
            here = jnp.logical_and(here, slot < 4)

        @pl.when(here)
        def _():
            pltpu.make_async_copy(tiles.at[0, 0], land.at[r], recv.at[r]).wait()


def home_sends(tiles, land, send, recv, chip, core, t, start):
    s = 2 * chip + core
    slot = s % 10
    head = chip // PER_HEAD
    for r in range(SLOTS):
        here = chip < SERVED
        if r == 0:
            here = jnp.logical_and(here, slot < 4)
        tile = tile_of(slot, r)
        target = (tile // 2) * 2 + head // 3
        j, u = head % 3, tile % 2

        if start:

            @pl.when(jnp.logical_and(here, target == s))
            def _():
                pltpu.make_async_copy(tiles.at[r], land.at[j, u], recv.at[j, u]).start()

        @pl.when(jnp.logical_and(here, target != s))
        def _():
            cp = remote(tiles.at[r], land.at[j, u], send.at[r], recv.at[j, u], target, t)
            if start:
                cp.start()
            else:
                cp.wait_send()


def home_waits(tiles, land, recv):
    for j in range(3):
        for u in range(2):
            pltpu.make_async_copy(tiles.at[0], land.at[j, u], recv.at[j, u]).wait()


def weight_load(ref, buf, sem, core, width):
    return pltpu.make_async_copy(
        ref.at[:, pl.ds(pl.multiple_of(core * width, 128), width)], buf, sem
    )


def project_kernel(
    x_ref, gain_ref, wq_ref, wk_ref, wv_ref,
    normed_ref, q_ref, kv_ref,
    nbuf, wbuf, kvsrc, qsrc, wsem, nsend, nrecv, kvsend, kvrecv, fsend, qsend, qrecv, osem,
):
    chip, core, t = place()
    s = 2 * chip + core
    loads = [
        weight_load(ref, wbuf.at[k], wsem.at[k], core, 384)
        for k, ref in enumerate((wk_ref, wv_ref, wq_ref))
    ]
    for load in loads:
        load.start()
    x = x_ref[...]
    normed = (x * rms_scale(x) * gain_ref[...]).astype(BF)
    quad = QuadGather(nbuf, nsend, nrecv, chip, core, t)
    nbuf[pl.ds(pl.multiple_of(quad.mine, ROWS), ROWS), :] = normed
    greet_all(chip, core, t)
    quad.start()
    quad.finish()
    out = pltpu.make_async_copy(nbuf, normed_ref, osem)
    out.start()
    for k in range(2):
        loads[k].wait()
        value = matmul(nbuf[...], wbuf[k]).astype(BF)
        for j in range(3):
            kvsrc[j, :, k * 128 : (k + 1) * 128] = value[:, j * 128 : (j + 1) * 128]

    def kv_sends(start):
        for j in range(3):
            for p in range(PER_HEAD):
                w = (core * 3 + j) * PER_HEAD + p
                target = 2 * w + chip % 2

                if start:

                    @pl.when(target == s)
                    def _():
                        pltpu.make_async_copy(kvsrc.at[j], kv_ref.at[chip], kvrecv.at[chip]).start()

                @pl.when(target != s)
                def _():
                    cp = remote(
                        kvsrc.at[j], kv_ref.at[chip], kvsend.at[j * PER_HEAD + p],
                        kvrecv.at[chip], target, t,
                    )
                    if start:
                        cp.start()
                    else:
                        cp.wait_send()

    kv_sends(True)
    loads[2].wait()
    value = matmul(nbuf[...], wbuf[2]).astype(BF)
    for j in range(3):
        for u in range(2):
            qsrc[j, u] = value[u * 128 : (u + 1) * 128, j * 128 : (j + 1) * 128]
    tile_sends(qsrc, q_ref, qsend, qrecv, chip, core, t, True)

    @pl.when(chip < SERVED)
    def _():
        def forward(o):
            source = lax.rem((chip // 2 + o) * 2 + core, CHIPS)
            view = kv_ref.at[source]
            return source, remote(view, view, fsend.at[o], kvrecv.at[source], s + 1 - 2 * core, t)

        def take(o, carry):
            source, cp = forward(o)
            pltpu.make_async_copy(kvsrc.at[0], kv_ref.at[source], kvrecv.at[source]).wait()
            cp.start()
            return carry

        lax.fori_loop(0, CHIPS // 2, take, 0)

        def finish(o, carry):
            source = 2 * o + 1 - core
            pltpu.make_async_copy(kvsrc.at[0], kv_ref.at[source], kvrecv.at[source]).wait()
            forward(o)[1].wait_send()
            return carry

        lax.fori_loop(0, CHIPS // 2, finish, 0)

    tile_waits(qsrc, q_ref, qsend, qrecv, chip, core, t)
    kv_sends(False)
    tile_sends(qsrc, q_ref, qsend, qrecv, chip, core, t, False)
    quad.drain()
    out.wait()


VM = pl.BlockSpec(memory_space=pltpu.VMEM)
SM = pl.BlockSpec(memory_space=pltpu.SMEM)
ANY = pl.BlockSpec(memory_space=pl.ANY)


def shape(dims, dtype):
    return jax.ShapeDtypeStruct(dims, dtype)


def project(x, gain, wq, wk, wv):
    return pl.pallas_call(
        project_kernel,
        name="project",
        out_shape=(
            shape((BLOCK, D), BF),
            shape((SLOTS, TILE, 128), BF),
            shape((CHIPS, BLOCK, 256), BF),
        ),
        in_specs=[VM, VM, ANY, ANY, ANY],
        out_specs=(ANY, ANY, ANY),
        scratch_shapes=[
            pltpu.VMEM((BLOCK, D), BF),
            pltpu.VMEM((3, D, 384), BF),
            pltpu.VMEM((3, BLOCK, 256), BF),
            pltpu.VMEM((3, 2, TILE, 128), BF),
            pltpu.SemaphoreType.DMA((3,)),
            *GATHER_SEMS,
            pltpu.SemaphoreType.DMA((15,)),
            pltpu.SemaphoreType.DMA((CHIPS,)),
            pltpu.SemaphoreType.DMA((CHIPS // 2,)),
            pltpu.SemaphoreType.DMA((6,)),
            pltpu.SemaphoreType.DMA((SLOTS,)),
            pltpu.SemaphoreType.DMA,
        ],
        compiler_params=pltpu.CompilerParams(
            collective_id=0, has_side_effects=True, vmem_limit_bytes=VMEM_LIMIT
        ),
    )(x, gain, wq, wk, wv)


def eye():
    row = lax.broadcasted_iota(jnp.int32, (128, 128), 0)
    col = lax.broadcasted_iota(jnp.int32, (128, 128), 1)
    return jnp.where(row == col, 1.0, 0.0).astype(BF)


def both_maps(q_t):
    top = lax.broadcasted_iota(jnp.int32, q_t.shape, 0) < 64
    return jnp.concatenate([jnp.where(top, q_t, 0.0), jnp.where(top, 0.0, q_t)], axis=1)


def key_mask(start, count, tile, width):
    key = start + lax.broadcasted_iota(jnp.int32, (count, width), 0)
    query = tile * TILE + lax.broadcasted_iota(jnp.int32, (count, width), 1) % TILE
    return key <= query


def group_norm(parts, lam):
    first, second = parts[:, :TILE], parts[:, TILE:]
    differ = first - lam * second
    rms = rms_scale(differ, 0)
    return rms, differ * rms


def attend_kernel(
    tiles_ref, lam_ref, gain_ref, q_ref, kv_ref, mixed_ref, parts_ref, log_ref, v_t, kmax, acc, total
):
    keys = CHIPS * BLOCK
    lam = lam_ref[0]

    @pl.when(tiles_ref[SLOTS - 1] >= 0)
    def _():
        unit = eye()

        def flip(b, best):
            block = kv_ref[pl.ds(b * KB, KB), :]
            v_t[:, pl.ds(pl.multiple_of(b * KB, KB), KB)] = matmul_t(unit, block[:, 128:]).astype(BF)
            k_t = matmul_t(unit, block[:, :128])
            square = k_t * k_t
            return (
                jnp.maximum(best[0], jnp.sum(square[:64], axis=0, keepdims=True)),
                jnp.maximum(best[1], jnp.sum(square[64:], axis=0, keepdims=True)),
            )

        zero = jnp.zeros((1, KB), F32)
        best = lax.fori_loop(0, keys // KB, flip, (zero, zero))
        for m in range(2):
            kmax[m] = jnp.max(best[m])

    for r in range(SLOTS):
        tile = tiles_ref[r]

        @pl.when(tile >= 0)
        def _():
            q_t = q_ref[r].astype(F32).T
            square = q_t * q_t
            bound = SCORE * jnp.concatenate(
                [
                    jnp.sqrt(jnp.sum(square[:64], axis=0, keepdims=True) * kmax[0]),
                    jnp.sqrt(jnp.sum(square[64:], axis=0, keepdims=True) * kmax[1]),
                ],
                axis=1,
            )
            q_both = both_maps(q_t).astype(BF)
            acc[...] = jnp.zeros_like(acc)
            total[...] = jnp.zeros_like(total)

            def step(b, masked):
                start = pl.multiple_of(b * KB, KB)
                score = matmul(kv_ref[pl.ds(start, KB), :128], q_both)
                prob = jnp.exp2(score * SCORE - bound)
                if masked:
                    prob = jnp.where(key_mask(start, KB, tile, 2 * TILE), prob, 0.0)
                total[...] += jnp.sum(prob, axis=0, keepdims=True)
                acc[...] += matmul(v_t[:, pl.ds(start, KB)], prob.astype(BF))

            full = tile * TILE // KB

            def body(b, carry):
                step(b, False)
                return carry

            lax.fori_loop(0, full, body, 0)
            step(full, True)
            parts = acc[...] / total[...]
            parts_ref[r] = parts
            log_ref[r] = bound + jnp.log(total[...]) * LOG2E
            rms, hat = group_norm(parts, lam)
            mixed_ref[r] = (hat * gain_ref[...] * OUT_SCALE).T.astype(BF)


def attend(tiles, lam, gain, q, kv):
    return pl.pallas_call(
        attend_kernel,
        name="attend",
        out_shape=(
            shape((SLOTS, TILE, 128), BF),
            shape((SLOTS, 128, 2 * TILE), F32),
            shape((SLOTS, 1, 2 * TILE), F32),
        ),
        in_specs=[SM, SM, VM, VM, VM],
        out_specs=(VM, VM, VM),
        scratch_shapes=[
            pltpu.VMEM((128, CHIPS * BLOCK), BF),
            pltpu.SMEM((2,), F32),
            pltpu.VMEM((128, 2 * TILE), F32),
            pltpu.VMEM((1, 2 * TILE), F32),
        ],
        compiler_params=pltpu.CompilerParams(vmem_limit_bytes=VMEM_LIMIT),
        cost_estimate=pl.CostEstimate(
            flops=6 * 10**9, bytes_accessed=6 * 2**20, transcendentals=7 * 10**6
        ),
    )(tiles, lam, gain, q, kv)


def middle_kernel(
    x_ref, cot_ref, mask_ref, gain_ref, tiles_ref, wo_ref, wg_ref, wu_ref, wd_ref,
    out_ref, dres_ref, gainpart_ref, ffn_ref, dout_ref, dgate_ref, dup_ref, hid_ref, mix_ref,
    dresall_ref, dmix_ref,
    land, wo, wg, wu, wd, fbuf, obuf, rbuf, dms, *rest,
):
    chip, core, t = place()
    reduces = [rest[9 * k : 9 * k + 9] for k in range(3)]
    gathers = [rest[27 + 2 * k : 29 + 2 * k] for k in range(3)]
    wsem, hsend, hrecv, tsend, trecv, osem = rest[33:]
    loads = [
        weight_load(wo_ref, wo, wsem.at[0], core, 384),
        weight_load(wg_ref, wg, wsem.at[1], core, 1024),
        weight_load(wu_ref, wu, wsem.at[2], core, 1024),
        weight_load(wd_ref, wd, wsem.at[3], core, 1024),
    ]
    for load in loads:
        load.start()
    gather_f = QuadGather(fbuf, *gathers[0], chip, core, t)
    gather_o = QuadGather(obuf, *gathers[1], chip, core, t)
    gather_r = QuadGather(rbuf, *gathers[2], chip, core, t)
    mine = pl.ds(pl.multiple_of(gather_f.mine, ROWS), ROWS)
    dout = cot_ref[...] * mask_ref[...]
    obuf[mine, :] = dout.astype(BF)
    greet_all(chip, core, t)
    home_sends(tiles_ref, land, hsend, hrecv, chip, core, t, True)
    gather_o.start()
    loads[0].wait()
    home_waits(tiles_ref, land, hrecv)
    for j in range(3):
        for u in range(2):
            mix_ref[u * 128 : (u + 1) * 128, j * 128 : (j + 1) * 128] = land[j, u]

    red = QuadReduce(*reduces[0], chip, core, t)
    red.run(lambda k: matmul_t(mix_ref[...], wo[k * CW : (k + 1) * CW, :]))
    resid = x_ref[...] + jnp.concatenate([red.result(k) for k in range(NC)], axis=1)
    ffn_rms = rms_scale(resid)
    ffn_hat = resid * ffn_rms
    fbuf[mine, :] = (ffn_hat * gain_ref[...]).astype(BF)
    gather_f.start()
    gather_o.finish()
    gather_f.finish()
    for load in loads[1:]:
        load.wait()

    def hidden_step(n, carry):
        cols = pl.ds(pl.multiple_of(n * 256, 256), 256)
        gate = matmul(fbuf[...], wg[:, cols])
        up = matmul(fbuf[...], wu[:, cols])
        d_hidden = matmul(obuf[...], wd[:, cols])
        sig = 1.0 / (1.0 + jnp.exp(-gate))
        silu = gate * sig
        hid_ref[:, cols] = (silu * up).astype(BF)
        dgate_ref[:, cols] = (d_hidden * up * sig * (1.0 + gate * (1.0 - sig))).astype(BF)
        dup_ref[:, cols] = (d_hidden * silu).astype(BF)
        return carry

    lax.fori_loop(0, 4, hidden_step, 0)
    red2 = QuadReduce(*reduces[1], chip, core, t)
    red2.run(
        lambda k: matmul_t(dgate_ref[...], wg[k * CW : (k + 1) * CW, :])
        + matmul_t(dup_ref[...], wu[k * CW : (k + 1) * CW, :])
    )
    red3 = QuadReduce(*reduces[2], chip, core, t)
    d_ffn = jnp.concatenate([red2.result(k) for k in range(NC)], axis=1)
    gainpart_ref[...] = jnp.sum(d_ffn * ffn_hat, axis=0, keepdims=True)
    d_resid = dout + norm_back(d_ffn, gain_ref[...], ffn_rms, ffn_hat)
    dres_ref[...] = d_resid
    rbuf[mine, :] = d_resid.astype(BF)
    gather_r.start()
    red3.run(lambda k: matmul_t(hid_ref[...], wd[k * CW : (k + 1) * CW, :]))
    gather_r.finish()
    d_mixed = matmul(rbuf[...], wo[...]).astype(BF)
    for j in range(3):
        for u in range(2):
            dms[j, u] = d_mixed[u * 128 : (u + 1) * 128, j * 128 : (j + 1) * 128]
    tile_sends(dms, dmix_ref, tsend, trecv, chip, core, t, True)
    saves = [
        pltpu.make_async_copy(fbuf, ffn_ref, osem.at[0]),
        pltpu.make_async_copy(obuf, dout_ref, osem.at[1]),
        pltpu.make_async_copy(rbuf, dresall_ref, osem.at[2]),
    ]
    for save in saves:
        save.start()
    out_ref[...] = resid + jnp.concatenate([red3.result(k) for k in range(NC)], axis=1)
    tile_waits(dms, dmix_ref, tsend, trecv, chip, core, t)
    tile_sends(dms, dmix_ref, tsend, trecv, chip, core, t, False)
    home_sends(tiles_ref, land, hsend, hrecv, chip, core, t, False)
    for gather in (gather_f, gather_o, gather_r):
        gather.drain()
    for reduce in (red, red2, red3):
        reduce.drain()
    for save in saves:
        save.wait()


def middle(x, cot, mask, gain, tiles, wo, wg, wu, wd):
    return pl.pallas_call(
        middle_kernel,
        name="middle",
        out_shape=(
            shape((ROWS, D), F32),
            shape((ROWS, D), F32),
            shape((1, D), F32),
            shape((BLOCK, D), BF),
            shape((BLOCK, D), BF),
            shape((BLOCK, 1024), BF),
            shape((BLOCK, 1024), BF),
            shape((BLOCK, 1024), BF),
            shape((BLOCK, 384), BF),
            shape((BLOCK, D), BF),
            shape((SLOTS, TILE, 128), BF),
        ),
        in_specs=[VM, VM, VM, VM, ANY, ANY, ANY, ANY, ANY],
        out_specs=(VM, VM, VM, ANY, ANY, VM, VM, VM, VM, ANY, ANY),
        scratch_shapes=[
            pltpu.VMEM((3, 2, TILE, 128), BF),
            pltpu.VMEM((D, 384), BF),
            pltpu.VMEM((D, 1024), BF),
            pltpu.VMEM((D, 1024), BF),
            pltpu.VMEM((D, 1024), BF),
            pltpu.VMEM((BLOCK, D), BF),
            pltpu.VMEM((BLOCK, D), BF),
            pltpu.VMEM((BLOCK, D), BF),
            pltpu.VMEM((3, 2, TILE, 128), BF),
            *(REDUCE_SCRATCH * 3),
            *(GATHER_SEMS * 3),
            pltpu.SemaphoreType.DMA((4,)),
            pltpu.SemaphoreType.DMA((SLOTS,)),
            pltpu.SemaphoreType.DMA((3, 2)),
            pltpu.SemaphoreType.DMA((6,)),
            pltpu.SemaphoreType.DMA((SLOTS,)),
            pltpu.SemaphoreType.DMA((3,)),
        ],
        compiler_params=pltpu.CompilerParams(
            collective_id=1, has_side_effects=True, vmem_limit_bytes=VMEM_LIMIT
        ),
    )(x, cot, mask, gain, tiles, wo, wg, wu, wd)


BB = 256


def attend_back_kernel(
    tiles_ref, lam_ref, gain_ref, q_ref, kv_ref, dmix_ref, parts_ref, log_ref,
    dq_ref, dkv_ref, sub_ref, dlam_ref,
    k_t, acc, dq_acc, sub_acc, lam_acc,
):
    keys = CHIPS * BLOCK
    lam = lam_ref[0]
    sub_acc[...] = jnp.zeros_like(sub_acc)
    lam_acc[...] = jnp.zeros_like(lam_acc)

    @pl.when(tiles_ref[SLOTS - 1] >= 0)
    def _():
        unit = eye()

        def flip(b, carry):
            rows = pl.ds(pl.multiple_of(b * KB, KB), KB)
            k_t[:, rows] = matmul_t(unit, kv_ref[rows, :128]).astype(BF)
            acc[rows, :] = jnp.zeros((KB, 256), F32)
            return carry

        lax.fori_loop(0, keys // KB, flip, 0)

    for r in range(SLOTS):
        tile = tiles_ref[r]

        @pl.when(tile >= 0)
        def _():
            q_t = q_ref[r].astype(F32).T
            q_both_t = both_maps(q_t).astype(BF)
            q = q_ref[r].astype(F32)
            left = lax.broadcasted_iota(jnp.int32, q.shape, 1) < 64
            q_both = jnp.concatenate(
                [jnp.where(left, q, 0.0), jnp.where(left, 0.0, q)], axis=0
            ).astype(BF)
            parts = parts_ref[r]
            first, second = parts[:, :TILE], parts[:, TILE:]
            rms, hat = group_norm(parts, lam)
            e_t = dmix_ref[r].astype(F32).T * OUT_SCALE
            sub_acc[...] += jnp.sum(e_t * hat, axis=1, keepdims=True)
            d_differ = norm_back(e_t, gain_ref[...], rms, hat, 0).astype(BF)
            d_wide = d_differ.astype(F32)
            d_rows = d_wide.T.astype(BF)
            second_dot = jnp.sum(d_wide * second, axis=0, keepdims=True)
            lam_acc[...] -= second_dot
            first_delta = jnp.sum(d_wide * first, axis=0, keepdims=True)
            second_delta = -lam * second_dot
            log_total = log_ref[r]
            dq_acc[...] = jnp.zeros_like(dq_acc)

            def step(b, masked):
                start = pl.multiple_of(b * BB, BB)
                rows = pl.ds(start, BB)
                block = kv_ref[rows, :]
                score = matmul(block[:, :128], q_both_t)
                prob = jnp.exp2(score * SCORE - log_total)
                if masked:
                    prob = jnp.where(key_mask(start, BB, tile, 2 * TILE), prob, 0.0)
                upper = matmul(block[:, 128:], d_differ)
                p1, p2 = prob[:, :TILE], prob[:, TILE:]
                ds = jnp.concatenate(
                    [p1 * (upper - first_delta), p2 * (-lam * upper - second_delta)], axis=1
                ).astype(BF)
                both = (p1 - lam * p2).astype(BF)
                acc[rows, :128] += matmul(ds, q_both)
                acc[rows, 128:] += matmul(both, d_rows)
                dq_acc[...] += matmul(k_t[:, rows], ds)

            full = tile * TILE // BB

            def body(b, carry):
                step(b, False)
                return carry

            lax.fori_loop(0, full, body, 0)
            step(full, True)
            dq_t = jnp.concatenate([dq_acc[:64, :TILE], dq_acc[64:, TILE:]], axis=0)
            dq_ref[r] = (dq_t * 0.125).T.astype(BF)

    @pl.when(tiles_ref[SLOTS - 1] >= 0)
    def _():
        def save(b, carry):
            rows = pl.ds(pl.multiple_of(b * KB, KB), KB)
            dkv_ref[rows, :128] = (acc[rows, :128] * 0.125).astype(BF)
            dkv_ref[rows, 128:] = acc[rows, 128:].astype(BF)
            return carry

        lax.fori_loop(0, keys // KB, save, 0)

    sub_ref[...] = sub_acc[...]
    dlam_ref[...] = jnp.sum(lam_acc[...], axis=1, keepdims=True)


def attend_back(tiles, lam, gain, q, kv, dmix, parts, logs):
    return pl.pallas_call(
        attend_back_kernel,
        name="attend_back",
        out_shape=(
            shape((SLOTS, TILE, 128), BF),
            shape((CHIPS * BLOCK, 256), BF),
            shape((128, 1), F32),
            shape((1, 1), F32),
        ),
        in_specs=[SM, SM] + [VM] * 6,
        out_specs=(VM, VM, VM, VM),
        scratch_shapes=[
            pltpu.VMEM((128, CHIPS * BLOCK), BF),
            pltpu.VMEM((CHIPS * BLOCK, 256), F32),
            pltpu.VMEM((128, 2 * TILE), F32),
            pltpu.VMEM((128, 1), F32),
            pltpu.VMEM((1, TILE), F32),
        ],
        compiler_params=pltpu.CompilerParams(vmem_limit_bytes=VMEM_LIMIT),
        cost_estimate=pl.CostEstimate(
            flops=2 * 10**10, bytes_accessed=10 * 2**20, transcendentals=7 * 10**6
        ),
    )(tiles, lam, gain, q, kv, dmix, parts, logs)


def finish_kernel(
    x_ref, gain_ref, dres_ref, dq_ref, dkv_ref, wq_ref, wk_ref, wv_ref,
    grad_ref, gainpart_ref, dqkv_ref,
    wbuf, sib, both, home, land, *rest,
):
    chip, core, t = place()
    s = 2 * chip + core
    reduce = rest[:9]
    wsem, dsend, drecv, ksend, krecv, hsend, hrecv = rest[9:]
    loads = [
        weight_load(ref, wbuf.at[k], wsem.at[k], core, 384)
        for k, ref in enumerate((wq_ref, wk_ref, wv_ref))
    ]
    for load in loads:
        load.start()
    greet_all(chip, core, t)
    head = chip // PER_HEAD
    half = CHIPS // 2

    def to_sibling(o):
        return remote(
            dkv_ref.at[2 * o + 1 - core], sib.at[o], dsend.at[o], drecv.at[o], s + 1 - 2 * core, t
        )

    def order(o):
        return lax.rem(chip // 2 + 1 + o, half)

    def to_home(o, start):
        block = 2 * o + core
        target = 2 * block + head // 3
        spot = (head % 3) * PER_HEAD + chip % PER_HEAD

        if start:

            @pl.when(target == s)
            def _():
                pltpu.make_async_copy(both.at[o], home.at[spot], krecv.at[spot]).start()

        @pl.when(target != s)
        def _():
            cp = remote(both.at[o], home.at[spot], ksend.at[o], krecv.at[spot], target, t)
            if start:
                cp.start()
            else:
                cp.wait_send()

    @pl.when(chip < SERVED)
    def _():
        def first(k, carry):
            to_sibling(order(k)).start()
            return carry

        lax.fori_loop(0, half, first, 0)

    home_sends(dq_ref, land, hsend, hrecv, chip, core, t, True)

    @pl.when(chip < SERVED)
    def _():
        def second(k, carry):
            o = order(k)
            to_sibling(o).wait_recv()
            both[o] = (dkv_ref[2 * o + core].astype(F32) + sib[o].astype(F32)).astype(BF)
            to_home(o, True)
            return carry

        lax.fori_loop(0, half, second, 0)

    for load in loads:
        load.wait()
    home_waits(dq_ref, land, hrecv)
    for j in range(3):
        for u in range(2):
            dqkv_ref[u * 128 : (u + 1) * 128, j * 128 : (j + 1) * 128] = land[j, u]
    for j in range(3):
        total = jnp.zeros((BLOCK, 256), F32)
        for p in range(PER_HEAD):
            spot = j * PER_HEAD + p
            pltpu.make_async_copy(both.at[0], home.at[spot], krecv.at[spot]).wait()
            total = total + home[spot].astype(F32)
        dqkv_ref[:, 384 + j * 128 : 512 + j * 128] = total[:, :128].astype(BF)
        dqkv_ref[:, 768 + j * 128 : 896 + j * 128] = total[:, 128:].astype(BF)
    red = QuadReduce(*reduce, chip, core, t)

    def term(k):
        rows = slice(k * CW, (k + 1) * CW)
        return (
            matmul_t(dqkv_ref[:, :384], wbuf[0, rows, :])
            + matmul_t(dqkv_ref[:, 384:768], wbuf[1, rows, :])
            + matmul_t(dqkv_ref[:, 768:], wbuf[2, rows, :])
        )

    red.run(term)
    x = x_ref[...]
    rms = rms_scale(x)
    hat = x * rms
    d_normed = jnp.concatenate([red.result(k) for k in range(NC)], axis=1)
    gainpart_ref[...] = jnp.sum(d_normed * hat, axis=0, keepdims=True)
    grad_ref[...] = dres_ref[...] + norm_back(d_normed, gain_ref[...], rms, hat)
    red.drain()
    home_sends(dq_ref, land, hsend, hrecv, chip, core, t, False)

    @pl.when(chip < SERVED)
    def _():
        def last(o, carry):
            to_sibling(o).wait_send()
            to_home(o, False)
            return carry

        lax.fori_loop(0, half, last, 0)


def finish(x, gain, dres, dq, dkv, wq, wk, wv):
    return pl.pallas_call(
        finish_kernel,
        name="finish",
        out_shape=(shape((ROWS, D), F32), shape((1, D), F32), shape((BLOCK, 1152), BF)),
        in_specs=[VM, VM, VM, ANY, VM, ANY, ANY, ANY],
        out_specs=(VM, VM, VM),
        scratch_shapes=[
            pltpu.VMEM((3, D, 384), BF),
            pltpu.VMEM((CHIPS // 2, BLOCK, 256), BF),
            pltpu.VMEM((CHIPS // 2, BLOCK, 256), BF),
            pltpu.VMEM((3 * PER_HEAD, BLOCK, 256), BF),
            pltpu.VMEM((3, 2, TILE, 128), BF),
            *REDUCE_SCRATCH,
            pltpu.SemaphoreType.DMA((3,)),
            pltpu.SemaphoreType.DMA((CHIPS // 2,)),
            pltpu.SemaphoreType.DMA((CHIPS // 2,)),
            pltpu.SemaphoreType.DMA((CHIPS // 2,)),
            pltpu.SemaphoreType.DMA((3 * PER_HEAD,)),
            pltpu.SemaphoreType.DMA((SLOTS,)),
            pltpu.SemaphoreType.DMA((3, 2)),
        ],
        compiler_params=pltpu.CompilerParams(
            collective_id=2, has_side_effects=True, vmem_limit_bytes=VMEM_LIMIT
        ),
    )(x, gain, dres, dq, dkv, wq, wk, wv)


def row_product(left, right):
    return lax.dot_general(left, right, (((0,), (0,)), ((), ())), preferred_element_type=F32)


def weight_grad(left, right, core):
    part = row_product(left, right).astype(BF)
    groups = [[2 * i + c for i in range(CHIPS)] for c in range(2)]
    rows = lax.psum_scatter(
        part, "seq", scatter_dimension=0, axis_index_groups=groups, tiled=True
    ).astype(F32)
    near = lax.dynamic_slice_in_dim(rows, core * 24, 24, 0)
    away = lax.dynamic_slice_in_dim(rows, (1 - core) * 24, 24, 0)
    got = lax.ppermute(away, "seq", [(i, i ^ 1) for i in range(2 * CHIPS)])
    even = jnp.concatenate([near, got], axis=1)
    odd = jnp.concatenate([got, near], axis=1)
    return jnp.where(core == 0, even, odd)


def on_device(
    hidden_in, cotangent, needle_mask, attn_gain, lambdas, subln_gain, ffn_gain,
    weight_query, weight_key, weight_value, weight_out, weight_gate, weight_up, weight_down,
):
    chip, core, t = place()
    first_exp = jnp.exp(jnp.sum(lambdas[0] * lambdas[1], axis=-1))
    second_exp = jnp.exp(jnp.sum(lambdas[2] * lambdas[3], axis=-1))
    lambda_all = first_exp - second_exp + LAMBDA_INIT
    head = jnp.minimum(t * 6 + chip // PER_HEAD, 11)
    lam = lax.dynamic_slice_in_dim(lambda_all, head, 1)
    slot = (2 * chip + core) % 10
    served = chip < SERVED
    tiles = jnp.stack(
        [
            jnp.where(served if r else jnp.logical_and(served, slot < 4), tile_of(slot, r), -1)
            for r in range(SLOTS)
        ]
    ).astype(jnp.int32)
    attn_row = attn_gain.reshape(1, D)
    ffn_row = ffn_gain.reshape(1, D)
    sub_col = subln_gain.reshape(128, 1)
    mask = needle_mask.astype(F32).reshape(ROWS, 1)

    normed_all, q, kv = project(hidden_in, attn_row, weight_query, weight_key, weight_value)
    kv = kv.reshape(CHIPS * BLOCK, 256)
    mixed_tiles, parts, logs = attend(tiles, lam, sub_col, q, kv)
    (
        output, d_resid, ffn_part, ffn_all, dout_all, d_gate, d_up, hidden, mixed, dres_all, dmix,
    ) = middle(
        hidden_in, cotangent, mask, ffn_row, mixed_tiles, weight_out, weight_gate, weight_up, weight_down
    )
    dq, dkv, sub_part, dlam = attend_back(tiles, lam, sub_col, q, kv, dmix, parts, logs)
    grad_input, attn_part, dqkv = finish(
        hidden_in, attn_row, d_resid, dq, dkv.reshape(CHIPS, BLOCK, 256),
        weight_query, weight_key, weight_value,
    )
    here = jnp.logical_and(jnp.arange(12) == head, served)
    dlam_all = jnp.where(here, dlam[0, 0], 0.0)
    gains = lax.psum(
        jnp.concatenate([attn_part[0], ffn_part[0], sub_part[:, 0], dlam_all]), ("seq", "tp")
    )
    d_lambda = gains[2 * D + 128 :]
    grad_lambdas = jnp.stack(
        [
            (d_lambda * first_exp)[:, None] * lambdas[1],
            (d_lambda * first_exp)[:, None] * lambdas[0],
            -(d_lambda * second_exp)[:, None] * lambdas[3],
            -(d_lambda * second_exp)[:, None] * lambdas[2],
        ]
    )
    return (
        output,
        grad_input,
        weight_grad(normed_all, dqkv[:, :384], core),
        weight_grad(normed_all, dqkv[:, 384:768], core),
        weight_grad(normed_all, dqkv[:, 768:], core),
        weight_grad(dres_all, mixed, core),
        weight_grad(ffn_all, d_gate, core),
        weight_grad(ffn_all, d_up, core),
        weight_grad(dout_all, hidden, core),
        gains[:D],
        grad_lambdas,
        gains[2 * D : 2 * D + 128],
        gains[D : 2 * D],
    )


def solution(mesh):
    split = P(None, "tp")
    rows = P(("seq", "tp"), None)
    both = P("seq", "tp")
    return jax.shard_map(
        on_device,
        mesh=mesh,
        in_specs=(rows, rows, P(("seq", "tp"))) + (P(),) * 4 + (split,) * 7,
        out_specs=(rows, rows) + (both,) * 7 + (P(),) * 4,
        check_vma=False,
    )
```

time: 3880 us -> 1790 us (0.46)
  starting transfers between devices: 1300 us -> 20.7 us
  local copies, waits for them, and re-layouts: 351 us -> 11.6 us
  waiting for transfers between devices: 1660 us -> 1390 us
  Pallas kernels: 0 us -> 258 us
  matrix products: 265 us -> 16.8 us
  other arithmetic: 123 us -> 13.7 us
  blocking collectives: 118 us -> 67 us
    ppermute x256 -> x7, starting transfers between devices: 1300 us -> 20.4 us  [weight_grad(): got = lax.ppermute(away, 'seq', [(i, i ^ 1) for i in range(2 * CHIPS)])]
    ppermute x256 -> x7, waiting for transfers between devices: 281 us -> 0.02 us  [weight_grad(): got = lax.ppermute(away, 'seq', [(i, i ^ 1) for i in range(2 * CHIPS)])]
    pallas_call x0 -> x5, Pallas kernels: none -> 258 us  [the longest x1 62.5 us: middle(): pl.pallas_call(middle_kernel, name='middle', out_shape=(shape((ROWS, D),...]
    another operation x132 -> x1, local copies, waits for them, and re-layouts: 213 us -> 0.6 us  [on_device(): jnp.stack([jnp.where(served if r else jnp.logical_and(served, slot < 4),...]
    dot_general x160 -> x0, matrix products: 205 us -> none  [the longest x34 79.1 us: block_scores(): jnp.einsum('qhd,khd->hqk', query_heads[..., offset:offset + half], key_he...]
    reduce_scatter x11 -> x7, waiting for transfers between devices: 1280 us -> 1390 us  [weight_grad(): lax.psum_scatter(part, 'seq', scatter_dimension=0, axis_index_groups=grou...]
    all_gather x2 -> x0, waiting for transfers between devices: 104 us -> none  [the longest x1 89.1 us: on_device(): key_piece = lax.all_gather(keys, 'seq', axis=0, tiled=True)]
    while x130 -> x0, local copies, waits for them, and re-layouts: 99.2 us -> none
  transfers between devices with their start and end apart: 269 -> 14, of which waited for: 135 -> 7; matrix products, arithmetic and copies ran while one was open for 6% -> 1% of each run, Pallas kernels for 0% -> 6%
where the time goes in v1:
time: 1790 us
  waiting for transfers between devices  1390 us (78%)
  Pallas kernels  258 us (14%)
  blocking collectives  67 us (4%)
  starting transfers between devices  20.7 us (1%)
    reduce_scatter x7, waiting for transfers between devices, weight_grad(): lax.psum_scatter(part, 'seq', scatter_dimension=0, axis_index_groups=grou...  1390 us
    psum x1, blocking collectives, on_device(): lax.psum(jnp.concatenate([attn_part[0], ffn_part[0], sub_part[:, 0], dlam...  67 us
    pallas_call x1, Pallas kernels, middle(): pl.pallas_call(middle_kernel, name='middle', out_shape=(shape((ROWS, D),...  62.5 us
    pallas_call x1, Pallas kernels, project(): pl.pallas_call(project_kernel, name='project', out_shape=(shape((BLOCK, D...  57.9 us
    pallas_call x1, Pallas kernels, finish(): pl.pallas_call(finish_kernel, name='finish', out_shape=(shape((ROWS, D),...  53.8 us
    pallas_call x1, Pallas kernels, attend_back(): pl.pallas_call(attend_back_kernel, name='attend_back', out_shape=(shape((...  51.1 us
  transfers between devices with their start and end apart: 14, of which 7 were waited for; matrix products, arithmetic and copies ran while one was open for 1% of the time, Pallas kernels for 6%

profile of v1, /device:TPU:31, one launch (start us, length us, event | category | flops | bytes accessed | tf_op | source)
XLA Modules:
  0.0 1787.4 jit_solution(307077711071440246)
XLA Ops:
  7.3 1.1 multiply_reduce_fusion.1
  8.4 1.3 reshape.70.gain_ref
  9.7 1.4 copy.30.gain_ref
  11.1 0.7 convert_bitcast_fusion
  11.7 0.7 copy.31.mask_ref
  12.4 1.3 reshape.68.gain_ref
  13.7 0.6 dynamic_slice.45.lam_ref
  14.3 57.9 %project.1 = (bf16[256,1536]{1,0:T(8,128)(2,1)}, bf16[7,128,128]{2,1,0:T(8,128)(2,1)}, bf16[32,256,256]{2,1,0:T(8,128)(2,1)}) custom-call(f32[64,1536]{1,0:T(8,128)} %x_ref.5, f32[1,1536]{1,0:T(1,128)} %reshape.70.gain_ref, bf16[1536,768]{1,0:T(8,128)(2,1)} %wq_ref.3, bf16[1536,768]{1,0:T(8,128)(2,1)} %wk_ref.3, bf16[1536,768]{1,0:T(8,128)(2,1)} %wv_ref.3), custom_call_target="tpu_custom_call" | custom-call | tf_op jit(solution)/shard_map/project/pallas_call | solution.py:365
  72.2 0.6 stack.38.tiles_ref
  72.8 32.3 %attend.1 = (bf16[7,128,128]{2,1,0:T(8,128)(2,1)}, f32[7,128,256]{2,1,0:T(8,128)}, f32[7,1,256]{2,1,0:T(1,128)}) custom-call(s32[7]{0:T(128)} %stack.38.tiles_ref, f32[1]{0:T(128)} %dynamic_slice.45.lam_ref, f32[128,1]{1,0:T(8,128)} %copy.30.gain_ref, bf16[7,128,128]{2,1,0:T(8,128)(2,1)} %get-tuple-element.37.q_ref, bf16[8192,256]{1,0:T(8,128)(2,1)} %bitcast.26), custom_call_target="tpu_custom_call" | custom-call | flops 6000000000 | bytes 6291456 | tf_op jit(solution)/shard_map/attend/pallas_call | solution.py:487
  105.2 62.5 %middle.1 = (f32[64,1536]{1,0:T(8,128)}, f32[64,1536]{1,0:T(8,128)}, f32[1,1536]{1,0:T(1,128)}, bf16[256,1536]{1,0:T(8,128)(2,1)}, bf16[256,1536]{1,0:T(8,128)(2...) custom-call(f32[64,1536]{1,0:T(8,128)} %x_ref.5, ...), custom_call_target="tpu_custom_call" | custom-call | tf_op jit(solution)/shard_map/middle/pallas_call | solution.py:607
  167.7 2.8 convolution_convert_fusion.3
  170.6 51.1 %attend_back.1 = (bf16[7,128,128]{2,1,0:T(8,128)(2,1)}, bf16[8192,256]{1,0:T(8,128)(2,1)}, f32[128,1]{1,0:T(8,128)}, f32[1,1]{1,0:T(1,128)}) custom-call(s32[7]{0:T(128)} %stack.38.tiles_ref, f32[1]{0:T(128)} %dynamic_slice.45.lam_ref, f32[128,1]{1,0:T(8,128)} %copy.30.gain_ref, bf16[7,128,128]{2,1,0:T(8,128)(2,1)} %get-tuple-element.37.q_ref, ...), custom_call_target="tpu_custom_call" | custom-call | flops 20000000000 | bytes 10485760 | tf_op jit(solution)/shard_map/attend_back/pallas_call | solution.py:746
  221.7 53.8 %finish.1 = (f32[64,1536]{1,0:T(8,128)}, f32[1,1536]{1,0:T(1,128)}, bf16[256,1152]{1,0:T(8,128)(2,1)}) custom-call(f32[64,1536]{1,0:T(8,128)} %x_ref.5, f32[1,1536]{1,0:T(1,128)} %reshape.70.gain_ref, f32[64,1536]{1,0:T(8,128)} %get-tuple-element.41.dres_ref, bf16[7,128,128]{2,1,0:T(8,128)(2,1)} %get-tuple-element.45.dq_ref, bf16[32,256,256]{2,1,0:T(8,128)(2,1)} %bitcast.24, ...), custom_call_target="tpu_custom_call" | custom-call | tf_op jit(solution)/shard_map/finish/pallas_call | solution.py:883
  275.6 2.6 convolution_convert_fusion.4
  278.2 0.0 reduce-scatter.10.cloned.1.call-start
  278.3 1.6 convolution_convert_fusion.5
  280.0 1.7 convolution_convert_fusion.6
  281.7 0.0 reduce-scatter.20.cloned.1.call-start
  281.8 2.7 convolution_convert_fusion
  284.5 1.1 copy-done
  285.6 0.1 copy-done.5
  285.7 2.7 convolution_convert_fusion.1
  288.5 1.0 copy-done.4
  289.4 2.7 convolution_convert_fusion.2
  292.2 0.6 copy-done.12
  292.9 0.1 copy-done.10
  293.0 0.1 reduce.4
  293.2 0.7 and_select_fusion
  293.8 67.0 %psum.7 = f32[3212]{0:T(1024)S(1)} all-reduce(f32[3212]{0:T(1024)S(1)} %pad_maximum_fusion.1), channel_id=1, replica_groups=mesh['seq'=64,'tp'=2] {'seq','tp'}, use_global_device_ids=true, to_apply=%region_9.10 | all-reduce | flops 3212 | bytes 25696 | tf_op jit(solution)/shard_map/psum | solution.py:966
  360.8 0.5 slice.50
  361.3 0.1 slice_multiply_fusion.2
  361.4 0.6 pad_maximum_fusion
  362.1 0.6 fusion.3
  362.7 51.4 %reduce-scatter.14.cloned.1.call-done = bf16[48,384]{1,0:T(8,128)(2,1)} async-done(((bf16[1536,384]{1,0:T(8,128)(2,1)}), bf16[48,384]{1,0:T(8,128)(2,1)}) %reduce-scatter.14.cloned.1.call-update) | async-done | bytes 36880 | tf_op jit(solution)/shard_map/reduce_scatter | solution.py:917
  414.1 0.8 convert_element_type.53
  414.9 2.9 collective-permute-start.3
  417.7 221.1 %reduce-scatter.12.cloned.1.call-done = bf16[48,384]{1,0:T(8,128)(2,1)} async-done(((bf16[1536,384]{1,0:T(8,128)(2,1)}), bf16[48,384]{1,0:T(8,128)(2,1)}) %reduce-scatter.12.cloned.1.call-update) | async-done | bytes 36880 | tf_op jit(solution)/shard_map/reduce_scatter | solution.py:917
  638.9 0.8 convert_element_type.51
  639.6 2.9 collective-permute-start.2
  642.6 221.0 %reduce-scatter.10.cloned.1.call-done = bf16[48,384]{1,0:T(8,128)(2,1)} async-done(((bf16[1536,384]{1,0:T(8,128)(2,1)}), bf16[48,384]{1,0:T(8,128)(2,1)}) %reduce-scatter.10.cloned.1.call-update) | async-done | bytes 36880 | tf_op jit(solution)/shard_map/reduce_scatter | solution.py:917
  863.6 0.8 convert_element_type.49
  864.4 2.9 collective-permute-start.1
  867.3 220.9 %reduce-scatter.8.cloned.1.call-done = bf16[48,384]{1,0:T(8,128)(2,1)} async-done(((bf16[1536,384]{1,0:T(8,128)(2,1)}), bf16[48,384]{1,0:T(8,128)(2,1)}) %reduce-scatter.8.cloned.1.call-update) | async-done | bytes 36880 | tf_op jit(solution)/shard_map/reduce_scatter | solution.py:917
  1088.2 0.8 convert_element_type.47
  1089.0 2.9 collective-permute-start
  1091.9 0.6 maximum_select_fusion.6
  1092.6 0.6 maximum_select_fusion.5
  1093.2 0.6 maximum_select_fusion.4
  1093.9 0.6 maximum_select_fusion.3
  1094.5 222.0 %reduce-scatter.20.cloned.1.call-done = bf16[48,1024]{1,0:T(8,128)(2,1)} async-done(((bf16[1536,1024]{1,0:T(8,128)(2,1)}), bf16[48,1024]{1,0:T(8,128)(2,1)}) %reduce-scatter.20.cloned.1.call-update) | async-done | bytes 98320 | tf_op jit(solution)/shard_map/reduce_scatter | solution.py:917
  1316.5 0.9 convert_element_type.59
  1317.4 2.9 collective-permute-start.6
  1320.4 224.4 %reduce-scatter.18.cloned.1.call-done = bf16[48,1024]{1,0:T(8,128)(2,1)} async-done(((bf16[1536,1024]{1,0:T(8,128)(2,1)}), bf16[48,1024]{1,0:T(8,128)(2,1)}) %reduce-scatter.18.cloned.1.call-update) | async-done | bytes 98320 | tf_op jit(solution)/shard_map/reduce_scatter | solution.py:917
  1544.8 0.9 convert_element_type.57
  1545.7 2.9 collective-permute-start.5
  1548.6 224.5 %reduce-scatter.16.cloned.1.call-done = bf16[48,1024]{1,0:T(8,128)(2,1)} async-done(((bf16[1536,1024]{1,0:T(8,128)(2,1)}), bf16[48,1024]{1,0:T(8,128)(2,1)}) %reduce-scatter.16.cloned.1.call-update) | async-done | bytes 98320 | tf_op jit(solution)/shard_map/reduce_scatter | solution.py:917
  1773.2 0.9 convert_element_type.55
  1774.1 2.9 collective-permute-start.4
  1777.0 0.7 maximum_select_fusion.2
  1777.7 0.7 maximum_select_fusion.1
  1778.4 0.7 maximum_select_fusion
  1779.1 0.7 copy.35
  1779.8 0.7 copy.36
  (52 shorter events, 0.6 us)
Async XLA Ops:
  7.2 406.9 %reduce-scatter.14.cloned.1.call-start = ((), (), s32[]{:S(2)}) async-start(), calls=%async_computation.10 | async-start | bytes 1216512 | tf_op jit(solution)/shard_map/reduce_scatter | solution.py:917
  170.5 468.3 %reduce-scatter.12.cloned.1.call-start = ((), (), s32[]{:S(2)}) async-start(), calls=%async_computation.9 | async-start | bytes 1216512 | tf_op jit(solution)/shard_map/reduce_scatter | solution.py:917
  221.7 53.9 %copy-start.1 = (bf16[256,1536]{1,0:T(8,128)(2,1)S(1)}, bf16[256,1536]{1,0:T(8,128)(2,1)}, u32[]{:S(2)}) copy-start(bf16[256,1536]{1,0:T(8,128)(2,1)} %get-tuple-element.48) | copy-start | bytes 2359300
  275.6 2.7 copy-start.3
  278.2 585.4 %reduce-scatter.10.cloned.1.call-start = ((), (), s32[]{:S(2)}) async-start(), calls=%async_computation.8 | async-start | bytes 1216512 | tf_op jit(solution)/shard_map/reduce_scatter | solution.py:917
  279.9 1.8 copy-start.2
  279.9 1.8 copy-start.6
  280.0 808.3 %reduce-scatter.8.cloned.1.call-start = ((), (), s32[]{:S(2)}) async-start(), calls=%async_computation.7 | async-start | bytes 1216512 | tf_op jit(solution)/shard_map/reduce_scatter | solution.py:917
  281.7 1034.8 %reduce-scatter.20.cloned.1.call-start = ((), (), s32[]{:S(2)}) async-start(), calls=%async_computation.13 | async-start | bytes 3244032 | tf_op jit(solution)/shard_map/reduce_scatter | solution.py:917
  284.4 1.1 copy-start
  284.4 1.3 copy-start.5
  284.5 1260.3 %reduce-scatter.18.cloned.1.call-start = ((), (), s32[]{:S(2)}) async-start(), calls=%async_computation.12 | async-start | bytes 3244032 | tf_op jit(solution)/shard_map/reduce_scatter | solution.py:917
  288.4 1.0 copy-start.4
  288.4 1484.7 %reduce-scatter.16.cloned.1.call-start = ((), (), s32[]{:S(2)}) async-start(), calls=%async_computation.11 | async-start | bytes 3244032 | tf_op jit(solution)/shard_map/reduce_scatter | solution.py:917
  292.2 0.7 copy-start.12
  292.2 0.9 copy-start.10
  292.2 1.0 copy-start.11
  292.2 69.2 %copy-start.9 = (f32[4,12,64]{2,0,1:T(4,128)S(1)}, f32[4,12,64]{2,0,1:T(4,128)}, u32[]{:S(2)}) copy-start(f32[4,12,64]{2,0,1:T(4,128)} %param.18) | copy-start | bytes 36868
  414.8 1364.2 %copy-start.7 = (f32[64,1536]{1,0:T(8,128)S(1)}, f32[64,1536]{1,0:T(8,128)}, u32[]{:S(2)}) copy-start(f32[64,1536]{1,0:T(8,128)} %get-tuple-element.100) | copy-start | bytes 1179652
  414.9 677.1 %collective-permute-start.3 = (f32[24,384]{1,0:T(8,128)S(1)}, f32[24,384]{1,0:T(8,128)S(1)}, u32[]{:S(2)}, u32[]{:S(2)}) collective-permute-start(f32[24,384]{1,0:T(8,128)S(1)} %get-tuple-element.70), channel_id=1, source_target_pairs={{0,2},{2,0},{4,6},{6,4},{8,10},{10,8},{12,14},{14,12},{16,18},{18,... | collective-permute-start | bytes 110600 | tf_op jit(solution)/shard_map/ppermute | solution.py:922
  639.6 452.9 %collective-permute-start.2 = (f32[24,384]{1,0:T(8,128)S(1)}, f32[24,384]{1,0:T(8,128)S(1)}, u32[]{:S(2)}, u32[]{:S(2)}) collective-permute-start(f32[24,384]{1,0:T(8,128)S(1)} %get-tuple-element.72), channel_id=1, source_target_pairs={{0,2},{2,0},{4,6},{6,4},{8,10},{10,8},{12,14},{14,12},{16,18},{18,... | collective-permute-start | bytes 110600 | tf_op jit(solution)/shard_map/ppermute | solution.py:922
  864.4 228.8 %collective-permute-start.1 = (f32[24,384]{1,0:T(8,128)S(1)}, f32[24,384]{1,0:T(8,128)S(1)}, u32[]{:S(2)}, u32[]{:S(2)}) collective-permute-start(f32[24,384]{1,0:T(8,128)S(1)} %get-tuple-element.74), channel_id=1, source_target_pairs={{0,2},{2,0},{4,6},{6,4},{8,10},{10,8},{12,14},{14,12},{16,18},{18,... | collective-permute-start | bytes 110600 | tf_op jit(solution)/shard_map/ppermute | solution.py:922
  1089.0 690.8 %copy-start.8 = (f32[64,1536]{1,0:T(8,128)S(1)}, f32[64,1536]{1,0:T(8,128)}, u32[]{:S(2)}) copy-start(f32[64,1536]{1,0:T(8,128)} %get-tuple-element.101) | copy-start | bytes 1179652
  1089.0 4.9 collective-permute-start
  1317.4 459.6 %collective-permute-start.6 = (f32[24,1024]{1,0:T(8,128)S(1)}, f32[24,1024]{1,0:T(8,128)S(1)}, u32[]{:S(2)}, u32[]{:S(2)}) collective-permute-start(f32[24,1024]{1,0:T(8,128)S(1)} %get-tuple-element.64), channel_id=1, source_target_pairs={{0,2},{2,0},{4,6},{6,4},{8,10},{10,8},{12,14},{14,12},{16,18},{18,... | collective-permute-start | bytes 294920 | tf_op jit(solution)/shard_map/ppermute | solution.py:922
  1545.7 232.0 %collective-permute-start.5 = (f32[24,1024]{1,0:T(8,128)S(1)}, f32[24,1024]{1,0:T(8,128)S(1)}, u32[]{:S(2)}, u32[]{:S(2)}) collective-permute-start(f32[24,1024]{1,0:T(8,128)S(1)} %get-tuple-element.66), channel_id=1, source_target_pairs={{0,2},{2,0},{4,6},{6,4},{8,10},{10,8},{12,14},{14,12},{16,18},{18,... | collective-permute-start | bytes 294920 | tf_op jit(solution)/shard_map/ppermute | solution.py:922
  1774.1 4.3 collective-permute-start.4
Sparse Core Ops, SparseCore 0:
  170.7 243.3 reduce-scatter.13
  419.0 219.8 reduce-scatter.11
  643.8 219.7 reduce-scatter.9
  868.4 219.7 reduce-scatter.7
  1093.1 223.3 reduce-scatter.19
  1321.4 223.3 reduce-scatter.17
  1549.8 223.3 reduce-scatter.15

commit v2 on v1

v2 whole, which is shorter than its diff:
```python
import math

import jax
import jax.numpy as jnp
from jax import lax
from jax.experimental import pallas as pl
from jax.experimental.pallas import tpu as pltpu
from jax.sharding import PartitionSpec as P

MESH = pl.DeviceIdType.MESH
BF = jnp.bfloat16
F32 = jnp.float32
EPS = 1e-06
LAMBDA_INIT = 0.8 - 0.6 * math.exp(-3.6)
OUT_SCALE = 1.0 - LAMBDA_INIT
D = 1536
CHIPS = 32
SERVED = 30
PER_HEAD = 5
ROWS = 64
BLOCK = 256
TILE = 128
SLOTS = 7
KB = 512
LOG2E = 1.4426950408889634
SCORE = 0.125 * LOG2E
VMEM_LIMIT = 60 * 2**20


def place():
    s = lax.axis_index("seq")
    return s // 2, s % 2, lax.axis_index("tp")


def owner_of(tile):
    step = (tile - 4) // 10
    pos = (tile - 4) % 10
    slot = jnp.where(step % 2 == 0, pos, 9 - pos)
    early = tile < 4
    return jnp.where(early, tile, slot), jnp.where(early, 0, step + 1)


def tile_of(slot, r):
    if r == 0:
        return slot
    return 4 + 10 * (r - 1) + (slot if (r - 1) % 2 == 0 else 9 - slot)


def matmul(a, b):
    return jnp.dot(a, b, preferred_element_type=F32)


def matmul_t(a, b):
    return lax.dot_general(a, b, (((1,), (1,)), ((), ())), preferred_element_type=F32)


def rms_scale(values, axis=-1):
    return lax.rsqrt(jnp.mean(values * values, axis=axis, keepdims=True) + EPS)


def norm_back(grad_normed, gain, rms, hat, axis=-1):
    scaled = grad_normed * gain
    return rms * (scaled - hat * jnp.mean(scaled * hat, axis=axis, keepdims=True))


def greet_all(chip, core, t):
    barrier = pltpu.get_barrier_semaphore()
    s = 2 * chip + core

    def greet(o, carry):
        pl.semaphore_signal(
            barrier, inc=1, device_id=(lax.rem(s + o, 2 * CHIPS), t), device_id_type=MESH
        )
        return carry

    lax.fori_loop(1, 2 * CHIPS, greet, 0)
    pl.semaphore_signal(barrier, inc=1, device_id=(s, 1 - t), device_id_type=MESH)
    pl.semaphore_wait(barrier, 2 * CHIPS)


def remote(src, dst, send_sem, recv_sem, s, t):
    return pltpu.make_async_remote_copy(
        src_ref=src,
        dst_ref=dst,
        send_sem=send_sem,
        recv_sem=recv_sem,
        device_id=(s, t),
        device_id_type=MESH,
    )


def rows_at(ref, start, count):
    return ref.at[pl.ds(pl.multiple_of(start, ROWS), count)]


class QuadGather:
    def __init__(self, buf, send, recv, chip, core, t):
        self.buf, self.send, self.recv = buf, send, recv
        self.chip, self.core, self.t = chip, core, t
        mine = core * 128 + t * ROWS
        self.mine = mine
        self.near = core * 128 + (1 - t) * ROWS
        sib = (2 * chip + 1 - core, t)
        self.to_near = self.copy(mine, 0, (2 * chip + core, 1 - t))
        self.to_sib = self.copy(mine, 1, sib)
        self.forward = self.copy(self.near, 2, sib)

    def copy(self, row, k, target):
        view = rows_at(self.buf, row, ROWS)
        return remote(view, view, self.send.at[k], self.recv.at[k], *target)

    def start(self):
        self.to_near.start()
        self.to_sib.start()

    def finish(self):
        self.to_near.wait_recv()
        self.forward.start()
        self.to_sib.wait_recv()
        self.forward.wait_recv()

    def drain(self):
        self.to_near.wait_send()
        self.to_sib.wait_send()
        self.forward.wait_send()


class RingGather:
    def __init__(self, pieces, land, send, recv, axis, chip, core, t):
        at = chip % 4 if axis == "x" else chip // 8
        self.local = pltpu.make_async_copy(pieces(at), land.at[at], recv.at[at])
        self.copies = []
        for k in (1, 3, 2):
            if axis == "x":
                peer, chip_to = (at + k) % 4, chip - at + (at + k) % 4
            else:
                peer, chip_to = (at + k) % 4, (chip + 8 * k) % CHIPS
            self.copies.append(
                remote(pieces(peer), land.at[at], send.at[k - 1], recv.at[at], 2 * chip_to + core, t)
            )
        self.waits = [
            pltpu.make_async_copy(pieces(at), land.at[k], recv.at[k]) for k in range(4)
        ]

    def start(self):
        self.local.start()
        for cp in self.copies:
            cp.start()

    def finish(self):
        for cp in self.waits:
            cp.wait()

    def drain(self):
        for cp in self.copies:
            cp.wait_send()


RING_SEMS = [pltpu.SemaphoreType.DMA((3,)), pltpu.SemaphoreType.DMA((4,))]


def greet_ring(chip, core, t):
    barrier = pltpu.get_barrier_semaphore()
    x = chip % 4
    for k in (1, 2, 3):
        for peer in ((chip + 8 * k) % CHIPS, chip - x + (x + k) % 4):
            pl.semaphore_signal(
                barrier, inc=1, device_id=(2 * peer + core, t), device_id_type=MESH
            )
    pl.semaphore_wait(barrier, 6)


def block_grad(dst, start, left, right, step):
    width = right.shape[1]

    def one(m, carry):
        cols = pl.ds(pl.multiple_of(m * step, 128), step)
        part = left[:, :, cols].reshape(4 * BLOCK, step)
        dst[cols, start : start + width] = lax.dot_general(
            part, right, (((0,), (0,)), ((), ())), preferred_element_type=F32
        ).astype(BF)
        return carry

    lax.fori_loop(0, left.shape[2] // step, one, 0)


CHUNK = 48


class Scatter:
    def __init__(self, part, land, send, recv, count, first, spot, chip, core, t):
        self.part, self.land, self.send, self.recv = part, land, send, recv
        self.count, self.first, self.spot = count, first, spot
        self.chip, self.core, self.t = chip, core, t

    def source(self, i):
        return self.part.at[pl.ds(pl.multiple_of(i * CHUNK, 16), CHUNK)]

    def each(self, start):
        def one(o, carry):
            i = lax.rem(self.chip + 1 + 3 * o, self.count)
            owner = self.first + i
            cp = remote(
                self.source(i), self.land.at[self.spot], self.send.at[i], self.recv.at[self.spot],
                2 * owner + self.core, self.t,
            )
            if start:

                @pl.when(owner == self.chip)
                def _():
                    pltpu.make_async_copy(
                        self.source(i), self.land.at[self.spot], self.recv.at[self.spot]
                    ).start()

            @pl.when(owner != self.chip)
            def _():
                if start:
                    cp.start()
                else:
                    cp.wait_send()

            return carry

        lax.fori_loop(0, self.count, one, 0)

    def wait(self):
        def one(k, carry):
            pltpu.make_async_copy(self.source(0), self.land.at[k], self.recv.at[k]).wait()
            return carry

        lax.fori_loop(0, self.count, one, 0)

    def total(self, b, cols):
        def one(k, carry):
            return carry + self.land[8 * b + k, :, cols].astype(F32)

        return lax.fori_loop(0, 8, one, jnp.zeros((CHUNK, cols.stop - cols.start), F32))


def scatter_sems(count):
    return [pltpu.SemaphoreType.DMA((count,)), pltpu.SemaphoreType.DMA((count,))]


GATHER_SEMS = [pltpu.SemaphoreType.DMA((3,)), pltpu.SemaphoreType.DMA((3,))]
CW = 512
NC = D // CW


class QuadReduce:
    def __init__(self, part, dsend, drecv, ysend, yrecv, ds, dr, ys, yr, chip, core, t):
        self.part, self.dsend, self.drecv = part, dsend, drecv
        self.ysend, self.yrecv = ysend, yrecv
        self.core, self.t = core, t
        self.d = [
            remote(dsend.at[k], drecv.at[k], ds.at[k], dr.at[k], 2 * chip + 1 - core, t)
            for k in range(NC)
        ]
        self.y = [
            remote(ysend.at[k], yrecv.at[k], ys.at[k], yr.at[k], 2 * chip + core, 1 - t)
            for k in range(NC)
        ]

    def rows(self, start, count, k):
        return self.part[pl.ds(pl.multiple_of(start, ROWS), count), k * CW : (k + 1) * CW]

    def put(self, k, value):
        self.part[:, k * CW : (k + 1) * CW] = value
        self.dsend[k] = self.rows((1 - self.core) * 128, 128, k).astype(BF)
        self.d[k].start()

    def middle(self, k):
        self.d[k].wait_recv()
        near = (1 - self.t) * ROWS
        far = self.rows(self.core * 128 + near, ROWS, k)
        got = self.drecv[k, pl.ds(pl.multiple_of(near, ROWS), ROWS), :]
        self.ysend[k] = (far + got.astype(F32)).astype(BF)
        self.y[k].start()

    def result(self, k):
        mine = self.t * ROWS
        own = self.rows(self.core * 128 + mine, ROWS, k)
        got = self.drecv[k, pl.ds(pl.multiple_of(mine, ROWS), ROWS), :].astype(F32)
        self.y[k].wait_recv()
        return own + got + self.yrecv[k].astype(F32)

    def run(self, term):
        for k in range(NC):
            self.put(k, term(k))
            if k:
                self.middle(k - 1)
        self.middle(NC - 1)

    def drain(self):
        for k in range(NC):
            self.d[k].wait_send()
            self.y[k].wait_send()


REDUCE_SCRATCH = [
    pltpu.VMEM((BLOCK, D), F32),
    pltpu.VMEM((NC, 128, CW), BF),
    pltpu.VMEM((NC, 128, CW), BF),
    pltpu.VMEM((NC, ROWS, CW), BF),
    pltpu.VMEM((NC, ROWS, CW), BF),
] + [pltpu.SemaphoreType.DMA((NC,))] * 4


def tile_sends(tiles, land, send, recv, chip, core, t, start):
    s = 2 * chip + core
    for j in range(3):
        for u in range(2):
            slot, index = owner_of(2 * chip + u)
            target = (core * 3 + j) * 10 + slot
            k = j * 2 + u

            if start:

                @pl.when(target == s)
                def _():
                    pltpu.make_async_copy(tiles.at[j, u], land.at[index], recv.at[index]).start()

            @pl.when(target != s)
            def _():
                cp = remote(tiles.at[j, u], land.at[index], send.at[k], recv.at[index], target, t)
                if start:
                    cp.start()
                else:
                    cp.wait_send()


def tile_waits(tiles, land, send, recv, chip, core, t):
    slot = (2 * chip + core) % 10
    for r in range(SLOTS):
        here = chip < SERVED
        if r == 0:
            here = jnp.logical_and(here, slot < 4)

        @pl.when(here)
        def _():
            pltpu.make_async_copy(tiles.at[0, 0], land.at[r], recv.at[r]).wait()


def home_sends(tiles, land, send, recv, chip, core, t, start):
    s = 2 * chip + core
    slot = s % 10
    head = chip // PER_HEAD
    for r in range(SLOTS):
        here = chip < SERVED
        if r == 0:
            here = jnp.logical_and(here, slot < 4)
        tile = tile_of(slot, r)
        target = (tile // 2) * 2 + head // 3
        j, u = head % 3, tile % 2

        if start:

            @pl.when(jnp.logical_and(here, target == s))
            def _():
                pltpu.make_async_copy(tiles.at[r], land.at[j, u], recv.at[j, u]).start()

        @pl.when(jnp.logical_and(here, target != s))
        def _():
            cp = remote(tiles.at[r], land.at[j, u], send.at[r], recv.at[j, u], target, t)
            if start:
                cp.start()
            else:
                cp.wait_send()


def home_waits(tiles, land, recv):
    for j in range(3):
        for u in range(2):
            pltpu.make_async_copy(tiles.at[0], land.at[j, u], recv.at[j, u]).wait()


def weight_load(ref, buf, sem, core, width):
    return pltpu.make_async_copy(
        ref.at[:, pl.ds(pl.multiple_of(core * width, 128), width)], buf, sem
    )


def project_kernel(
    x_ref, cot_ref, mask_ref, gain_ref, wq_ref, wk_ref, wv_ref,
    normed_ref, dout_ref, q_ref, kv_ref,
    nbuf, obuf, wbuf, kvsrc, qsrc, wsem, nsend, nrecv, osend, orecv, kvsend, kvrecv, fsend, qsend,
    qrecv, osem,
):
    chip, core, t = place()
    s = 2 * chip + core
    loads = [
        weight_load(ref, wbuf.at[k], wsem.at[k], core, 384)
        for k, ref in enumerate((wk_ref, wv_ref, wq_ref))
    ]
    for load in loads:
        load.start()
    x = x_ref[...]
    normed = (x * rms_scale(x) * gain_ref[...]).astype(BF)
    quad = QuadGather(nbuf, nsend, nrecv, chip, core, t)
    mine = pl.ds(pl.multiple_of(quad.mine, ROWS), ROWS)
    nbuf[mine, :] = normed
    quad_o = QuadGather(obuf, osend, orecv, chip, core, t)
    greet_all(chip, core, t)
    quad.start()
    obuf[mine, :] = (cot_ref[...] * mask_ref[...]).astype(BF)
    quad.finish()
    saves = pieces_out(nbuf, normed_ref, osem, 0, 4)
    for k in range(2):
        loads[k].wait()
        value = matmul(nbuf[...], wbuf[k]).astype(BF)
        for j in range(3):
            kvsrc[j, :, k * 128 : (k + 1) * 128] = value[:, j * 128 : (j + 1) * 128]

    def kv_sends(start):
        def one(o, carry):
            w = lax.rem(chip + 7 * o, 3 * PER_HEAD)
            j = w // PER_HEAD
            target = 2 * (core * 3 * PER_HEAD + w) + chip % 2
            if start:

                @pl.when(target == s)
                def _():
                    pltpu.make_async_copy(kvsrc.at[j], kv_ref.at[chip], kvrecv.at[chip]).start()

            @pl.when(target != s)
            def _():
                cp = remote(kvsrc.at[j], kv_ref.at[chip], kvsend.at[w], kvrecv.at[chip], target, t)
                if start:
                    cp.start()
                else:
                    cp.wait_send()

            return carry

        lax.fori_loop(0, 3 * PER_HEAD, one, 0)

    kv_sends(True)
    loads[2].wait()
    value = matmul(nbuf[...], wbuf[2]).astype(BF)
    for j in range(3):
        for u in range(2):
            qsrc[j, u] = value[u * 128 : (u + 1) * 128, j * 128 : (j + 1) * 128]
    tile_sends(qsrc, q_ref, qsend, qrecv, chip, core, t, True)
    quad_o.start()

    @pl.when(chip < SERVED)
    def _():
        def forward(o):
            source = lax.rem((chip // 2 + o) * 2 + core, CHIPS)
            view = kv_ref.at[source]
            return source, remote(view, view, fsend.at[o], kvrecv.at[source], s + 1 - 2 * core, t)

        def take(o, carry):
            source, cp = forward(o)
            pltpu.make_async_copy(kvsrc.at[0], kv_ref.at[source], kvrecv.at[source]).wait()
            cp.start()
            return carry

        lax.fori_loop(0, CHIPS // 2, take, 0)

        def finish(o, carry):
            source = 2 * o + 1 - core
            pltpu.make_async_copy(kvsrc.at[0], kv_ref.at[source], kvrecv.at[source]).wait()
            forward(o)[1].wait_send()
            return carry

        lax.fori_loop(0, CHIPS // 2, finish, 0)

    quad_o.finish()
    saves += pieces_out(obuf, dout_ref, osem, 4, 2)
    tile_waits(qsrc, q_ref, qsend, qrecv, chip, core, t)
    kv_sends(False)
    tile_sends(qsrc, q_ref, qsend, qrecv, chip, core, t, False)
    quad.drain()
    quad_o.drain()
    for save in saves:
        save.wait()


def pieces_out(buf, ref, sem, first, count):
    width = D // count
    copies = [
        pltpu.make_async_copy(
            buf.at[:, a * width : (a + 1) * width], ref.at[a], sem.at[first + a]
        )
        for a in range(count)
    ]
    for cp in copies:
        cp.start()
    return copies


VM = pl.BlockSpec(memory_space=pltpu.VMEM)
SM = pl.BlockSpec(memory_space=pltpu.SMEM)
ANY = pl.BlockSpec(memory_space=pl.ANY)


def shape(dims, dtype):
    return jax.ShapeDtypeStruct(dims, dtype)


HALVES = (2, BLOCK, 768)
QUARTERS = (4, BLOCK, 384)


def project(x, cot, mask, gain, wq, wk, wv):
    return pl.pallas_call(
        project_kernel,
        name="project",
        out_shape=(
            shape(QUARTERS, BF),
            shape(HALVES, BF),
            shape((SLOTS, TILE, 128), BF),
            shape((CHIPS, BLOCK, 256), BF),
        ),
        in_specs=[VM, VM, VM, VM, ANY, ANY, ANY],
        out_specs=(ANY,) * 4,
        scratch_shapes=[
            pltpu.VMEM((BLOCK, D), BF),
            pltpu.VMEM((BLOCK, D), BF),
            pltpu.VMEM((3, D, 384), BF),
            pltpu.VMEM((3, BLOCK, 256), BF),
            pltpu.VMEM((3, 2, TILE, 128), BF),
            pltpu.SemaphoreType.DMA((3,)),
            *(GATHER_SEMS * 2),
            pltpu.SemaphoreType.DMA((15,)),
            pltpu.SemaphoreType.DMA((CHIPS,)),
            pltpu.SemaphoreType.DMA((CHIPS // 2,)),
            pltpu.SemaphoreType.DMA((6,)),
            pltpu.SemaphoreType.DMA((SLOTS,)),
            pltpu.SemaphoreType.DMA((6,)),
        ],
        compiler_params=pltpu.CompilerParams(
            collective_id=0, has_side_effects=True, vmem_limit_bytes=VMEM_LIMIT
        ),
    )(x, cot, mask, gain, wq, wk, wv)


def eye():
    row = lax.broadcasted_iota(jnp.int32, (128, 128), 0)
    col = lax.broadcasted_iota(jnp.int32, (128, 128), 1)
    return jnp.where(row == col, 1.0, 0.0).astype(BF)


def both_maps(q_t):
    top = lax.broadcasted_iota(jnp.int32, q_t.shape, 0) < 64
    return jnp.concatenate([jnp.where(top, q_t, 0.0), jnp.where(top, 0.0, q_t)], axis=1)


def key_mask(start, count, tile, width):
    key = start + lax.broadcasted_iota(jnp.int32, (count, width), 0)
    query = tile * TILE + lax.broadcasted_iota(jnp.int32, (count, width), 1) % TILE
    return key <= query


def group_norm(parts, lam):
    first, second = parts[:, :TILE], parts[:, TILE:]
    differ = first - lam * second
    rms = rms_scale(differ, 0)
    return rms, differ * rms


def lambda_of(lambdas_ref, chip, t):
    first = jnp.exp(jnp.sum(lambdas_ref[0] * lambdas_ref[1], axis=-1, keepdims=True))
    second = jnp.exp(jnp.sum(lambdas_ref[2] * lambdas_ref[3], axis=-1, keepdims=True))
    every = first - second + LAMBDA_INIT
    mine = lax.broadcasted_iota(jnp.int32, every.shape, 0) == 6 * t + chip // PER_HEAD
    return jnp.sum(jnp.where(mine, every, 0.0), axis=0, keepdims=True)


STEP = 2048


def attend_kernel(
    lambdas_ref, gain_ref, q_ref, kv_ref, normed_ref,
    mixed_ref, parts_ref, log_ref, xnormed_ref, znormed_ref,
    v_t, kmax, acc, total, *sems,
):
    chip, core, t = place()
    slot = (2 * chip + core) % 10
    served = chip < SERVED
    keys = CHIPS * BLOCK
    greet_ring(chip, core, t)
    gathers = [
        RingGather(lambda p: normed_ref.at[p], xnormed_ref, *sems[:2], "x", chip, core, t),
        RingGather(lambda p: normed_ref.at[p], znormed_ref, *sems[2:], "z", chip, core, t),
    ]
    for gather in gathers:
        gather.start()
    lam = lambda_of(lambdas_ref, chip, t)

    @pl.when(served)
    def _():
        unit = eye()

        def flip(b, best):
            for u in range(2):
                start = pl.multiple_of(b * 2 * KB + u * KB, KB)
                block = kv_ref[pl.ds(start, KB), :]
                v_t[:, pl.ds(start, KB)] = matmul_t(unit, block[:, 128:]).astype(BF)
                k_t = matmul_t(unit, block[:, :128])
                square = k_t * k_t
                best = (
                    jnp.maximum(best[0], jnp.sum(square[:64], axis=0, keepdims=True)),
                    jnp.maximum(best[1], jnp.sum(square[64:], axis=0, keepdims=True)),
                )
            return best

        zero = jnp.zeros((1, KB), F32)
        best = lax.fori_loop(0, keys // (2 * KB), flip, (zero, zero))
        for m in range(2):
            kmax[m] = jnp.max(best[m])

    for r in range(SLOTS):
        tile = tile_of(slot, r)

        @pl.when(served if r else jnp.logical_and(served, slot < 4))
        def _():
            q_t = q_ref[r].astype(F32).T
            square = q_t * q_t
            bound = SCORE * jnp.concatenate(
                [
                    jnp.sqrt(jnp.sum(square[:64], axis=0, keepdims=True) * kmax[0]),
                    jnp.sqrt(jnp.sum(square[64:], axis=0, keepdims=True) * kmax[1]),
                ],
                axis=1,
            )
            q_both = both_maps(q_t).astype(BF)
            acc[...] = jnp.zeros_like(acc)
            total[...] = jnp.zeros_like(total)

            def step(b, masked):
                sums, out = None, None
                for u in range(STEP // KB):
                    start = pl.multiple_of(b * STEP + u * KB, KB)
                    score = matmul(kv_ref[pl.ds(start, KB), :128], q_both)
                    prob = jnp.exp2(score * SCORE - bound)
                    if masked:
                        prob = jnp.where(key_mask(start, KB, tile, 2 * TILE), prob, 0.0)
                    part = jnp.sum(prob.reshape(KB // 8, 8, 2 * TILE), axis=0)
                    term = matmul(v_t[:, pl.ds(start, KB)], prob.astype(BF))
                    sums = part if sums is None else sums + part
                    out = term if out is None else out + term
                total[...] += sums
                acc[...] += out

            full = tile * TILE // STEP

            def body(b, carry):
                step(b, False)
                return carry

            lax.fori_loop(0, full, body, 0)
            step(full, True)
            whole = jnp.sum(total[...], axis=0, keepdims=True)
            parts = acc[...] / whole
            parts_ref[r] = parts
            log_ref[r] = bound + jnp.log(whole) * LOG2E
            rms, hat = group_norm(parts, lam)
            mixed_ref[r] = (hat * gain_ref[...] * OUT_SCALE).T.astype(BF)

    for gather in gathers:
        gather.finish()
        gather.drain()


GATHERED = (4, BLOCK, 768)
GATHERED_Q = (4, BLOCK, 384)


def attend(lambdas, gain, q, kv, normed):
    return pl.pallas_call(
        attend_kernel,
        name="attend",
        out_shape=(
            shape((SLOTS, TILE, 128), BF),
            shape((SLOTS, 128, 2 * TILE), F32),
            shape((SLOTS, 1, 2 * TILE), F32),
            shape(GATHERED_Q, BF),
            shape(GATHERED_Q, BF),
        ),
        in_specs=[VM, VM, VM, VM, ANY],
        out_specs=(VM, VM, VM, ANY, ANY),
        scratch_shapes=[
            pltpu.VMEM((128, CHIPS * BLOCK), BF),
            pltpu.SMEM((2,), F32),
            pltpu.VMEM((128, 2 * TILE), F32),
            pltpu.VMEM((8, 2 * TILE), F32),
            *(RING_SEMS * 2),
        ],
        compiler_params=pltpu.CompilerParams(
            collective_id=3, has_side_effects=True, vmem_limit_bytes=VMEM_LIMIT
        ),
    )(lambdas, gain, q, kv, normed)


def middle_kernel(
    x_ref, cot_ref, mask_ref, gain_ref, tiles_ref, wo_ref, wg_ref, wu_ref, wd_ref,
    dout_ref,
    out_ref, dres_ref, gainpart_ref, dresall_ref, dmix_ref,
    lffn_ref, lgu_ref, lhid_ref, ldout_ref, lmix_ref,
    land, wo, wg, wu, wd, fbuf, rbuf, dms, doutall_ref, gu_ref, hid_ref, mix_ref, *rest,
):
    chip, core, t = place()
    reduces = [rest[9 * k : 9 * k + 9] for k in range(3)]
    gathers = [rest[27 + 2 * k : 29 + 2 * k] for k in range(2)]
    wsem, hsend, hrecv, tsend, trecv, osem = rest[31:37]
    sems = rest[37:]
    ring_dout = RingGather(lambda p: doutall_ref.at[p // 2], ldout_ref, *sems[0:2], "z", chip, core, t)
    ring_mix = RingGather(lambda p: mix_ref, lmix_ref, *sems[2:4], "x", chip, core, t)
    ring_ffn = RingGather(
        lambda p: fbuf.at[:, pl.ds(pl.multiple_of((p // 2) * 768, 128), 768)],
        lffn_ref, *sems[4:6], "x", chip, core, t,
    )
    ring_hid = RingGather(lambda p: hid_ref.at[p % 2], lhid_ref, *sems[6:8], "z", chip, core, t)
    ring_gu = RingGather(lambda p: gu_ref.at[p % 2], lgu_ref, *sems[8:10], "x", chip, core, t)
    rings = (ring_dout, ring_mix, ring_ffn, ring_hid, ring_gu)
    take_dout = pltpu.make_async_copy(dout_ref, doutall_ref, osem.at[4])
    take_dout.start()
    loads = [
        weight_load(wo_ref, wo, wsem.at[0], core, 384),
        weight_load(wg_ref, wg, wsem.at[1], core, 1024),
        weight_load(wu_ref, wu, wsem.at[2], core, 1024),
        weight_load(wd_ref, wd, wsem.at[3], core, 1024),
    ]
    for load in loads:
        load.start()
    gather_f = QuadGather(fbuf, *gathers[0], chip, core, t)
    gather_r = QuadGather(rbuf, *gathers[1], chip, core, t)
    mine = pl.ds(pl.multiple_of(gather_f.mine, ROWS), ROWS)
    dout = cot_ref[...] * mask_ref[...]
    greet_all(chip, core, t)
    home_sends(tiles_ref, land, hsend, hrecv, chip, core, t, True)
    take_dout.wait()
    ring_dout.start()
    loads[0].wait()
    home_waits(tiles_ref, land, hrecv)
    for j in range(3):
        for u in range(2):
            mix_ref[u * 128 : (u + 1) * 128, j * 128 : (j + 1) * 128] = land[j, u]
    ring_mix.start()
    red = QuadReduce(*reduces[0], chip, core, t)
    red.run(lambda k: matmul_t(mix_ref[...], wo[k * CW : (k + 1) * CW, :]))
    resid = x_ref[...] + jnp.concatenate([red.result(k) for k in range(NC)], axis=1)
    ffn_rms = rms_scale(resid)
    ffn_hat = resid * ffn_rms
    fbuf[mine, :] = (ffn_hat * gain_ref[...]).astype(BF)
    gather_f.start()
    gather_f.finish()
    ring_ffn.start()
    for load in loads[1:]:
        load.wait()

    def hidden_step(n, carry):
        cols = pl.ds(pl.multiple_of(n * 256, 256), 256)
        b, at = n // 2, n % 2
        gate = matmul(fbuf[...], wg[:, cols])
        up = matmul(fbuf[...], wu[:, cols])
        d_hidden = matmul(doutall_ref[0], wd[:768, cols]) + matmul(doutall_ref[1], wd[768:, cols])
        sig = 1.0 / (1.0 + jnp.exp(-gate))
        silu = gate * sig
        to = pl.ds(pl.multiple_of(at * 256, 256), 256)
        up_to = pl.ds(pl.multiple_of(512 + at * 256, 256), 256)
        hid_ref[b, :, to] = (silu * up).astype(BF)
        gu_ref[b, :, to] = (d_hidden * up * sig * (1.0 + gate * (1.0 - sig))).astype(BF)
        gu_ref[b, :, up_to] = (d_hidden * silu).astype(BF)
        return carry

    lax.fori_loop(0, 4, hidden_step, 0)
    ring_hid.start()
    ring_gu.start()
    red2 = QuadReduce(*reduces[1], chip, core, t)

    def ffn_term(k):
        rows = slice(k * CW, (k + 1) * CW)
        return (
            matmul_t(gu_ref[0, :, :512], wg[rows, :512])
            + matmul_t(gu_ref[1, :, :512], wg[rows, 512:])
            + matmul_t(gu_ref[0, :, 512:], wu[rows, :512])
            + matmul_t(gu_ref[1, :, 512:], wu[rows, 512:])
        )

    red2.run(ffn_term)
    red3 = QuadReduce(*reduces[2], chip, core, t)
    d_ffn = jnp.concatenate([red2.result(k) for k in range(NC)], axis=1)
    gainpart_ref[...] = jnp.sum(d_ffn * ffn_hat, axis=0, keepdims=True)
    d_resid = dout + norm_back(d_ffn, gain_ref[...], ffn_rms, ffn_hat)
    dres_ref[...] = d_resid
    rbuf[mine, :] = d_resid.astype(BF)
    gather_r.start()
    red3.run(
        lambda k: matmul_t(hid_ref[0], wd[k * CW : (k + 1) * CW, :512])
        + matmul_t(hid_ref[1], wd[k * CW : (k + 1) * CW, 512:])
    )
    gather_r.finish()
    d_mixed = matmul(rbuf[...], wo[...]).astype(BF)
    for j in range(3):
        for u in range(2):
            dms[j, u] = d_mixed[u * 128 : (u + 1) * 128, j * 128 : (j + 1) * 128]
    tile_sends(dms, dmix_ref, tsend, trecv, chip, core, t, True)
    saves = pieces_out(rbuf, dresall_ref, osem, 0, 4)
    out_ref[...] = resid + jnp.concatenate([red3.result(k) for k in range(NC)], axis=1)
    tile_waits(dms, dmix_ref, tsend, trecv, chip, core, t)
    tile_sends(dms, dmix_ref, tsend, trecv, chip, core, t, False)
    home_sends(tiles_ref, land, hsend, hrecv, chip, core, t, False)
    for gather in (gather_f, gather_r):
        gather.drain()
    for reduce in (red, red2, red3):
        reduce.drain()
    for save in saves:
        save.wait()
    for ring in rings:
        ring.finish()
        ring.drain()


def middle(x, cot, mask, gain, tiles, wo, wg, wu, wd, dout_all):
    return pl.pallas_call(
        middle_kernel,
        name="middle",
        out_shape=(
            shape((ROWS, D), F32),
            shape((ROWS, D), F32),
            shape((1, D), F32),
            shape(QUARTERS, BF),
            shape((SLOTS, TILE, 128), BF),
            shape(GATHERED, BF),
            shape((4, BLOCK, 1024), BF),
            shape((4, BLOCK, 512), BF),
            shape(GATHERED, BF),
            shape(GATHERED_Q, BF),
        ),
        in_specs=[VM, VM, VM, VM] + [ANY] * 6,
        out_specs=(VM, VM, VM) + (ANY,) * 7,
        scratch_shapes=[
            pltpu.VMEM((3, 2, TILE, 128), BF),
            pltpu.VMEM((D, 384), BF),
            pltpu.VMEM((D, 1024), BF),
            pltpu.VMEM((D, 1024), BF),
            pltpu.VMEM((D, 1024), BF),
            pltpu.VMEM((BLOCK, D), BF),
            pltpu.VMEM((BLOCK, D), BF),
            pltpu.VMEM((3, 2, TILE, 128), BF),
            pltpu.VMEM(HALVES, BF),
            pltpu.VMEM((2, BLOCK, 1024), BF),
            pltpu.VMEM((2, BLOCK, 512), BF),
            pltpu.VMEM((BLOCK, 384), BF),
            *(REDUCE_SCRATCH * 3),
            *(GATHER_SEMS * 2),
            pltpu.SemaphoreType.DMA((4,)),
            pltpu.SemaphoreType.DMA((SLOTS,)),
            pltpu.SemaphoreType.DMA((3, 2)),
            pltpu.SemaphoreType.DMA((6,)),
            pltpu.SemaphoreType.DMA((SLOTS,)),
            pltpu.SemaphoreType.DMA((5,)),
            *(RING_SEMS * 5),
        ],
        compiler_params=pltpu.CompilerParams(
            collective_id=1, has_side_effects=True, vmem_limit_bytes=VMEM_LIMIT
        ),
    )(x, cot, mask, gain, tiles, wo, wg, wu, wd, dout_all)


SPAN = 1024
SPANS = CHIPS * BLOCK // SPAN
PER_SPAN = SPAN // BLOCK // 2


def attend_back_kernel(
    lambdas_ref, gain_ref, q_ref, kv_ref, dmix_ref, parts_ref, log_ref,
    lffn_ref, lgu_ref, lhid_ref, ldout_ref, dres_ref,
    dqkv_ref, small_ref, gate_ref, up_ref, down_ref, xdres_ref,
    k_t, acc, q_cols, q_rows, d_cols, d_rows, deltas, dq_acc, dq_out, own, given, sib, both, home, land,
    lffn, lgu, lhid, ldout, pgu, pdown, sgu, sdown, swap, swapped, *sems,
):
    chip, core, t = place()
    s = 2 * chip + core
    slot = s % 10
    head = chip // PER_HEAD
    served = chip < SERVED
    x, z = chip % 4, chip // 8
    loads = [
        pltpu.make_async_copy(src, dst, sems[0].at[k])
        for k, (src, dst) in enumerate(
            ((lhid_ref, lhid), (ldout_ref, ldout), (lffn_ref, lffn), (lgu_ref, lgu))
        )
    ]
    for load in loads:
        load.start()
    lam = lambda_of(lambdas_ref, chip, t)
    greet_all(chip, core, t)
    ring_dres = RingGather(lambda p: dres_ref.at[p], xdres_ref, *sems[1:3], "x", chip, core, t)
    send_down = Scatter(
        pdown, sdown, *sems[3:5], 16, 16 * (z // 2), 8 * (z % 2) + chip % 8, chip, core, t
    )
    send_gu = Scatter(
        pgu, sgu, *sems[5:7], 16, 16 * (x // 2), 8 * (x % 2) + chip // 4, chip, core, t
    )
    swap_sem, dsend, drecv, ksend, krecv, hsend, hrecv = sems[7:]
    loads[0].wait()
    loads[1].wait()
    block_grad(pdown, 0, ldout, lhid[...].reshape(4 * BLOCK, 512), 256)
    send_down.each(True)
    loads[2].wait()
    loads[3].wait()
    block_grad(pgu, 0, lffn, lgu[:, :, :512].reshape(4 * BLOCK, 512), 256)
    block_grad(pgu, 512, lffn, lgu[:, :, 512:].reshape(4 * BLOCK, 512), 256)
    send_gu.each(True)
    ring_dres.start()
    small_ref[...] = jnp.zeros_like(small_ref)

    def to_sibling(o):
        return remote(given.at[o], sib.at[o], dsend.at[o], drecv.at[o], s + 1 - 2 * core, t)

    def to_home(o, start):
        target = 2 * (2 * o + core) + head // 3
        spot = (head % 3) * PER_HEAD + chip % PER_HEAD
        if start:

            @pl.when(target == s)
            def _():
                pltpu.make_async_copy(both.at[o], home.at[spot], krecv.at[spot]).start()

        @pl.when(target != s)
        def _():
            cp = remote(both.at[o], home.at[spot], ksend.at[o], krecv.at[spot], target, t)
            if start:
                cp.start()
            else:
                cp.wait_send()

    def tile_at(r):
        late = 4 + 10 * (r - 1) + jnp.where((r - 1) % 2 == 0, slot, 9 - slot)
        return jnp.where(r == 0, slot, late)

    @pl.when(served)
    def _():
        unit = eye()

        def flip(b, carry):
            for u in range(2):
                rows = pl.ds(pl.multiple_of(b * 2 * KB + u * KB, KB), KB)
                k_t[:, rows] = matmul_t(unit, kv_ref[rows, :128]).astype(BF)
            return carry

        lax.fori_loop(0, SPANS, flip, 0)

    for r in range(SLOTS):

        @pl.when(served if r else jnp.logical_and(served, slot < 4))
        def _():
            q_cols[r] = both_maps(q_ref[r].astype(F32).T).astype(BF)
            q = q_ref[r].astype(F32)
            left = lax.broadcasted_iota(jnp.int32, q.shape, 1) < 64
            q_rows[r] = jnp.concatenate(
                [jnp.where(left, q, 0.0), jnp.where(left, 0.0, q)], axis=0
            ).astype(BF)
            parts = parts_ref[r]
            first, second = parts[:, :TILE], parts[:, TILE:]
            rms, hat = group_norm(parts, lam)
            e_t = dmix_ref[r].astype(F32).T * OUT_SCALE
            column = jnp.sum(e_t * hat, axis=1, keepdims=True)
            d_differ = norm_back(e_t, gain_ref[...], rms, hat, 0).astype(BF)
            d_wide = d_differ.astype(F32)
            d_cols[r] = d_differ
            d_rows[r] = d_wide.T.astype(BF)
            second_dot = jnp.sum(d_wide * second, axis=0, keepdims=True)
            row = lax.broadcasted_iota(jnp.int32, (128, 128), 0)
            lane = lax.broadcasted_iota(jnp.int32, (128, 128), 1)
            small_ref[0:1, :] += jnp.sum(jnp.where(row == lane, column, 0.0), axis=0, keepdims=True)
            here = lax.broadcasted_iota(jnp.int32, (1, 128), 1) == 6 * t + head
            small_ref[1:2, :] -= jnp.where(here, jnp.sum(second_dot, axis=1, keepdims=True), 0.0)
            deltas[r, 0:1, :] = jnp.sum(d_wide * first, axis=0, keepdims=True)
            deltas[r, 1:2, :] = -lam * second_dot
            dq_acc[r] = jnp.zeros((128, 2 * TILE), F32)

    @pl.when(served)
    def _():
        def span(k, carry):
            b = lax.rem(chip + k, SPANS)
            start = pl.multiple_of(b * SPAN, SPAN)
            rows = pl.ds(start, SPAN)
            acc[...] = jnp.zeros_like(acc)

            def step(r, masked):
                block = kv_ref[rows, :]
                score = matmul(block[:, :128], q_cols[r])
                prob = jnp.exp2(score * SCORE - log_ref[r])
                if masked:
                    prob = jnp.where(key_mask(start, SPAN, tile_at(r), 2 * TILE), prob, 0.0)
                upper = matmul(block[:, 128:], d_cols[r])
                p1, p2 = prob[:, :TILE], prob[:, TILE:]
                ds = jnp.concatenate(
                    [p1 * (upper - deltas[r, 0:1, :]), p2 * (-lam * upper - deltas[r, 1:2, :])],
                    axis=1,
                ).astype(BF)
                mix = (p1 - lam * p2).astype(BF)
                acc[:, :128] += matmul(ds, q_rows[r])
                acc[:, 128:] += matmul(mix, d_rows[r])
                dq_acc[r] += matmul(k_t[:, rows], ds)

            def masked_step(r, carry):
                step(r, True)
                return carry

            def full_step(r, carry):
                step(r, False)
                return carry

            reach, past = 0, 0
            for r in range(SLOTS):
                last = tile_of(slot, r) * TILE // SPAN
                counts = (slot < 4) if r == 0 else True
                reach += jnp.where(jnp.logical_and(counts, last >= b), 1, 0)
                past += jnp.where(jnp.logical_and(counts, last > b), 1, 0)
            lax.fori_loop(SLOTS - reach, SLOTS - past, masked_step, 0)
            lax.fori_loop(SLOTS - past, SLOTS, full_step, 0)
            for u in range(PER_SPAN):
                o = PER_SPAN * b + u
                for ref, which in ((given, 1 - core), (own, core)):
                    part = acc[pl.ds(pl.multiple_of((2 * u + which) * BLOCK, BLOCK), BLOCK), :]
                    ref[o, :, :128] = (part[:, :128] * 0.125).astype(BF)
                    ref[o, :, 128:] = part[:, 128:].astype(BF)
                to_sibling(o).start()

            @pl.when(k > 0)
            def _():
                pass_on(k - 1)

            return carry

        def pass_on(k):
            for u in range(PER_SPAN):
                o = PER_SPAN * lax.rem(chip + k, SPANS) + u
                to_sibling(o).wait_recv()
                both[o] = (own[o].astype(F32) + sib[o].astype(F32)).astype(BF)
                to_home(o, True)

        lax.fori_loop(0, SPANS, span, 0)
        pass_on(SPANS - 1)

    for r in range(SLOTS):

        @pl.when(served if r else jnp.logical_and(served, slot < 4))
        def _():
            dq_t = jnp.concatenate([dq_acc[r, :64, :TILE], dq_acc[r, 64:, TILE:]], axis=0)
            dq_out[r] = (dq_t * 0.125).T.astype(BF)

    home_sends(dq_out, land, hsend, hrecv, chip, core, t, True)
    send_down.wait()
    for b in range(2):
        total = send_down.total(b, slice(0, 512))
        for h in range(2):
            swap[h, :, 2048 + b * 512 : 2560 + b * 512] = total[h * 24 : h * 24 + 24]
    send_gu.wait()
    for b in range(2):
        for m in range(2):
            total = send_gu.total(b, slice(m * 512, m * 512 + 512))
            at = m * 1024 + b * 512
            for h in range(2):
                swap[h, :, at : at + 512] = total[h * 24 : h * 24 + 24]
    swap_copy = remote(
        swap.at[1 - core], swapped, swap_sem.at[0], swap_sem.at[1], s + 1 - 2 * core, t
    )
    swap_copy.start()
    home_waits(dq_out, land, hrecv)
    for j in range(3):
        for u in range(2):
            dqkv_ref[0, u * 128 : (u + 1) * 128, j * 128 : (j + 1) * 128] = land[j, u]
    for j in range(3):
        total = jnp.zeros((BLOCK, 256), F32)
        for p in range(PER_HEAD):
            spot = j * PER_HEAD + p
            pltpu.make_async_copy(both.at[0], home.at[spot], krecv.at[spot]).wait()
            total = total + home[spot].astype(F32)
        dqkv_ref[1, :, j * 128 : (j + 1) * 128] = total[:, :128].astype(BF)
        dqkv_ref[2, :, j * 128 : (j + 1) * 128] = total[:, 128:].astype(BF)
    swap_copy.wait()
    swap_out(swap, swapped, ((gate_ref, 0), (up_ref, 1024), (down_ref, 2048)), 1024, core)
    ring_dres.finish()
    ring_dres.drain()
    send_gu.each(False)
    send_down.each(False)
    home_sends(dq_out, land, hsend, hrecv, chip, core, t, False)

    @pl.when(served)
    def _():
        def last(o, carry):
            to_sibling(o).wait_send()
            to_home(o, False)
            return carry

        lax.fori_loop(0, CHIPS // 2, last, 0)


def swap_out(swap, swapped, outs, width, core):
    mine = swap[core]
    for c in range(2):

        @pl.when(core == c)
        def _():
            for ref, at in outs:
                ref[:, c * width : (c + 1) * width] = mine[:, at : at + width]
                other = (1 - c) * width
                ref[:, other : other + width] = swapped[:, at : at + width]


def attend_back(lambdas, gain, q, kv, dmix, parts, logs, lffn, lgu, lhid, ldout, dres):
    half = (CHIPS // 2, BLOCK, 256)
    return pl.pallas_call(
        attend_back_kernel,
        name="attend_back",
        out_shape=(
            shape((3, BLOCK, 384), BF),
            shape((2, 128), F32),
            shape((24, 2048), F32),
            shape((24, 2048), F32),
            shape((24, 2048), F32),
            shape(GATHERED_Q, BF),
        ),
        in_specs=[VM] * 7 + [ANY] * 5,
        out_specs=(VM,) * 5 + (ANY,),
        scratch_shapes=[
            pltpu.VMEM((128, CHIPS * BLOCK), BF),
            pltpu.VMEM((SPAN, 256), F32),
            pltpu.VMEM((SLOTS, 128, 2 * TILE), BF),
            pltpu.VMEM((SLOTS, 2 * TILE, 128), BF),
            pltpu.VMEM((SLOTS, 128, TILE), BF),
            pltpu.VMEM((SLOTS, TILE, 128), BF),
            pltpu.VMEM((SLOTS, 2, TILE), F32),
            pltpu.VMEM((SLOTS, 128, 2 * TILE), F32),
            pltpu.VMEM((SLOTS, TILE, 128), BF),
            pltpu.VMEM(half, BF),
            pltpu.VMEM(half, BF),
            pltpu.VMEM(half, BF),
            pltpu.VMEM(half, BF),
            pltpu.VMEM((3 * PER_HEAD, BLOCK, 256), BF),
            pltpu.VMEM((3, 2, TILE, 128), BF),
            pltpu.VMEM(GATHERED, BF),
            pltpu.VMEM((4, BLOCK, 1024), BF),
            pltpu.VMEM((4, BLOCK, 512), BF),
            pltpu.VMEM(GATHERED, BF),
            pltpu.VMEM((768, 1024), BF),
            pltpu.VMEM((768, 512), BF),
            pltpu.VMEM((16, CHUNK, 1024), BF),
            pltpu.VMEM((16, CHUNK, 512), BF),
            pltpu.VMEM((2, 24, 3072), F32),
            pltpu.VMEM((24, 3072), F32),
            pltpu.SemaphoreType.DMA((4,)),
            *RING_SEMS,
            *scatter_sems(16),
            *scatter_sems(16),
            pltpu.SemaphoreType.DMA((2,)),
            pltpu.SemaphoreType.DMA((CHIPS // 2,)),
            pltpu.SemaphoreType.DMA((CHIPS // 2,)),
            pltpu.SemaphoreType.DMA((CHIPS // 2,)),
            pltpu.SemaphoreType.DMA((3 * PER_HEAD,)),
            pltpu.SemaphoreType.DMA((SLOTS,)),
            pltpu.SemaphoreType.DMA((3, 2)),
        ],
        compiler_params=pltpu.CompilerParams(
            collective_id=4, has_side_effects=True, vmem_limit_bytes=VMEM_LIMIT
        ),
    )(lambdas, gain, q, kv, dmix, parts, logs, lffn, lgu, lhid, ldout, dres)


def finish_kernel(
    x_ref, gain_ref, dres_ref, dqkv_ref, wq_ref, wk_ref, wv_ref,
    xnormed_ref, znormed_ref, xdres_ref, xmix_ref, ffnpart_ref, small_ref,
    grad_ref, gq_ref, gk_ref, gv_ref, go_ref, sums_ref,
    wbuf, xnormed, znormed, xdres, xmix, rq, rk, rv, pqo, pkv, sqo, skv, swap, swapped,
    vec, vecs, quarter, quarters, *rest,
):
    chip, core, t = place()
    s = 2 * chip + core
    x, z = chip % 4, chip // 8
    reduce = rest[:9]
    wsem, lsem = rest[9:11]
    rings = [
        RingGather(lambda p, k=k: dqkv_ref.at[k], land, *sems, axis, chip, core, t)
        for k, land, sems, axis in (
            (1, rk, rest[11:13], "z"), (0, rq, rest[13:15], "x"), (2, rv, rest[15:17], "z")
        )
    ]
    send_qo = Scatter(pqo, sqo, *rest[17:19], 8, 8 * x, chip // 4, chip, core, t)
    send_kv = Scatter(pkv, skv, *rest[19:21], 8, 8 * z, chip % 8, chip, core, t)
    swap_sem, asem, bsem, csem = rest[21:]
    loads = [
        weight_load(ref, wbuf.at[k], wsem.at[k], core, 384)
        for k, ref in enumerate((wq_ref, wk_ref, wv_ref))
    ]
    lefts = [
        pltpu.make_async_copy(src, dst, lsem.at[k])
        for k, (src, dst) in enumerate(
            ((xdres_ref, xdres), (xmix_ref, xmix), (xnormed_ref, xnormed), (znormed_ref, znormed))
        )
    ]
    for load in loads + lefts:
        load.start()
    greet_all(chip, core, t)
    for ring in rings:
        ring.start()
    for load in loads:
        load.wait()
    red = QuadReduce(*reduce, chip, core, t)

    def term(k):
        rows = slice(k * CW, (k + 1) * CW)
        return (
            matmul_t(dqkv_ref[0], wbuf[0, rows, :])
            + matmul_t(dqkv_ref[1], wbuf[1, rows, :])
            + matmul_t(dqkv_ref[2], wbuf[2, rows, :])
        )

    red.run(term)
    for left in lefts:
        left.wait()
    block_grad(pqo, 384, xdres, xmix[...].reshape(4 * BLOCK, 384), 384)
    x = x_ref[...]
    rms = rms_scale(x)
    hat = x * rms
    d_normed = jnp.concatenate([red.result(k) for k in range(NC)], axis=1)
    part = jnp.sum(d_normed * hat, axis=0, keepdims=True)
    vec[...] = jnp.zeros_like(vec)
    for k in range(12):
        vec[k : k + 1, :] = part[:, k * 128 : (k + 1) * 128]
        vec[12 + k : 13 + k, :] = ffnpart_ref[:, k * 128 : (k + 1) * 128]
    vec[24:26, :] = small_ref[...]
    members = ((s + 1 - 2 * core, t), (s, 1 - t), (s + 1 - 2 * core, 1 - t))
    first_sum = [
        remote(vec, vecs.at[k], asem.at[0, k], asem.at[1, k], *member)
        for k, member in enumerate(members)
    ]
    for cp in first_sum:
        cp.start()
    grad_ref[...] = dres_ref[...] + norm_back(d_normed, gain_ref[...], rms, hat)
    for cp in first_sum:
        cp.wait_recv()
    share = pl.ds(pl.multiple_of((2 * core + t) * 8, 8), 8)
    quarter[...] = (vec[share, :] + vecs[0, share, :]) + (vecs[1, share, :] + vecs[2, share, :])

    def spread(k, start):
        to = 2 * lax.rem(chip + k, CHIPS) + core
        cp = remote(quarter, quarters.at[chip], bsem.at[0, k], bsem.at[1, chip], to, t)
        if start:
            cp.start()
        else:
            cp.wait_send()

    def spread_start(k, carry):
        spread(k, True)
        return carry

    def spread_end(k, carry):
        spread(k, False)
        return carry

    own = pltpu.make_async_copy(quarter, quarters.at[chip], bsem.at[1, chip])
    own.start()
    lax.fori_loop(1, CHIPS, spread_start, 0)
    rings[1].finish()
    block_grad(pqo, 0, xnormed, rq[...].reshape(4 * BLOCK, 384), 384)
    send_qo.each(True)
    rings[0].finish()
    block_grad(pkv, 0, znormed, rk[...].reshape(4 * BLOCK, 384), 384)
    rings[2].finish()
    block_grad(pkv, 384, znormed, rv[...].reshape(4 * BLOCK, 384), 384)
    send_kv.each(True)

    def collect(k, total):
        pltpu.make_async_copy(quarter, quarters.at[k], bsem.at[1, k]).wait()
        return total + quarters[k]

    sums_ref[share, :] = lax.fori_loop(0, CHIPS, collect, jnp.zeros((8, 128), F32))
    last_sum = [
        remote(sums_ref.at[share], sums_ref.at[share], csem.at[0, k], csem.at[1, k], *member)
        for k, member in enumerate(members)
    ]
    for cp in last_sum:
        cp.start()
    for send, first in ((send_qo, (0, 3)), (send_kv, (1, 2))):
        send.wait()
        for m in range(2):
            total = send.total(0, slice(m * 384, m * 384 + 384))
            at = first[m] * 384
            for h in range(2):
                swap[h, :, at : at + 384] = total[h * 24 : h * 24 + 24]
    swap_copy = remote(
        swap.at[1 - core], swapped, swap_sem.at[0], swap_sem.at[1], s + 1 - 2 * core, t
    )
    swap_copy.start()
    for cp in last_sum:
        cp.wait()
    for cp in first_sum:
        cp.wait_send()
    lax.fori_loop(1, CHIPS, spread_end, 0)
    send_qo.each(False)
    send_kv.each(False)
    for ring in rings:
        ring.drain()
    red.drain()
    swap_copy.wait()
    outs = ((gq_ref, 0), (gk_ref, 384), (gv_ref, 768), (go_ref, 1152))
    swap_out(swap, swapped, outs, 384, core)


def finish(x, gain, dres, dqkv, wq, wk, wv, xnormed, znormed, xdres, xmix, ffn_part, small):
    return pl.pallas_call(
        finish_kernel,
        name="finish",
        out_shape=(shape((ROWS, D), F32),) + (shape((24, 768), F32),) * 4 + (shape((32, 128), F32),),
        in_specs=[VM] * 4 + [ANY] * 7 + [VM] * 2,
        out_specs=(VM,) * 6,
        scratch_shapes=[
            pltpu.VMEM((3, D, 384), BF),
            *([pltpu.VMEM(GATHERED_Q, BF)] * 7),
            pltpu.VMEM((384, 768), BF),
            pltpu.VMEM((384, 768), BF),
            pltpu.VMEM((8, CHUNK, 768), BF),
            pltpu.VMEM((8, CHUNK, 768), BF),
            pltpu.VMEM((2, 24, 1536), F32),
            pltpu.VMEM((24, 1536), F32),
            pltpu.VMEM((32, 128), F32),
            pltpu.VMEM((3, 32, 128), F32),
            pltpu.VMEM((8, 128), F32),
            pltpu.VMEM((CHIPS, 8, 128), F32),
            *REDUCE_SCRATCH,
            pltpu.SemaphoreType.DMA((3,)),
            pltpu.SemaphoreType.DMA((4,)),
            *(RING_SEMS * 3),
            *scatter_sems(8),
            *scatter_sems(8),
            pltpu.SemaphoreType.DMA((2,)),
            pltpu.SemaphoreType.DMA((2, 3)),
            pltpu.SemaphoreType.DMA((2, CHIPS)),
            pltpu.SemaphoreType.DMA((2, 3)),
        ],
        compiler_params=pltpu.CompilerParams(
            collective_id=2, has_side_effects=True, vmem_limit_bytes=VMEM_LIMIT
        ),
    )(x, gain, dres, dqkv, wq, wk, wv, xnormed, znormed, xdres, xmix, ffn_part, small)


def publish(*arrays):
    count = len(arrays)

    def kernel(*refs):
        copies = [
            pltpu.make_async_copy(refs[k], refs[count + k], refs[2 * count].at[k])
            for k in range(count)
        ]
        for cp in copies:
            cp.start()
        for cp in copies:
            cp.wait()

    return pl.pallas_call(
        kernel,
        name="publish",
        out_shape=tuple(shape(a.shape, a.dtype) for a in arrays),
        in_specs=[ANY] * count,
        out_specs=(ANY,) * count,
        scratch_shapes=[pltpu.SemaphoreType.DMA((count,))],
    )(*arrays)


def on_device(
    hidden_in, cotangent, needle_mask, attn_gain, lambdas, subln_gain, ffn_gain,
    weight_query, weight_key, weight_value, weight_out, weight_gate, weight_up, weight_down,
):
    attn_row = attn_gain.reshape(1, D)
    ffn_row = ffn_gain.reshape(1, D)
    sub_col = subln_gain.reshape(128, 1)
    mask = needle_mask.astype(F32).reshape(ROWS, 1)

    normed, dout, q, kv = project(
        hidden_in, cotangent, mask, attn_row, weight_query, weight_key, weight_value
    )
    kv = kv.reshape(CHIPS * BLOCK, 256)
    mixed, parts, logs, xnormed, znormed = attend(lambdas, sub_col, q, kv, normed)
    output, d_resid, ffn_part, dres, dmix, lffn, lgu, lhid, ldout, xmix = middle(
        hidden_in, cotangent, mask, ffn_row, mixed,
        weight_out, weight_gate, weight_up, weight_down, dout,
    )
    dqkv, small, grad_gate, grad_up, grad_down, xdres = attend_back(
        lambdas, sub_col, q, kv, dmix, parts, logs, lffn, lgu, lhid, ldout, dres
    )
    grad_input, grad_query, grad_key, grad_value, grad_out, sums = finish(
        hidden_in, attn_row, d_resid, dqkv, weight_query, weight_key, weight_value,
        xnormed, znormed, xdres, xmix, ffn_part, small,
    )
    first_exp = jnp.exp(jnp.sum(lambdas[0] * lambdas[1], axis=-1))
    second_exp = jnp.exp(jnp.sum(lambdas[2] * lambdas[3], axis=-1))
    d_first = sums[25, :12] * first_exp
    d_second = -sums[25, :12] * second_exp
    grad_lambdas = jnp.stack(
        [
            d_first[:, None] * lambdas[1],
            d_first[:, None] * lambdas[0],
            d_second[:, None] * lambdas[3],
            d_second[:, None] * lambdas[2],
        ]
    )
    results = publish(
        output, grad_input, grad_query, grad_key, grad_value, grad_out, grad_gate, grad_up, grad_down
    )
    return (
        *results,
        sums[:12].reshape(D),
        grad_lambdas,
        sums[24],
        sums[12:24].reshape(D),
    )


def solution(mesh):
    split = P(None, "tp")
    rows = P(("seq", "tp"), None)
    both = P("seq", "tp")
    return jax.shard_map(
        on_device,
        mesh=mesh,
        in_specs=(rows, rows, P(("seq", "tp"))) + (P(),) * 4 + (split,) * 7,
        out_specs=(rows, rows) + (both,) * 7 + (P(),) * 4,
        check_vma=False,
    )
```

time: 1790 us -> 347 us (0.19)
  waiting for transfers between devices: 1390 us -> 0 us
  Pallas kernels: 258 us -> 335 us
  blocking collectives: 67 us -> 0 us
  starting transfers between devices: 20.7 us -> 0 us
    reduce_scatter x7 -> x0, waiting for transfers between devices: 1390 us -> none  [weight_grad(): lax.psum_scatter(part, 'seq', scatter_dimension=0, axis_index_groups=grou...]
    psum x1 -> x0, blocking collectives: 67 us -> none  [on_device(): lax.psum(jnp.concatenate([attn_part[0], ffn_part[0], sub_part[:, 0], dlam...]
    pallas_call x1 -> x2, Pallas kernels: 57.9 us -> 107 us  [the longest x1 55.3 us: project(): pl.pallas_call(project_kernel, name='project', out_shape=(shape(QUARTERS,...]
    pallas_call x1, Pallas kernels: 51.1 us -> 79.3 us  [attend_back(): pl.pallas_call(attend_back_kernel, name='attend_back', out_shape=(shape((...]
    ppermute x7 -> x0, starting transfers between devices: 20.4 us -> none  [weight_grad(): got = lax.ppermute(away, 'seq', [(i, i ^ 1) for i in range(2 * CHIPS)])]
  transfers between devices with their start and end apart: 14 -> 0, of which waited for: 7 -> 0; matrix products, arithmetic and copies ran while one was open for 1% -> 0% of each run, Pallas kernels for 6% -> 0%
where the time goes in v2:
time: 347 us; the launch traced here: 344 us
  Pallas kernels  335 us (97%)
  local copies, waits for them, and re-layouts  6.55 us (2%)
    pallas_call x1, Pallas kernels, attend_back(): pl.pallas_call(attend_back_kernel, name='attend_back', out_shape=(shape((...  79.3 us
    pallas_call x1, Pallas kernels, middle(): pl.pallas_call(middle_kernel, name='middle', out_shape=(shape((ROWS, D),...  77.1 us
    pallas_call x1, Pallas kernels, project(): pl.pallas_call(project_kernel, name='project', out_shape=(shape(QUARTERS,...  55.3 us
    pallas_call x1, Pallas kernels, publish(): pl.pallas_call(kernel, name='publish', out_shape=tuple((shape(a.shape, a....  51.8 us
    pallas_call x1, Pallas kernels, finish(): pl.pallas_call(finish_kernel, name='finish', out_shape=(shape((ROWS, D),...  48.5 us
    pallas_call x1, Pallas kernels, attend(): pl.pallas_call(attend_kernel, name='attend', out_shape=(shape((SLOTS, TIL...  22.8 us

profile of v2, /device:TPU:31, one launch (start us, length us, event | category | flops | bytes accessed | tf_op | source)
XLA Modules:
  0.0 344.3 jit_solution(13638224618520430217)
XLA Ops:
  0.6 0.7 convert_bitcast_fusion
  1.3 0.7 copy.30.mask_ref
  2.0 1.3 reshape.97.gain_ref
  3.3 0.0 copy-start.2
  3.3 0.0 copy-start
  3.3 55.3 %project.1 = (bf16[4,256,384]{2,1,0:T(8,128)(2,1)}, bf16[2,256,768]{2,1,0:T(8,128)(2,1)}, bf16[7,128,128]{2,1,0:T(8,128)(2,1)}, bf16[32,256,256]{2,1,0:T(8,128)(2,1)}) custom-call(f32[64,1536]{1,0:T(8,128)} %x_ref.5, f32[64,1536]{1,0:T(8,128)} %cot_ref.3, f32[64,1]{1,0:T(8,128)} %copy.30.mask_ref, f32[1,1536]{1,0:T(1,128)} %reshape.97.gain_ref, ...), custom_call_target="tpu_custom_call" | custom-call | tf_op jit(solution)/shard_map/project/pallas_call | solution.py:506
  58.7 0.0 copy-done.2
  58.7 0.7 copy.29.gain_ref
  59.4 0.0 copy-done
  59.4 0.6 copy.28.lambdas_ref
  60.0 0.0 copy-start.1
  60.0 22.8 %attend.1 = (bf16[7,128,128]{2,1,0:T(8,128)(2,1)}, f32[7,128,256]{2,1,0:T(8,128)}, f32[7,1,256]{2,1,0:T(1,128)}, bf16[4,256,384]{2,1,0:T(8,128)(2,1)}, bf16[4,256,384]{2,1,0:T(8,128)(2,1)}) custom-call(f32[4,12,64]{2,1,0:T(8,128)} %copy.28.lambdas_ref, f32[128,1]{1,0:T(8,128)} %copy.29.gain_ref, bf16[7,128,128]{2,1,0:T(8,128)(2,1)} %get-tuple-element.53.q_ref, ...), custom_call_target="tpu_custom_call" | custom-call | tf_op jit(solution)/shard_map/attend/pallas_call | solution.py:671
  82.8 0.0 copy-done.1
  82.9 0.6 reshape.95.gain_ref
  83.5 77.1 %middle.1 = (f32[64,1536]{1,0:T(8,128)}, f32[64,1536]{1,0:T(8,128)}, f32[1,1536]{1,0:T(1,128)}, bf16[4,256,384]{2,1,0:T(8,128)(2,1)}, bf16[7,128,128]{2,1,0:T(8,...) custom-call(f32[64,1536]{1,0:T(8,128)} %x_ref.5, ...), custom_call_target="tpu_custom_call" | custom-call | tf_op jit(solution)/shard_map/middle/pallas_call | solution.py:817
  160.6 79.3 %attend_back.1 = (bf16[3,256,384]{2,1,0:T(8,128)(2,1)}, f32[2,128]{1,0:T(2,128)}, f32[24,2048]{1,0:T(8,128)}, f32[24,2048]{1,0:T(8,128)}, f32[24,2048]{1,0:T(8,128)}, /*index=5*/bf16[4,256,384]{2,1,0:T(8,128)(2,1)}) custom-call(f32[4,12,64]{2,1,0:T(8,128)} %copy.28.lambdas_ref, f32[128,1]{1,0:T(8,128)} %copy.29.gain_ref, ...), custom_call_target="tpu_custom_call" | custom-call | tf_op jit(solution)/shard_map/attend_back/pallas_call | solution.py:1109
  239.8 48.5 %finish.1 = (f32[64,1536]{1,0:T(8,128)}, f32[24,768]{1,0:T(8,128)}, f32[24,768]{1,0:T(8,128)}, f32[24,768]{1,0:T(8,128)}, f32[24,768]{1,0:T(8,128)}, /*index=5*/f32[32,128]{1,0:T(8,128)}) custom-call(f32[64,1536]{1,0:T(8,128)} %x_ref.5, f32[1,1536]{1,0:T(1,128)} %reshape.97.gain_ref, f32[64,1536]{1,0:T(8,128)} %get-tuple-element.59.dres_ref, ...), custom_call_target="tpu_custom_call" | custom-call | tf_op jit(solution)/shard_map/finish/pallas_call | solution.py:1307
  288.3 0.2 multiply_reduce_fusion.1
  288.5 0.7 bitcast_multiply_fusion
  289.1 0.1 slice_multiply_fusion.2
  289.2 0.6 pad_maximum_fusion
  289.9 51.8 %publish.1 = (f32[64,1536]{1,0:T(8,128)}, f32[64,1536]{1,0:T(8,128)}, f32[24,768]{1,0:T(8,128)}, f32[24,768]{1,0:T(8,128)}, f32[24,768]{1,0:T(8,128)}, /*index=5...) custom-call(f32[64,1536]{1,0:T(8,128)} %get-tuple-element.58.refs_0_, ...), custom_call_target="tpu_custom_call" | custom-call | tf_op jit(solution)/shard_map/publish/pallas_call | solution.py:1356
  341.7 1.4 slice_bitcast_fusion
  343.1 1.2 slice_bitcast_fusion.2
Async XLA Ops:
  3.3 55.3 %copy-start.2 = (f32[128]{0:T(128)S(1)}, f32[128]{0:T(128)}, u32[]{:S(2)}) copy-start(f32[128]{0:T(128)} %param.19) | copy-start | bytes 1540
  3.3 56.1 %copy-start = (f32[4,12,64]{2,0,1:T(4,128)S(1)}, f32[4,12,64]{2,0,1:T(4,128)}, u32[]{:S(2)}) copy-start(f32[4,12,64]{2,0,1:T(4,128)} %param.18) | copy-start | bytes 36868
  60.0 22.8 %copy-start.1 = (f32[1536]{0:T(1024)S(1)}, f32[1536]{0:T(1024)}, u32[]{:S(2)}) copy-start(f32[1536]{0:T(1024)} %param.20) | copy-start | bytes 18436

commit v3 on v2

--- a/solution.py
+++ b/solution.py
@@ -156,18 +156,59 @@
             cp.wait_send()
 
 
+class RingGatherOnce:
+    def __init__(self, pieces, land, send, recv, pass_send, pass_recv, axis, chip, core, t):
+        at = chip % 4 if axis == "x" else chip // 8
+        self.mine = pl.ds(pl.multiple_of(core * 128, 128), 128)
+        self.local = pltpu.make_async_copy(pieces(at), land.at[at], recv.at[0])
+        self.local_at = at
+        self.copies, self.passes = [], []
+        for k in (1, 3, 2):
+            peer = (at + k) % 4
+            chip_to = chip - at + peer if axis == "x" else (chip + 8 * k) % CHIPS
+            self.copies.append(
+                remote(
+                    pieces(peer).at[self.mine], land.at[at, self.mine],
+                    send.at[k - 1], recv.at[4 - k], 2 * chip_to + core, t,
+                )
+            )
+            view = land.at[peer, self.mine]
+            self.passes.append(
+                (
+                    pltpu.make_async_copy(pieces(at).at[self.mine], view, recv.at[k]),
+                    remote(view, view, pass_send.at[k - 1], pass_recv.at[k - 1], 2 * chip + 1 - core, t),
+                )
+            )
+
+    def start(self):
+        self.local.start()
+        for cp in self.copies:
+            cp.start()
+
+    def forward(self):
+        for arrive, cp in self.passes:
+            arrive.wait()
+            cp.start()
+
+    def finish(self):
+        self.local.wait()
+        for _, cp in self.passes:
+            cp.wait_recv()
+
+    def drain(self):
+        for cp in self.copies:
+            cp.wait_send()
+        for _, cp in self.passes:
+            cp.wait_send()
+
+
+ONCE_SEMS = [
+    pltpu.SemaphoreType.DMA((3,)),
+    pltpu.SemaphoreType.DMA((4,)),
+    pltpu.SemaphoreType.DMA((3,)),
+    pltpu.SemaphoreType.DMA((3,)),
+]
 RING_SEMS = [pltpu.SemaphoreType.DMA((3,)), pltpu.SemaphoreType.DMA((4,))]
-
-
-def greet_ring(chip, core, t):
-    barrier = pltpu.get_barrier_semaphore()
-    x = chip % 4
-    for k in (1, 2, 3):
-        for peer in ((chip + 8 * k) % CHIPS, chip - x + (x + k) % 4):
-            pl.semaphore_signal(
-                barrier, inc=1, device_id=(2 * peer + core, t), device_id_type=MESH
-            )
-    pl.semaphore_wait(barrier, 6)
 
 
 def block_grad(dst, start, left, right, step):
@@ -379,14 +420,77 @@
     )
 
 
-def project_kernel(
-    x_ref, cot_ref, mask_ref, gain_ref, wq_ref, wk_ref, wv_ref,
-    normed_ref, dout_ref, q_ref, kv_ref,
-    nbuf, obuf, wbuf, kvsrc, qsrc, wsem, nsend, nrecv, osend, orecv, kvsend, kvrecv, fsend, qsend,
-    qrecv, osem,
+def pieces_out(buf, ref, sem, first, count):
+    width = D // count
+    copies = [
+        pltpu.make_async_copy(
+            buf.at[:, a * width : (a + 1) * width], ref.at[a], sem.at[first + a]
+        )
+        for a in range(count)
+    ]
+    for cp in copies:
+        cp.start()
+    return copies
+
+
+VM = pl.BlockSpec(memory_space=pltpu.VMEM)
+ANY = pl.BlockSpec(memory_space=pl.ANY)
+
+
+def shape(dims, dtype):
+    return jax.ShapeDtypeStruct(dims, dtype)
+
+
+HALVES = (2, BLOCK, 768)
+QUARTERS = (4, BLOCK, 384)
+GATHERED = (4, BLOCK, 768)
+GATHERED_Q = (4, BLOCK, 384)
+KV = (CHIPS, BLOCK, 256)
+STEP = 2048
+
+
+def eye(size):
+    row = lax.broadcasted_iota(jnp.int32, (size, size), 0)
+    col = lax.broadcasted_iota(jnp.int32, (size, size), 1)
+    return jnp.where(row == col, 1.0, 0.0).astype(BF)
+
+
+def both_maps(q_t):
+    top = lax.broadcasted_iota(jnp.int32, q_t.shape, 0) < 64
+    return jnp.concatenate([jnp.where(top, q_t, 0.0), jnp.where(top, 0.0, q_t)], axis=1)
+
+
+def key_mask(start, count, tile, width):
+    key = start + lax.broadcasted_iota(jnp.int32, (count, width), 0)
+    query = tile * TILE + lax.broadcasted_iota(jnp.int32, (count, width), 1) % TILE
+    return key <= query
+
+
+def group_norm(parts, lam):
+    first, second = parts[:, :TILE], parts[:, TILE:]
+    differ = first - lam * second
+    rms = rms_scale(differ, 0)
+    return rms, differ * rms
+
+
+def lambda_of(lambdas_ref, chip, t):
+    first = jnp.exp(jnp.sum(lambdas_ref[0] * lambdas_ref[1], axis=-1, keepdims=True))
+    second = jnp.exp(jnp.sum(lambdas_ref[2] * lambdas_ref[3], axis=-1, keepdims=True))
+    every = first - second + LAMBDA_INIT
+    mine = lax.broadcasted_iota(jnp.int32, every.shape, 0) == 6 * t + chip // PER_HEAD
+    return jnp.sum(jnp.where(mine, every, 0.0), axis=0, keepdims=True)
+
+
+def forward_kernel(
+    x_ref, cot_ref, mask_ref, gain_ref, lambdas_ref, sub_ref, wq_ref, wk_ref, wv_ref,
+    dout_ref, q_ref, kv_ref, mixed_ref, parts_ref, log_ref, xnormed_ref, znormed_ref,
+    nbuf, obuf, wbuf, kvsrc, qsrc, kv, q, v_t, peaks, kmax, acc, total,
+    wsem, nsend, nrecv, osend, orecv, kvsend, kvrecv, fsend, qsend, qrecv, osem, *sems,
 ):
     chip, core, t = place()
     s = 2 * chip + core
+    slot = s % 10
+    served = chip < SERVED
     loads = [
         weight_load(ref, wbuf.at[k], wsem.at[k], core, 384)
         for k, ref in enumerate((wk_ref, wv_ref, wq_ref))
@@ -402,8 +506,9 @@
     greet_all(chip, core, t)
     quad.start()
     obuf[mine, :] = (cot_ref[...] * mask_ref[...]).astype(BF)
+    lam = lambda_of(lambdas_ref, chip, t)
+    unit = eye(256)
     quad.finish()
-    saves = pieces_out(nbuf, normed_ref, osem, 0, 4)
     for k in range(2):
         loads[k].wait()
         value = matmul(nbuf[...], wbuf[k]).astype(BF)
@@ -419,11 +524,11 @@
 
                 @pl.when(target == s)
                 def _():
-                    pltpu.make_async_copy(kvsrc.at[j], kv_ref.at[chip], kvrecv.at[chip]).start()
+                    pltpu.make_async_copy(kvsrc.at[j], kv.at[chip], kvrecv.at[chip]).start()
 
             @pl.when(target != s)
             def _():
-                cp = remote(kvsrc.at[j], kv_ref.at[chip], kvsend.at[w], kvrecv.at[chip], target, t)
+                cp = remote(kvsrc.at[j], kv.at[chip], kvsend.at[w], kvrecv.at[chip], target, t)
                 if start:
                     cp.start()
                 else:
@@ -439,183 +544,87 @@
     for j in range(3):
         for u in range(2):
             qsrc[j, u] = value[u * 128 : (u + 1) * 128, j * 128 : (j + 1) * 128]
-    tile_sends(qsrc, q_ref, qsend, qrecv, chip, core, t, True)
+    tile_sends(qsrc, q, qsend, qrecv, chip, core, t, True)
     quad_o.start()
 
-    @pl.when(chip < SERVED)
+    def forward(o):
+        source = lax.rem((chip // 2 + o) * 2 + core, CHIPS)
+        view = kv.at[source]
+        return source, remote(view, view, fsend.at[o], kvrecv.at[source], s + 1 - 2 * core, t)
+
+    def turn(source):
+        block = kv[source]
+        at = pl.ds(pl.multiple_of(source * BLOCK, BLOCK), BLOCK)
+        turned = matmul_t(unit, block)
+        v_t[:, at] = turned[128:].astype(BF)
+        square = turned[:128] * turned[:128]
+        for m in range(2):
+            largest = jnp.sum(square[64 * m : 64 * m + 64], axis=0, keepdims=True)
+            peaks[m : m + 1, :] = jnp.maximum(peaks[m : m + 1, :], largest)
+
+    def gathers():
+        def piece(p):
+            return nbuf.at[:, pl.ds(pl.multiple_of(p * 384, 128), 384)]
+
+        return [
+            RingGather(piece, xnormed_ref, *sems[:2], "x", chip, core, t),
+            RingGather(piece, znormed_ref, *sems[2:], "z", chip, core, t),
+        ]
+
+    @pl.when(served)
     def _():
-        def forward(o):
-            source = lax.rem((chip // 2 + o) * 2 + core, CHIPS)
-            view = kv_ref.at[source]
-            return source, remote(view, view, fsend.at[o], kvrecv.at[source], s + 1 - 2 * core, t)
+        peaks[...] = jnp.zeros_like(peaks)
 
         def take(o, carry):
             source, cp = forward(o)
-            pltpu.make_async_copy(kvsrc.at[0], kv_ref.at[source], kvrecv.at[source]).wait()
+            pltpu.make_async_copy(kvsrc.at[0], kv.at[source], kvrecv.at[source]).wait()
             cp.start()
+            turn(source)
             return carry
 
         lax.fori_loop(0, CHIPS // 2, take, 0)
 
         def finish(o, carry):
-            source = 2 * o + 1 - core
-            pltpu.make_async_copy(kvsrc.at[0], kv_ref.at[source], kvrecv.at[source]).wait()
+            source = lax.rem((chip // 2 + o) * 2 + 1 - core, CHIPS)
+            pltpu.make_async_copy(kvsrc.at[0], kv.at[source], kvrecv.at[source]).wait()
             forward(o)[1].wait_send()
+            turn(source)
             return carry
 
         lax.fori_loop(0, CHIPS // 2, finish, 0)
+        for m in range(2):
+            kmax[m] = jnp.max(peaks[m : m + 1, :])
 
     quad_o.finish()
-    saves += pieces_out(obuf, dout_ref, osem, 4, 2)
-    tile_waits(qsrc, q_ref, qsend, qrecv, chip, core, t)
-    kv_sends(False)
-    tile_sends(qsrc, q_ref, qsend, qrecv, chip, core, t, False)
-    quad.drain()
-    quad_o.drain()
-    for save in saves:
-        save.wait()
-
-
-def pieces_out(buf, ref, sem, first, count):
-    width = D // count
-    copies = [
-        pltpu.make_async_copy(
-            buf.at[:, a * width : (a + 1) * width], ref.at[a], sem.at[first + a]
-        )
-        for a in range(count)
-    ]
-    for cp in copies:
-        cp.start()
-    return copies
-
-
-VM = pl.BlockSpec(memory_space=pltpu.VMEM)
-SM = pl.BlockSpec(memory_space=pltpu.SMEM)
-ANY = pl.BlockSpec(memory_space=pl.ANY)
-
-
-def shape(dims, dtype):
-    return jax.ShapeDtypeStruct(dims, dtype)
-
-
-HALVES = (2, BLOCK, 768)
-QUARTERS = (4, BLOCK, 384)
-
-
-def project(x, cot, mask, gain, wq, wk, wv):
-    return pl.pallas_call(
-        project_kernel,
-        name="project",
-        out_shape=(
-            shape(QUARTERS, BF),
-            shape(HALVES, BF),
-            shape((SLOTS, TILE, 128), BF),
-            shape((CHIPS, BLOCK, 256), BF),
-        ),
-        in_specs=[VM, VM, VM, VM, ANY, ANY, ANY],
-        out_specs=(ANY,) * 4,
-        scratch_shapes=[
-            pltpu.VMEM((BLOCK, D), BF),
-            pltpu.VMEM((BLOCK, D), BF),
-            pltpu.VMEM((3, D, 384), BF),
-            pltpu.VMEM((3, BLOCK, 256), BF),
-            pltpu.VMEM((3, 2, TILE, 128), BF),
-            pltpu.SemaphoreType.DMA((3,)),
-            *(GATHER_SEMS * 2),
-            pltpu.SemaphoreType.DMA((15,)),
-            pltpu.SemaphoreType.DMA((CHIPS,)),
-            pltpu.SemaphoreType.DMA((CHIPS // 2,)),
-            pltpu.SemaphoreType.DMA((6,)),
-            pltpu.SemaphoreType.DMA((SLOTS,)),
-            pltpu.SemaphoreType.DMA((6,)),
-        ],
-        compiler_params=pltpu.CompilerParams(
-            collective_id=0, has_side_effects=True, vmem_limit_bytes=VMEM_LIMIT
-        ),
-    )(x, cot, mask, gain, wq, wk, wv)
-
-
-def eye():
-    row = lax.broadcasted_iota(jnp.int32, (128, 128), 0)
-    col = lax.broadcasted_iota(jnp.int32, (128, 128), 1)
-    return jnp.where(row == col, 1.0, 0.0).astype(BF)
-
-
-def both_maps(q_t):
-    top = lax.broadcasted_iota(jnp.int32, q_t.shape, 0) < 64
-    return jnp.concatenate([jnp.where(top, q_t, 0.0), jnp.where(top, 0.0, q_t)], axis=1)
-
-
-def key_mask(start, count, tile, width):
-    key = start + lax.broadcasted_iota(jnp.int32, (count, width), 0)
-    query = tile * TILE + lax.broadcasted_iota(jnp.int32, (count, width), 1) % TILE
-    return key <= query
-
-
-def group_norm(parts, lam):
-    first, second = parts[:, :TILE], parts[:, TILE:]
-    differ = first - lam * second
-    rms = rms_scale(differ, 0)
-    return rms, differ * rms
-
-
-def lambda_of(lambdas_ref, chip, t):
-    first = jnp.exp(jnp.sum(lambdas_ref[0] * lambdas_ref[1], axis=-1, keepdims=True))
-    second = jnp.exp(jnp.sum(lambdas_ref[2] * lambdas_ref[3], axis=-1, keepdims=True))
-    every = first - second + LAMBDA_INIT
-    mine = lax.broadcasted_iota(jnp.int32, every.shape, 0) == 6 * t + chip // PER_HEAD
-    return jnp.sum(jnp.where(mine, every, 0.0), axis=0, keepdims=True)
-
-
-STEP = 2048
-
-
-def attend_kernel(
-    lambdas_ref, gain_ref, q_ref, kv_ref, normed_ref,
-    mixed_ref, parts_ref, log_ref, xnormed_ref, znormed_ref,
-    v_t, kmax, acc, total, *sems,
-):
-    chip, core, t = place()
-    slot = (2 * chip + core) % 10
-    served = chip < SERVED
-    keys = CHIPS * BLOCK
-    greet_ring(chip, core, t)
-    gathers = [
-        RingGather(lambda p: normed_ref.at[p], xnormed_ref, *sems[:2], "x", chip, core, t),
-        RingGather(lambda p: normed_ref.at[p], znormed_ref, *sems[2:], "z", chip, core, t),
-    ]
-    for gather in gathers:
-        gather.start()
-    lam = lambda_of(lambdas_ref, chip, t)
+    saves = pieces_out(obuf, dout_ref, osem, 0, 2)
+    tile_waits(qsrc, q, qsend, qrecv, chip, core, t)
+    for ring in gathers():
+        ring.start()
+
+    def keep():
+        return [
+            pltpu.make_async_copy(kv, kv_ref, osem.at[2]),
+            pltpu.make_async_copy(q.at[pl.ds(1, SLOTS - 1)], q_ref.at[pl.ds(1, SLOTS - 1)], osem.at[3]),
+        ]
+
+    def keep_early():
+        return pltpu.make_async_copy(q.at[0], q_ref.at[0], osem.at[4])
 
     @pl.when(served)
     def _():
-        unit = eye()
-
-        def flip(b, best):
-            for u in range(2):
-                start = pl.multiple_of(b * 2 * KB + u * KB, KB)
-                block = kv_ref[pl.ds(start, KB), :]
-                v_t[:, pl.ds(start, KB)] = matmul_t(unit, block[:, 128:]).astype(BF)
-                k_t = matmul_t(unit, block[:, :128])
-                square = k_t * k_t
-                best = (
-                    jnp.maximum(best[0], jnp.sum(square[:64], axis=0, keepdims=True)),
-                    jnp.maximum(best[1], jnp.sum(square[64:], axis=0, keepdims=True)),
-                )
-            return best
-
-        zero = jnp.zeros((1, KB), F32)
-        best = lax.fori_loop(0, keys // (2 * KB), flip, (zero, zero))
-        for m in range(2):
-            kmax[m] = jnp.max(best[m])
+        for cp in keep():
+            cp.start()
+
+    @pl.when(jnp.logical_and(served, slot < 4))
+    def _():
+        keep_early().start()
 
     for r in range(SLOTS):
         tile = tile_of(slot, r)
 
         @pl.when(served if r else jnp.logical_and(served, slot < 4))
         def _():
-            q_t = q_ref[r].astype(F32).T
+            q_t = q[r].astype(F32).T
             square = q_t * q_t
             bound = SCORE * jnp.concatenate(
                 [
@@ -632,7 +641,8 @@
                 sums, out = None, None
                 for u in range(STEP // KB):
                     start = pl.multiple_of(b * STEP + u * KB, KB)
-                    score = matmul(kv_ref[pl.ds(start, KB), :128], q_both)
+                    pair = pl.ds(b * (STEP // BLOCK) + u * (KB // BLOCK), KB // BLOCK)
+                    score = matmul(kv[pair, :, :128].reshape(KB, 128), q_both)
                     prob = jnp.exp2(score * SCORE - bound)
                     if masked:
                         prob = jnp.where(key_mask(start, KB, tile, 2 * TILE), prob, 0.0)
@@ -656,131 +666,204 @@
             parts_ref[r] = parts
             log_ref[r] = bound + jnp.log(whole) * LOG2E
             rms, hat = group_norm(parts, lam)
-            mixed_ref[r] = (hat * gain_ref[...] * OUT_SCALE).T.astype(BF)
-
-    for gather in gathers:
-        gather.finish()
-        gather.drain()
-
-
-GATHERED = (4, BLOCK, 768)
-GATHERED_Q = (4, BLOCK, 384)
-
-
-def attend(lambdas, gain, q, kv, normed):
+            mixed_ref[r] = (hat * sub_ref[...] * OUT_SCALE).T.astype(BF)
+
+    for ring in gathers():
+        ring.finish()
+        ring.drain()
+    kv_sends(False)
+    tile_sends(qsrc, q, qsend, qrecv, chip, core, t, False)
+    quad.drain()
+    quad_o.drain()
+    for save in saves:
+        save.wait()
+
+    @pl.when(served)
+    def _():
+        for cp in keep():
+            cp.wait()
+
+    @pl.when(jnp.logical_and(served, slot < 4))
+    def _():
+        keep_early().wait()
+
+
+def forward_part(x, cot, mask, gain, lambdas, sub, wq, wk, wv):
     return pl.pallas_call(
-        attend_kernel,
-        name="attend",
+        forward_kernel,
+        name="forward",
         out_shape=(
+            shape(HALVES, BF),
+            shape((SLOTS, TILE, 128), BF),
+            shape(KV, BF),
             shape((SLOTS, TILE, 128), BF),
             shape((SLOTS, 128, 2 * TILE), F32),
             shape((SLOTS, 1, 2 * TILE), F32),
             shape(GATHERED_Q, BF),
             shape(GATHERED_Q, BF),
         ),
-        in_specs=[VM, VM, VM, VM, ANY],
-        out_specs=(VM, VM, VM, ANY, ANY),
+        in_specs=[VM] * 6 + [ANY] * 3,
+        out_specs=(ANY, ANY, ANY, VM, VM, VM, ANY, ANY),
         scratch_shapes=[
+            pltpu.VMEM((BLOCK, D), BF),
+            pltpu.VMEM((BLOCK, D), BF),
+            pltpu.VMEM((3, D, 384), BF),
+            pltpu.VMEM((3, BLOCK, 256), BF),
+            pltpu.VMEM((3, 2, TILE, 128), BF),
+            pltpu.VMEM(KV, BF),
+            pltpu.VMEM((SLOTS, TILE, 128), BF),
             pltpu.VMEM((128, CHIPS * BLOCK), BF),
+            pltpu.VMEM((8, BLOCK), F32),
             pltpu.SMEM((2,), F32),
             pltpu.VMEM((128, 2 * TILE), F32),
             pltpu.VMEM((8, 2 * TILE), F32),
+            pltpu.SemaphoreType.DMA((3,)),
+            *(GATHER_SEMS * 2),
+            pltpu.SemaphoreType.DMA((15,)),
+            pltpu.SemaphoreType.DMA((CHIPS,)),
+            pltpu.SemaphoreType.DMA((CHIPS // 2,)),
+            pltpu.SemaphoreType.DMA((6,)),
+            pltpu.SemaphoreType.DMA((SLOTS,)),
+            pltpu.SemaphoreType.DMA((5,)),
             *(RING_SEMS * 2),
         ],
         compiler_params=pltpu.CompilerParams(
-            collective_id=3, has_side_effects=True, vmem_limit_bytes=VMEM_LIMIT
+            collective_id=0, has_side_effects=True, vmem_limit_bytes=VMEM_LIMIT
         ),
-    )(lambdas, gain, q, kv, normed)
+    )(x, cot, mask, gain, lambdas, sub, wq, wk, wv)
+
+
+SPAN = 1024
+SPANS = CHIPS * BLOCK // SPAN
+PER_SPAN = SPAN // BLOCK // 2
+EARLY_SPANS = 4
 
 
 def middle_kernel(
-    x_ref, cot_ref, mask_ref, gain_ref, tiles_ref, wo_ref, wg_ref, wu_ref, wd_ref,
-    dout_ref,
-    out_ref, dres_ref, gainpart_ref, dresall_ref, dmix_ref,
-    lffn_ref, lgu_ref, lhid_ref, ldout_ref, lmix_ref,
-    land, wo, wg, wu, wd, fbuf, rbuf, dms, doutall_ref, gu_ref, hid_ref, mix_ref, *rest,
+    x_ref, cot_ref, mask_ref, gain_ref, lambdas_ref, sub_ref, tiles_ref, wo_ref, wg_ref, wu_ref, wd_ref,
+    dout_ref, q_ref, kv_ref, parts_ref, log_ref,
+    out_ref, dres_ref, gainpart_ref, dqkv_ref, small_ref, gate_ref, up_ref, down_ref,
+    lmix_ref, xdres_ref,
+    land, wo, wg, wu, wd, fbuf, rbuf, dms, dout_all, gu, hid, mix,
+    q, kv, parts_all, logs, dmix,
+    lffn, lgu, lhid, ldout, pgu, pdown, sgu, sdown, swap, swapped,
+    k_t, acc, q_cols, q_rows, d_cols, d_rows, deltas, dq_acc, dq_out, given, sib, both, home, *rest,
 ):
     chip, core, t = place()
-    reduces = [rest[9 * k : 9 * k + 9] for k in range(3)]
-    gathers = [rest[27 + 2 * k : 29 + 2 * k] for k in range(2)]
-    wsem, hsend, hrecv, tsend, trecv, osem = rest[31:37]
-    sems = rest[37:]
-    ring_dout = RingGather(lambda p: doutall_ref.at[p // 2], ldout_ref, *sems[0:2], "z", chip, core, t)
-    ring_mix = RingGather(lambda p: mix_ref, lmix_ref, *sems[2:4], "x", chip, core, t)
-    ring_ffn = RingGather(
-        lambda p: fbuf.at[:, pl.ds(pl.multiple_of((p // 2) * 768, 128), 768)],
-        lffn_ref, *sems[4:6], "x", chip, core, t,
-    )
-    ring_hid = RingGather(lambda p: hid_ref.at[p % 2], lhid_ref, *sems[6:8], "z", chip, core, t)
-    ring_gu = RingGather(lambda p: gu_ref.at[p % 2], lgu_ref, *sems[8:10], "x", chip, core, t)
-    rings = (ring_dout, ring_mix, ring_ffn, ring_hid, ring_gu)
-    take_dout = pltpu.make_async_copy(dout_ref, doutall_ref, osem.at[4])
-    take_dout.start()
+    s = 2 * chip + core
+    slot = s % 10
+    head = chip // PER_HEAD
+    served = chip < SERVED
+    x_at, z_at = chip % 4, chip // 8
+    taken = iter(rest)
+
+    def take(count):
+        return [next(taken) for _ in range(count)]
+
+    reduces = [take(9) for _ in range(2)]
+    gather_sems = [take(2) for _ in range(2)]
+    ring_sems = [take(2) for _ in range(5)]
+    once_sems = take(4)
+    scatter = [take(2) for _ in range(2)]
+    wsem, osem, hsend, hrecv, tsend, trecv, swap_sem = take(7)
+    dsend, drecv, ksend, krecv, gsend, grecv = take(6)
+
     loads = [
         weight_load(wo_ref, wo, wsem.at[0], core, 384),
         weight_load(wg_ref, wg, wsem.at[1], core, 1024),
         weight_load(wu_ref, wu, wsem.at[2], core, 1024),
         weight_load(wd_ref, wd, wsem.at[3], core, 1024),
     ]
-    for load in loads:
+    fetches = [
+        pltpu.make_async_copy(src, dst, osem.at[4 + k])
+        for k, (src, dst) in enumerate(
+            ((dout_ref, dout_all), (q_ref, q), (kv_ref, kv), (parts_ref, parts_all), (log_ref, logs))
+        )
+    ]
+    loads[0].start()
+    fetches[0].start()
+    for load in loads[1:]:
         load.start()
-    gather_f = QuadGather(fbuf, *gathers[0], chip, core, t)
-    gather_r = QuadGather(rbuf, *gathers[1], chip, core, t)
+    for fetch in fetches[1:]:
+        fetch.start()
+    gather_f = QuadGather(fbuf, *gather_sems[0], chip, core, t)
+    gather_r = QuadGather(rbuf, *gather_sems[1], chip, core, t)
+    ring_dout = RingGather(lambda p: dout_all.at[p // 2], ldout, *ring_sems[0], "x", chip, core, t)
+    ring_mix = RingGather(lambda p: mix, lmix_ref, *ring_sems[1], "x", chip, core, t)
+    ring_hid = RingGather(lambda p: hid.at[p % 2], lhid, *ring_sems[2], "x", chip, core, t)
+    ring_gu = RingGather(lambda p: gu.at[p % 2], lgu, *ring_sems[3], "z", chip, core, t)
+    ring_dres = RingGather(
+        lambda p: rbuf.at[:, pl.ds(pl.multiple_of(p * 384, 128), 384)],
+        xdres_ref, *ring_sems[4], "x", chip, core, t,
+    )
+    ring_ffn = RingGatherOnce(
+        lambda p: fbuf.at[:, pl.ds(pl.multiple_of((p // 2) * 768, 128), 768)],
+        lffn, *once_sems, "z", chip, core, t,
+    )
+    send_down = Scatter(
+        pdown, sdown, *scatter[0], 16, 16 * (x_at // 2), 8 * (x_at % 2) + chip // 4, chip, core, t
+    )
+    send_gu = Scatter(
+        pgu, sgu, *scatter[1], 16, 16 * (z_at // 2), 8 * (z_at % 2) + chip % 8, chip, core, t
+    )
     mine = pl.ds(pl.multiple_of(gather_f.mine, ROWS), ROWS)
     dout = cot_ref[...] * mask_ref[...]
+    lam = lambda_of(lambdas_ref, chip, t)
+    small_ref[...] = jnp.zeros_like(small_ref)
     greet_all(chip, core, t)
     home_sends(tiles_ref, land, hsend, hrecv, chip, core, t, True)
-    take_dout.wait()
-    ring_dout.start()
     loads[0].wait()
     home_waits(tiles_ref, land, hrecv)
     for j in range(3):
         for u in range(2):
-            mix_ref[u * 128 : (u + 1) * 128, j * 128 : (j + 1) * 128] = land[j, u]
+            mix[u * 128 : (u + 1) * 128, j * 128 : (j + 1) * 128] = land[j, u]
+    red = QuadReduce(*reduces[0], chip, core, t)
+    red.run(lambda k: matmul_t(mix[...], wo[k * CW : (k + 1) * CW, :]))
+    fetches[0].wait()
+    ring_dout.start()
     ring_mix.start()
-    red = QuadReduce(*reduces[0], chip, core, t)
-    red.run(lambda k: matmul_t(mix_ref[...], wo[k * CW : (k + 1) * CW, :]))
     resid = x_ref[...] + jnp.concatenate([red.result(k) for k in range(NC)], axis=1)
     ffn_rms = rms_scale(resid)
     ffn_hat = resid * ffn_rms
     fbuf[mine, :] = (ffn_hat * gain_ref[...]).astype(BF)
     gather_f.start()
+    for load in loads[1:]:
+        load.wait()
+    red.drain()
     gather_f.finish()
     ring_ffn.start()
-    for load in loads[1:]:
-        load.wait()
 
     def hidden_step(n, carry):
         cols = pl.ds(pl.multiple_of(n * 256, 256), 256)
         b, at = n // 2, n % 2
         gate = matmul(fbuf[...], wg[:, cols])
         up = matmul(fbuf[...], wu[:, cols])
-        d_hidden = matmul(doutall_ref[0], wd[:768, cols]) + matmul(doutall_ref[1], wd[768:, cols])
+        d_hidden = matmul(dout_all[0], wd[:768, cols]) + matmul(dout_all[1], wd[768:, cols])
         sig = 1.0 / (1.0 + jnp.exp(-gate))
         silu = gate * sig
         to = pl.ds(pl.multiple_of(at * 256, 256), 256)
         up_to = pl.ds(pl.multiple_of(512 + at * 256, 256), 256)
-        hid_ref[b, :, to] = (silu * up).astype(BF)
-        gu_ref[b, :, to] = (d_hidden * up * sig * (1.0 + gate * (1.0 - sig))).astype(BF)
-        gu_ref[b, :, up_to] = (d_hidden * silu).astype(BF)
+        hid[b, :, to] = (silu * up).astype(BF)
+        gu[b, :, to] = (d_hidden * up * sig * (1.0 + gate * (1.0 - sig))).astype(BF)
+        gu[b, :, up_to] = (d_hidden * silu).astype(BF)
         return carry
 
     lax.fori_loop(0, 4, hidden_step, 0)
-    ring_hid.start()
-    ring_gu.start()
-    red2 = QuadReduce(*reduces[1], chip, core, t)
+    red2 = QuadReduce(*reduces[0], chip, core, t)
 
     def ffn_term(k):
         rows = slice(k * CW, (k + 1) * CW)
         return (
-            matmul_t(gu_ref[0, :, :512], wg[rows, :512])
-            + matmul_t(gu_ref[1, :, :512], wg[rows, 512:])
-            + matmul_t(gu_ref[0, :, 512:], wu[rows, :512])
-            + matmul_t(gu_ref[1, :, 512:], wu[rows, 512:])
+            matmul_t(gu[0, :, :512], wg[rows, :512])
+            + matmul_t(gu[1, :, :512], wg[rows, 512:])
+            + matmul_t(gu[0, :, 512:], wu[rows, :512])
+            + matmul_t(gu[1, :, 512:], wu[rows, 512:])
         )
 
     red2.run(ffn_term)
-    red3 = QuadReduce(*reduces[2], chip, core, t)
+    ring_hid.start()
+    ring_gu.start()
+    red3 = QuadReduce(*reduces[1], chip, core, t)
     d_ffn = jnp.concatenate([red2.result(k) for k in range(NC)], axis=1)
     gainpart_ref[...] = jnp.sum(d_ffn * ffn_hat, axis=0, keepdims=True)
     d_resid = dout + norm_back(d_ffn, gain_ref[...], ffn_rms, ffn_hat)
@@ -788,128 +871,23 @@
     rbuf[mine, :] = d_resid.astype(BF)
     gather_r.start()
     red3.run(
-        lambda k: matmul_t(hid_ref[0], wd[k * CW : (k + 1) * CW, :512])
-        + matmul_t(hid_ref[1], wd[k * CW : (k + 1) * CW, 512:])
+        lambda k: matmul_t(hid[0], wd[k * CW : (k + 1) * CW, :512])
+        + matmul_t(hid[1], wd[k * CW : (k + 1) * CW, 512:])
     )
     gather_r.finish()
     d_mixed = matmul(rbuf[...], wo[...]).astype(BF)
     for j in range(3):
         for u in range(2):
             dms[j, u] = d_mixed[u * 128 : (u + 1) * 128, j * 128 : (j + 1) * 128]
-    tile_sends(dms, dmix_ref, tsend, trecv, chip, core, t, True)
-    saves = pieces_out(rbuf, dresall_ref, osem, 0, 4)
+    tile_sends(dms, dmix, tsend, trecv, chip, core, t, True)
+    ring_ffn.forward()
     out_ref[...] = resid + jnp.concatenate([red3.result(k) for k in range(NC)], axis=1)
-    tile_waits(dms, dmix_ref, tsend, trecv, chip, core, t)
-    tile_sends(dms, dmix_ref, tsend, trecv, chip, core, t, False)
-    home_sends(tiles_ref, land, hsend, hrecv, chip, core, t, False)
-    for gather in (gather_f, gather_r):
-        gather.drain()
-    for reduce in (red, red2, red3):
-        reduce.drain()
-    for save in saves:
-        save.wait()
-    for ring in rings:
-        ring.finish()
-        ring.drain()
-
-
-def middle(x, cot, mask, gain, tiles, wo, wg, wu, wd, dout_all):
-    return pl.pallas_call(
-        middle_kernel,
-        name="middle",
-        out_shape=(
-            shape((ROWS, D), F32),
-            shape((ROWS, D), F32),
-            shape((1, D), F32),
-            shape(QUARTERS, BF),
-            shape((SLOTS, TILE, 128), BF),
-            shape(GATHERED, BF),
-            shape((4, BLOCK, 1024), BF),
-            shape((4, BLOCK, 512), BF),
-            shape(GATHERED, BF),
-            shape(GATHERED_Q, BF),
-        ),
-        in_specs=[VM, VM, VM, VM] + [ANY] * 6,
-        out_specs=(VM, VM, VM) + (ANY,) * 7,
-        scratch_shapes=[
-            pltpu.VMEM((3, 2, TILE, 128), BF),
-            pltpu.VMEM((D, 384), BF),
-            pltpu.VMEM((D, 1024), BF),
-            pltpu.VMEM((D, 1024), BF),
-            pltpu.VMEM((D, 1024), BF),
-            pltpu.VMEM((BLOCK, D), BF),
-            pltpu.VMEM((BLOCK, D), BF),
-            pltpu.VMEM((3, 2, TILE, 128), BF),
-            pltpu.VMEM(HALVES, BF),
-            pltpu.VMEM((2, BLOCK, 1024), BF),
-            pltpu.VMEM((2, BLOCK, 512), BF),
-            pltpu.VMEM((BLOCK, 384), BF),
-            *(REDUCE_SCRATCH * 3),
-            *(GATHER_SEMS * 2),
-            pltpu.SemaphoreType.DMA((4,)),
-            pltpu.SemaphoreType.DMA((SLOTS,)),
-            pltpu.SemaphoreType.DMA((3, 2)),
-            pltpu.SemaphoreType.DMA((6,)),
-            pltpu.SemaphoreType.DMA((SLOTS,)),
-            pltpu.SemaphoreType.DMA((5,)),
-            *(RING_SEMS * 5),
-        ],
-        compiler_params=pltpu.CompilerParams(
-            collective_id=1, has_side_effects=True, vmem_limit_bytes=VMEM_LIMIT
-        ),
-    )(x, cot, mask, gain, tiles, wo, wg, wu, wd, dout_all)
-
-
-SPAN = 1024
-SPANS = CHIPS * BLOCK // SPAN
-PER_SPAN = SPAN // BLOCK // 2
-
-
-def attend_back_kernel(
-    lambdas_ref, gain_ref, q_ref, kv_ref, dmix_ref, parts_ref, log_ref,
-    lffn_ref, lgu_ref, lhid_ref, ldout_ref, dres_ref,
-    dqkv_ref, small_ref, gate_ref, up_ref, down_ref, xdres_ref,
-    k_t, acc, q_cols, q_rows, d_cols, d_rows, deltas, dq_acc, dq_out, own, given, sib, both, home, land,
-    lffn, lgu, lhid, ldout, pgu, pdown, sgu, sdown, swap, swapped, *sems,
-):
-    chip, core, t = place()
-    s = 2 * chip + core
-    slot = s % 10
-    head = chip // PER_HEAD
-    served = chip < SERVED
-    x, z = chip % 4, chip // 8
-    loads = [
-        pltpu.make_async_copy(src, dst, sems[0].at[k])
-        for k, (src, dst) in enumerate(
-            ((lhid_ref, lhid), (ldout_ref, ldout), (lffn_ref, lffn), (lgu_ref, lgu))
-        )
-    ]
-    for load in loads:
-        load.start()
-    lam = lambda_of(lambdas_ref, chip, t)
-    greet_all(chip, core, t)
-    ring_dres = RingGather(lambda p: dres_ref.at[p], xdres_ref, *sems[1:3], "x", chip, core, t)
-    send_down = Scatter(
-        pdown, sdown, *sems[3:5], 16, 16 * (z // 2), 8 * (z % 2) + chip % 8, chip, core, t
-    )
-    send_gu = Scatter(
-        pgu, sgu, *sems[5:7], 16, 16 * (x // 2), 8 * (x % 2) + chip // 4, chip, core, t
-    )
-    swap_sem, dsend, drecv, ksend, krecv, hsend, hrecv = sems[7:]
-    loads[0].wait()
-    loads[1].wait()
-    block_grad(pdown, 0, ldout, lhid[...].reshape(4 * BLOCK, 512), 256)
-    send_down.each(True)
-    loads[2].wait()
-    loads[3].wait()
-    block_grad(pgu, 0, lffn, lgu[:, :, :512].reshape(4 * BLOCK, 512), 256)
-    block_grad(pgu, 512, lffn, lgu[:, :, 512:].reshape(4 * BLOCK, 512), 256)
-    send_gu.each(True)
-    ring_dres.start()
-    small_ref[...] = jnp.zeros_like(small_ref)
+    for fetch in fetches[1:]:
+        fetch.wait()
 
     def to_sibling(o):
-        return remote(given.at[o], sib.at[o], dsend.at[o], drecv.at[o], s + 1 - 2 * core, t)
+        at = o % (2 * PER_SPAN)
+        return remote(given.at[at], sib.at[o], dsend.at[at], drecv.at[o], s + 1 - 2 * core, t)
 
     def to_home(o, start):
         target = 2 * (2 * o + core) + head // 3
@@ -934,32 +912,38 @@
 
     @pl.when(served)
     def _():
-        unit = eye()
+        unit = eye(128)
 
         def flip(b, carry):
-            for u in range(2):
-                rows = pl.ds(pl.multiple_of(b * 2 * KB + u * KB, KB), KB)
-                k_t[:, rows] = matmul_t(unit, kv_ref[rows, :128]).astype(BF)
+            rows = pl.ds(pl.multiple_of(b * KB, KB), KB)
+            block = kv[pl.ds(2 * b, 2), :, :128].reshape(KB, 128)
+            k_t[:, rows] = matmul_t(unit, block).astype(BF)
             return carry
 
-        lax.fori_loop(0, SPANS, flip, 0)
+        lax.fori_loop(0, CHIPS * BLOCK // KB, flip, 0)
+
+    tile_waits(dms, dmix, tsend, trecv, chip, core, t)
+    ring_dout.finish()
+    ring_hid.finish()
+    block_grad(pdown, 0, ldout, lhid[...].reshape(4 * BLOCK, 512), 256)
+    send_down.each(True)
 
     for r in range(SLOTS):
 
         @pl.when(served if r else jnp.logical_and(served, slot < 4))
         def _():
-            q_cols[r] = both_maps(q_ref[r].astype(F32).T).astype(BF)
-            q = q_ref[r].astype(F32)
-            left = lax.broadcasted_iota(jnp.int32, q.shape, 1) < 64
+            q_wide = q[r].astype(F32)
+            q_cols[r] = both_maps(q_wide.T).astype(BF)
+            left = lax.broadcasted_iota(jnp.int32, q_wide.shape, 1) < 64
             q_rows[r] = jnp.concatenate(
-                [jnp.where(left, q, 0.0), jnp.where(left, 0.0, q)], axis=0
+                [jnp.where(left, q_wide, 0.0), jnp.where(left, 0.0, q_wide)], axis=0
             ).astype(BF)
-            parts = parts_ref[r]
+            parts = parts_all[r]
             first, second = parts[:, :TILE], parts[:, TILE:]
             rms, hat = group_norm(parts, lam)
-            e_t = dmix_ref[r].astype(F32).T * OUT_SCALE
+            e_t = dmix[r].astype(F32).T * OUT_SCALE
             column = jnp.sum(e_t * hat, axis=1, keepdims=True)
-            d_differ = norm_back(e_t, gain_ref[...], rms, hat, 0).astype(BF)
+            d_differ = norm_back(e_t, sub_ref[...], rms, hat, 0).astype(BF)
             d_wide = d_differ.astype(F32)
             d_cols[r] = d_differ
             d_rows[r] = d_wide.T.astype(BF)
@@ -973,69 +957,85 @@
             deltas[r, 1:2, :] = -lam * second_dot
             dq_acc[r] = jnp.zeros((128, 2 * TILE), F32)
 
+    def pass_on(k):
+        for u in range(PER_SPAN):
+            o = PER_SPAN * lax.rem(chip + k, SPANS) + u
+            to_sibling(o).wait_recv()
+            both[o] = (both[o].astype(F32) + sib[o].astype(F32)).astype(BF)
+            to_home(o, True)
+
+    def span(k, carry):
+        b = lax.rem(chip + k, SPANS)
+        start = pl.multiple_of(b * SPAN, SPAN)
+        rows = pl.ds(start, SPAN)
+        blocks = pl.ds(b * (SPAN // BLOCK), SPAN // BLOCK)
+        acc[...] = jnp.zeros_like(acc)
+
+        def step(r, masked):
+            score = matmul(kv[blocks, :, :128].reshape(SPAN, 128), q_cols[r])
+            prob = jnp.exp2(score * SCORE - logs[r])
+            if masked:
+                prob = jnp.where(key_mask(start, SPAN, tile_at(r), 2 * TILE), prob, 0.0)
+            upper = matmul(kv[blocks, :, 128:].reshape(SPAN, 128), d_cols[r])
+            p1, p2 = prob[:, :TILE], prob[:, TILE:]
+            ds = jnp.concatenate(
+                [p1 * (upper - deltas[r, 0:1, :]), p2 * (-lam * upper - deltas[r, 1:2, :])],
+                axis=1,
+            ).astype(BF)
+            mixed = (p1 - lam * p2).astype(BF)
+            acc[:, :128] += matmul(ds, q_rows[r])
+            acc[:, 128:] += matmul(mixed, d_rows[r])
+            dq_acc[r] += matmul(k_t[:, rows], ds)
+
+        def masked_step(r, carry):
+            step(r, True)
+            return carry
+
+        def full_step(r, carry):
+            step(r, False)
+            return carry
+
+        reach, past = 0, 0
+        for r in range(SLOTS):
+            last = tile_of(slot, r) * TILE // SPAN
+            counts = (slot < 4) if r == 0 else True
+            reach += jnp.where(jnp.logical_and(counts, last >= b), 1, 0)
+            past += jnp.where(jnp.logical_and(counts, last > b), 1, 0)
+        lax.fori_loop(SLOTS - reach, SLOTS - past, masked_step, 0)
+        lax.fori_loop(SLOTS - past, SLOTS, full_step, 0)
+
+        @pl.when(k >= 2)
+        def _():
+            for u in range(PER_SPAN):
+                to_sibling(PER_SPAN * lax.rem(chip + k - 2, SPANS) + u).wait_send()
+
+        for u in range(PER_SPAN):
+            o = PER_SPAN * b + u
+            for ref, at, which in ((given, o % (2 * PER_SPAN), 1 - core), (both, o, core)):
+                part = acc[pl.ds(pl.multiple_of((2 * u + which) * BLOCK, BLOCK), BLOCK), :]
+                ref[at, :, :128] = (part[:, :128] * 0.125).astype(BF)
+                ref[at, :, 128:] = part[:, 128:].astype(BF)
+            to_sibling(o).start()
+
+        @pl.when(k > 0)
+        def _():
+            pass_on(k - 1)
+
+        return carry
+
     @pl.when(served)
     def _():
-        def span(k, carry):
-            b = lax.rem(chip + k, SPANS)
-            start = pl.multiple_of(b * SPAN, SPAN)
-            rows = pl.ds(start, SPAN)
-            acc[...] = jnp.zeros_like(acc)
-
-            def step(r, masked):
-                block = kv_ref[rows, :]
-                score = matmul(block[:, :128], q_cols[r])
-                prob = jnp.exp2(score * SCORE - log_ref[r])
-                if masked:
-                    prob = jnp.where(key_mask(start, SPAN, tile_at(r), 2 * TILE), prob, 0.0)
-                upper = matmul(block[:, 128:], d_cols[r])
-                p1, p2 = prob[:, :TILE], prob[:, TILE:]
-                ds = jnp.concatenate(
-                    [p1 * (upper - deltas[r, 0:1, :]), p2 * (-lam * upper - deltas[r, 1:2, :])],
-                    axis=1,
-                ).astype(BF)
-                mix = (p1 - lam * p2).astype(BF)
-                acc[:, :128] += matmul(ds, q_rows[r])
-                acc[:, 128:] += matmul(mix, d_rows[r])
-                dq_acc[r] += matmul(k_t[:, rows], ds)
-
-            def masked_step(r, carry):
-                step(r, True)
-                return carry
-
-            def full_step(r, carry):
-                step(r, False)
-                return carry
-
-            reach, past = 0, 0
-            for r in range(SLOTS):
-                last = tile_of(slot, r) * TILE // SPAN
-                counts = (slot < 4) if r == 0 else True
-                reach += jnp.where(jnp.logical_and(counts, last >= b), 1, 0)
-                past += jnp.where(jnp.logical_and(counts, last > b), 1, 0)
-            lax.fori_loop(SLOTS - reach, SLOTS - past, masked_step, 0)
-            lax.fori_loop(SLOTS - past, SLOTS, full_step, 0)
-            for u in range(PER_SPAN):
-                o = PER_SPAN * b + u
-                for ref, which in ((given, 1 - core), (own, core)):
-                    part = acc[pl.ds(pl.multiple_of((2 * u + which) * BLOCK, BLOCK), BLOCK), :]
-                    ref[o, :, :128] = (part[:, :128] * 0.125).astype(BF)
-                    ref[o, :, 128:] = part[:, 128:].astype(BF)
-                to_sibling(o).start()
-
-            @pl.when(k > 0)
-            def _():
-                pass_on(k - 1)
-
-            return carry
-
-        def pass_on(k):
-            for u in range(PER_SPAN):
-                o = PER_SPAN * lax.rem(chip + k, SPANS) + u
-                to_sibling(o).wait_recv()
-                both[o] = (own[o].astype(F32) + sib[o].astype(F32)).astype(BF)
-                to_home(o, True)
-
-        lax.fori_loop(0, SPANS, span, 0)
+        lax.fori_loop(0, EARLY_SPANS, span, 0)
+
+    ring_ffn.finish()
+    ring_gu.finish()
+    block_grad(pgu, 0, lffn, lgu[:, :, :512].reshape(4 * BLOCK, 512), 256)
+    block_grad(pgu, 512, lffn, lgu[:, :, 512:].reshape(4 * BLOCK, 512), 256)
+    send_gu.each(True)
+
+    @pl.when(served)
+    def _():
+        lax.fori_loop(EARLY_SPANS, SPANS, span, 0)
         pass_on(SPANS - 1)
 
     for r in range(SLOTS):
@@ -1045,24 +1045,14 @@
             dq_t = jnp.concatenate([dq_acc[r, :64, :TILE], dq_acc[r, 64:, TILE:]], axis=0)
             dq_out[r] = (dq_t * 0.125).T.astype(BF)
 
-    home_sends(dq_out, land, hsend, hrecv, chip, core, t, True)
+    home_sends(dq_out, land, gsend, grecv, chip, core, t, True)
+    ring_dres.start()
     send_down.wait()
     for b in range(2):
         total = send_down.total(b, slice(0, 512))
         for h in range(2):
             swap[h, :, 2048 + b * 512 : 2560 + b * 512] = total[h * 24 : h * 24 + 24]
-    send_gu.wait()
-    for b in range(2):
-        for m in range(2):
-            total = send_gu.total(b, slice(m * 512, m * 512 + 512))
-            at = m * 1024 + b * 512
-            for h in range(2):
-                swap[h, :, at : at + 512] = total[h * 24 : h * 24 + 24]
-    swap_copy = remote(
-        swap.at[1 - core], swapped, swap_sem.at[0], swap_sem.at[1], s + 1 - 2 * core, t
-    )
-    swap_copy.start()
-    home_waits(dq_out, land, hrecv)
+    home_waits(dq_out, land, grecv)
     for j in range(3):
         for u in range(2):
             dqkv_ref[0, u * 128 : (u + 1) * 128, j * 128 : (j + 1) * 128] = land[j, u]
@@ -1074,22 +1064,45 @@
             total = total + home[spot].astype(F32)
         dqkv_ref[1, :, j * 128 : (j + 1) * 128] = total[:, :128].astype(BF)
         dqkv_ref[2, :, j * 128 : (j + 1) * 128] = total[:, 128:].astype(BF)
+    send_gu.wait()
+    for b in range(2):
+        for m in range(2):
+            total = send_gu.total(b, slice(m * 512, m * 512 + 512))
+            at = m * 1024 + b * 512
+            for h in range(2):
+                swap[h, :, at : at + 512] = total[h * 24 : h * 24 + 24]
+    swap_copy = remote(
+        swap.at[1 - core], swapped, swap_sem.at[0], swap_sem.at[1], s + 1 - 2 * core, t
+    )
+    swap_copy.start()
+    ring_mix.finish()
+    ring_dres.finish()
+    for ring in (ring_dout, ring_mix, ring_hid, ring_gu, ring_dres, ring_ffn):
+        ring.drain()
+    send_gu.each(False)
+    send_down.each(False)
+    home_sends(tiles_ref, land, hsend, hrecv, chip, core, t, False)
+    home_sends(dq_out, land, gsend, grecv, chip, core, t, False)
+    tile_sends(dms, dmix, tsend, trecv, chip, core, t, False)
+    for gather in (gather_f, gather_r):
+        gather.drain()
+    red2.drain()
+    red3.drain()
+
+    @pl.when(served)
+    def _():
+        for k in (SPANS - 2, SPANS - 1):
+            for u in range(PER_SPAN):
+                to_sibling(PER_SPAN * lax.rem(chip + k, SPANS) + u).wait_send()
+
+        def last(o, carry):
+            to_home(o, False)
+            return carry
+
+        lax.fori_loop(0, CHIPS // 2, last, 0)
+
     swap_copy.wait()
     swap_out(swap, swapped, ((gate_ref, 0), (up_ref, 1024), (down_ref, 2048)), 1024, core)
-    ring_dres.finish()
-    ring_dres.drain()
-    send_gu.each(False)
-    send_down.each(False)
-    home_sends(dq_out, land, hsend, hrecv, chip, core, t, False)
-
-    @pl.when(served)
-    def _():
-        def last(o, carry):
-            to_sibling(o).wait_send()
-            to_home(o, False)
-            return carry
-
-        lax.fori_loop(0, CHIPS // 2, last, 0)
 
 
 def swap_out(swap, swapped, outs, width, core):
@@ -1104,63 +1117,94 @@
                 ref[:, other : other + width] = swapped[:, at : at + width]
 
 
-def attend_back(lambdas, gain, q, kv, dmix, parts, logs, lffn, lgu, lhid, ldout, dres):
+def middle_part(
+    x, cot, mask, gain, lambdas, sub, tiles, wo, wg, wu, wd, dout_all, q, kv, parts, logs
+):
     half = (CHIPS // 2, BLOCK, 256)
+    vm = pltpu.VMEM
+    sem = pltpu.SemaphoreType.DMA
     return pl.pallas_call(
-        attend_back_kernel,
-        name="attend_back",
+        middle_kernel,
+        name="middle",
         out_shape=(
+            shape((ROWS, D), F32),
+            shape((ROWS, D), F32),
+            shape((1, D), F32),
             shape((3, BLOCK, 384), BF),
             shape((2, 128), F32),
             shape((24, 2048), F32),
             shape((24, 2048), F32),
             shape((24, 2048), F32),
             shape(GATHERED_Q, BF),
+            shape(GATHERED_Q, BF),
         ),
-        in_specs=[VM] * 7 + [ANY] * 5,
-        out_specs=(VM,) * 5 + (ANY,),
+        in_specs=[VM] * 6 + [ANY] * 10,
+        out_specs=(VM,) * 8 + (ANY,) * 2,
         scratch_shapes=[
-            pltpu.VMEM((128, CHIPS * BLOCK), BF),
-            pltpu.VMEM((SPAN, 256), F32),
-            pltpu.VMEM((SLOTS, 128, 2 * TILE), BF),
-            pltpu.VMEM((SLOTS, 2 * TILE, 128), BF),
-            pltpu.VMEM((SLOTS, 128, TILE), BF),
-            pltpu.VMEM((SLOTS, TILE, 128), BF),
-            pltpu.VMEM((SLOTS, 2, TILE), F32),
-            pltpu.VMEM((SLOTS, 128, 2 * TILE), F32),
-            pltpu.VMEM((SLOTS, TILE, 128), BF),
-            pltpu.VMEM(half, BF),
-            pltpu.VMEM(half, BF),
-            pltpu.VMEM(half, BF),
-            pltpu.VMEM(half, BF),
-            pltpu.VMEM((3 * PER_HEAD, BLOCK, 256), BF),
-            pltpu.VMEM((3, 2, TILE, 128), BF),
-            pltpu.VMEM(GATHERED, BF),
-            pltpu.VMEM((4, BLOCK, 1024), BF),
-            pltpu.VMEM((4, BLOCK, 512), BF),
-            pltpu.VMEM(GATHERED, BF),
-            pltpu.VMEM((768, 1024), BF),
-            pltpu.VMEM((768, 512), BF),
-            pltpu.VMEM((16, CHUNK, 1024), BF),
-            pltpu.VMEM((16, CHUNK, 512), BF),
-            pltpu.VMEM((2, 24, 3072), F32),
-            pltpu.VMEM((24, 3072), F32),
-            pltpu.SemaphoreType.DMA((4,)),
-            *RING_SEMS,
+            vm((3, 2, TILE, 128), BF),
+            vm((D, 384), BF),
+            vm((D, 1024), BF),
+            vm((D, 1024), BF),
+            vm((D, 1024), BF),
+            vm((BLOCK, D), BF),
+            vm((BLOCK, D), BF),
+            vm((3, 2, TILE, 128), BF),
+            vm(HALVES, BF),
+            vm((2, BLOCK, 1024), BF),
+            vm((2, BLOCK, 512), BF),
+            vm((BLOCK, 384), BF),
+            vm((SLOTS, TILE, 128), BF),
+            vm(KV, BF),
+            vm((SLOTS, 128, 2 * TILE), F32),
+            vm((SLOTS, 1, 2 * TILE), F32),
+            vm((SLOTS, TILE, 128), BF),
+            vm(GATHERED, BF),
+            vm((4, BLOCK, 1024), BF),
+            vm((4, BLOCK, 512), BF),
+            vm(GATHERED, BF),
+            vm((768, 1024), BF),
+            vm((768, 512), BF),
+            vm((16, CHUNK, 1024), BF),
+            vm((16, CHUNK, 512), BF),
+            vm((2, 24, 3072), F32),
+            vm((24, 3072), F32),
+            vm((128, CHIPS * BLOCK), BF),
+            vm((SPAN, 256), F32),
+            vm((SLOTS, 128, 2 * TILE), BF),
+            vm((SLOTS, 2 * TILE, 128), BF),
+            vm((SLOTS, 128, TILE), BF),
+            vm((SLOTS, TILE, 128), BF),
+            vm((SLOTS, 2, TILE), F32),
+            vm((SLOTS, 128, 2 * TILE), F32),
+            vm((SLOTS, TILE, 128), BF),
+            vm((2 * PER_SPAN, BLOCK, 256), BF),
+            vm(half, BF),
+            vm(half, BF),
+            vm((3 * PER_HEAD, BLOCK, 256), BF),
+            *(REDUCE_SCRATCH * 2),
+            *(GATHER_SEMS * 2),
+            *(RING_SEMS * 5),
+            *ONCE_SEMS,
             *scatter_sems(16),
             *scatter_sems(16),
-            pltpu.SemaphoreType.DMA((2,)),
-            pltpu.SemaphoreType.DMA((CHIPS // 2,)),
-            pltpu.SemaphoreType.DMA((CHIPS // 2,)),
-            pltpu.SemaphoreType.DMA((CHIPS // 2,)),
-            pltpu.SemaphoreType.DMA((3 * PER_HEAD,)),
-            pltpu.SemaphoreType.DMA((SLOTS,)),
-            pltpu.SemaphoreType.DMA((3, 2)),
+            sem((4,)),
+            sem((9,)),
+            sem((SLOTS,)),
+            sem((3, 2)),
+            sem((6,)),
+            sem((SLOTS,)),
+            sem((2,)),
+            sem((2 * PER_SPAN,)),
+            sem((CHIPS // 2,)),
+            sem((CHIPS // 2,)),
+            sem((3 * PER_HEAD,)),
+            sem((SLOTS,)),
+            sem((3, 2)),
         ],
         compiler_params=pltpu.CompilerParams(
-            collective_id=4, has_side_effects=True, vmem_limit_bytes=VMEM_LIMIT
+            collective_id=1, has_side_effects=True, vmem_limit_bytes=VMEM_LIMIT
         ),
-    )(lambdas, gain, q, kv, dmix, parts, logs, lffn, lgu, lhid, ldout, dres)
+    )(x, cot, mask, gain, lambdas, sub, tiles, wo, wg, wu, wd, dout_all, q, kv, parts, logs)
 
 
 def finish_kernel(
@@ -1344,22 +1388,15 @@
     count = len(arrays)
 
     def kernel(*refs):
-        copies = [
-            pltpu.make_async_copy(refs[k], refs[count + k], refs[2 * count].at[k])
-            for k in range(count)
-        ]
-        for cp in copies:
-            cp.start()
-        for cp in copies:
-            cp.wait()
+        for k in range(count):
+            refs[count + k][...] = refs[k][...]
 
     return pl.pallas_call(
         kernel,
         name="publish",
         out_shape=tuple(shape(a.shape, a.dtype) for a in arrays),
-        in_specs=[ANY] * count,
-        out_specs=(ANY,) * count,
-        scratch_shapes=[pltpu.SemaphoreType.DMA((count,))],
+        in_specs=[VM] * count,
+        out_specs=(VM,) * count,
     )(*arrays)
 
 
@@ -1372,17 +1409,12 @@
     sub_col = subln_gain.reshape(128, 1)
     mask = needle_mask.astype(F32).reshape(ROWS, 1)
 
-    normed, dout, q, kv = project(
-        hidden_in, cotangent, mask, attn_row, weight_query, weight_key, weight_value
-    )
-    kv = kv.reshape(CHIPS * BLOCK, 256)
-    mixed, parts, logs, xnormed, znormed = attend(lambdas, sub_col, q, kv, normed)
-    output, d_resid, ffn_part, dres, dmix, lffn, lgu, lhid, ldout, xmix = middle(
-        hidden_in, cotangent, mask, ffn_row, mixed,
-        weight_out, weight_gate, weight_up, weight_down, dout,
-    )
-    dqkv, small, grad_gate, grad_up, grad_down, xdres = attend_back(
-        lambdas, sub_col, q, kv, dmix, parts, logs, lffn, lgu, lhid, ldout, dres
+    dout, q, kv, mixed, parts, logs, xnormed, znormed = forward_part(
+        hidden_in, cotangent, mask, attn_row, lambdas, sub_col, weight_query, weight_key, weight_value
+    )
+    output, d_resid, ffn_part, dqkv, small, grad_gate, grad_up, grad_down, xmix, xdres = middle_part(
+        hidden_in, cotangent, mask, ffn_row, lambdas, sub_col, mixed,
+        weight_out, weight_gate, weight_up, weight_down, dout, q, kv, parts, logs,
     )
     grad_input, grad_query, grad_key, grad_value, grad_out, sums = finish(
         hidden_in, attn_row, d_resid, dqkv, weight_query, weight_key, weight_value,

time: 347 us -> 285 us (0.82)
  Pallas kernels: 335 us -> 270 us
    pallas_call x1, Pallas kernels: 51.8 us -> 2.59 us  [publish(): pl.pallas_call(kernel, name='publish', out_shape=tuple((shape(a.shape, a....]
    pallas_call x4 -> x2, Pallas kernels: 234 us -> 220 us  [the longest x1 148 us: middle_part(): pl.pallas_call(middle_kernel, name='middle', out_shape=(shape((ROWS, D),...]
where the time goes in v3:
time: 285 us; the launch traced here: 281 us
  Pallas kernels  270 us (95%)
  local copies, waits for them, and re-layouts  7.92 us (3%)
    pallas_call x1, Pallas kernels, middle_part(): pl.pallas_call(middle_kernel, name='middle', out_shape=(shape((ROWS, D),...  148 us
    pallas_call x1, Pallas kernels, forward_part(): pl.pallas_call(forward_kernel, name='forward', out_shape=(shape(HALVES, B...  72.5 us
    pallas_call x1, Pallas kernels, finish(): pl.pallas_call(finish_kernel, name='finish', out_shape=(shape((ROWS, D),...  47.5 us

profile of v3, /device:TPU:31, one launch (start us, length us, event | category | flops | bytes accessed | tf_op | source)
XLA Modules:
  0.0 281.0 jit_solution(10334695908536223977)
XLA Ops:
  0.6 0.0 copy-start.1
  0.7 1.4 copy.32.sub_ref
  2.1 0.7 convert_bitcast_fusion
  2.7 0.7 copy.30.mask_ref
  3.4 1.4 copy.31.lambdas_ref
  4.8 1.3 reshape.94.gain_ref
  6.1 72.5 %forward.1 = (bf16[2,256,768]{2,1,0:T(8,128)(2,1)}, bf16[7,128,128]{2,1,0:T(8,128)(2,1)}, bf16[32,256,256]{2,1,0:T(8,128)(2,1)}, bf16[7,128,128]{2,1,0:T(8,128)(...) custom-call(f32[64,1536]{1,0:T(8,128)} %x_ref.5, ...), custom_call_target="tpu_custom_call" | custom-call | tf_op jit(solution)/shard_map/forward/pallas_call | solution.py:692
  78.5 0.0 copy-done.1
  78.5 0.6 reshape.92.gain_ref
  79.1 147.6 %middle.1 = (f32[64,1536]{1,0:T(8,128)}, f32[64,1536]{1,0:T(8,128)}, f32[1,1536]{1,0:T(1,128)}, bf16[3,256,384]{2,1,0:T(8,128)(2,1)}, f32[2,128]{1,0:T(2,128)}, ...) custom-call(f32[64,1536]{1,0:T(8,128)} %x_ref.5, ...), custom_call_target="tpu_custom_call" | custom-call | tf_op jit(solution)/shard_map/middle/pallas_call | solution.py:1126
  226.7 0.0 copy-start
  226.7 47.5 %finish.1 = (f32[64,1536]{1,0:T(8,128)}, f32[24,768]{1,0:T(8,128)}, f32[24,768]{1,0:T(8,128)}, f32[24,768]{1,0:T(8,128)}, f32[24,768]{1,0:T(8,128)}, /*index=5*/f32[32,128]{1,0:T(8,128)}) custom-call(f32[64,1536]{1,0:T(8,128)} %x_ref.5, f32[1,1536]{1,0:T(1,128)} %reshape.94.gain_ref, f32[64,1536]{1,0:T(8,128)} %get-tuple-element.53.dres_ref, ...), custom_call_target="tpu_custom_call" | custom-call | tf_op jit(solution)/shard_map/finish/pallas_call | solution.py:1351
  274.3 0.0 copy-done
  274.3 0.2 multiply_reduce_fusion.1
  274.5 0.7 bitcast_multiply_fusion
  275.1 0.1 slice_multiply_fusion.2
  275.2 0.6 pad_maximum_fusion
  275.9 2.6 publish.1
  278.5 1.4 slice_bitcast_fusion
  279.8 1.2 slice_bitcast_fusion.2
Async XLA Ops:
  0.6 77.9 %copy-start.1 = (f32[1536]{0:T(1024)S(1)}, f32[1536]{0:T(1024)}, u32[]{:S(2)}) copy-start(f32[1536]{0:T(1024)} %param.20) | copy-start | bytes 18436
  226.7 47.6 %copy-start = (f32[4,12,64]{2,0,1:T(4,128)S(1)}, f32[4,12,64]{2,0,1:T(4,128)}, u32[]{:S(2)}) copy-start(f32[4,12,64]{2,0,1:T(4,128)} %param.18) | copy-start | bytes 36868

commit v4 on v3

--- a/solution.py
+++ b/solution.py
@@ -15,8 +15,8 @@
 OUT_SCALE = 1.0 - LAMBDA_INIT
 D = 1536
 CHIPS = 32
-SERVED = 30
 PER_HEAD = 5
+WORKERS = 15
 ROWS = 64
 BLOCK = 256
 TILE = 128
@@ -24,12 +24,23 @@
 KB = 512
 LOG2E = 1.4426950408889634
 SCORE = 0.125 * LOG2E
-VMEM_LIMIT = 60 * 2**20
+VMEM_LIMIT = 63 * 2**20
 
 
 def place():
     s = lax.axis_index("seq")
     return s // 2, s % 2, lax.axis_index("tp")
+
+
+def worker(chip, core):
+    x, y, z = chip % 4, chip // 4 % 2, chip // 8
+    at = 4 * z + x
+    return (x + y + z) % 2, at, at % PER_HEAD * 2 + core, at < WORKERS
+
+
+def worker_chip(parity, at):
+    x, z = at % 4, at // 4
+    return (2 * z + (x + z + parity) % 2) * 4 + x
 
 
 def owner_of(tile):
@@ -211,18 +222,18 @@
 RING_SEMS = [pltpu.SemaphoreType.DMA((3,)), pltpu.SemaphoreType.DMA((4,))]
 
 
-def block_grad(dst, start, left, right, step):
+def block_grad(dst, start, left, right, step, at=0, total=768):
     width = right.shape[1]
 
     def one(m, carry):
         cols = pl.ds(pl.multiple_of(m * step, 128), step)
-        part = left[:, :, cols].reshape(4 * BLOCK, step)
+        part = left[:, :, pl.ds(pl.multiple_of(at + m * step, 128), step)].reshape(4 * BLOCK, step)
         dst[cols, start : start + width] = lax.dot_general(
             part, right, (((0,), (0,)), ((), ())), preferred_element_type=F32
         ).astype(BF)
         return carry
 
-    lax.fori_loop(0, left.shape[2] // step, one, 0)
+    lax.fori_loop(0, total // step, one, 0)
 
 
 CHUNK = 48
@@ -238,6 +249,9 @@
         return self.part.at[pl.ds(pl.multiple_of(i * CHUNK, 16), CHUNK)]
 
     def each(self, start):
+        self.some(0, self.count, start)
+
+    def some(self, first, end, start):
         def one(o, carry):
             i = lax.rem(self.chip + 1 + 3 * o, self.count)
             owner = self.first + i
@@ -262,7 +276,7 @@
 
             return carry
 
-        lax.fori_loop(0, self.count, one, 0)
+        lax.fori_loop(first, end, one, 0)
 
     def wait(self):
         def one(k, carry):
@@ -351,7 +365,7 @@
     for j in range(3):
         for u in range(2):
             slot, index = owner_of(2 * chip + u)
-            target = (core * 3 + j) * 10 + slot
+            target = 2 * worker_chip(core, j * PER_HEAD + slot // 2) + slot % 2
             k = j * 2 + u
 
             if start:
@@ -370,9 +384,9 @@
 
 
 def tile_waits(tiles, land, send, recv, chip, core, t):
-    slot = (2 * chip + core) % 10
+    _, _, slot, served = worker(chip, core)
     for r in range(SLOTS):
-        here = chip < SERVED
+        here = served
         if r == 0:
             here = jnp.logical_and(here, slot < 4)
 
@@ -383,15 +397,14 @@
 
 def home_sends(tiles, land, send, recv, chip, core, t, start):
     s = 2 * chip + core
-    slot = s % 10
-    head = chip // PER_HEAD
+    parity, at, slot, served = worker(chip, core)
     for r in range(SLOTS):
-        here = chip < SERVED
+        here = served
         if r == 0:
             here = jnp.logical_and(here, slot < 4)
         tile = tile_of(slot, r)
-        target = (tile // 2) * 2 + head // 3
-        j, u = head % 3, tile % 2
+        target = (tile // 2) * 2 + parity
+        j, u = at // PER_HEAD, tile % 2
 
         if start:
 
@@ -473,24 +486,42 @@
     return rms, differ * rms
 
 
-def lambda_of(lambdas_ref, chip, t):
-    first = jnp.exp(jnp.sum(lambdas_ref[0] * lambdas_ref[1], axis=-1, keepdims=True))
-    second = jnp.exp(jnp.sum(lambdas_ref[2] * lambdas_ref[3], axis=-1, keepdims=True))
+def long_row(ref):
+    return jnp.concatenate([ref[k : k + 1, :] for k in range(12)], axis=1)
+
+
+def as_column(row):
+    return jnp.broadcast_to(row, (128, 128)).T
+
+
+def mask_column(mask_ref):
+    mask = mask_ref[...].astype(F32)
+    return as_column(jnp.concatenate([mask, mask], axis=1))[:ROWS, :1]
+
+
+def lambda_parts(lambdas_ref):
+    vectors = [lambdas_ref[:, k, :] for k in range(4)]
+    first = jnp.exp(jnp.sum(vectors[0] * vectors[1], axis=-1, keepdims=True))
+    second = jnp.exp(jnp.sum(vectors[2] * vectors[3], axis=-1, keepdims=True))
+    return vectors, first, second
+
+
+def lambda_of(lambdas_ref, head):
+    _, first, second = lambda_parts(lambdas_ref)
     every = first - second + LAMBDA_INIT
-    mine = lax.broadcasted_iota(jnp.int32, every.shape, 0) == 6 * t + chip // PER_HEAD
+    mine = lax.broadcasted_iota(jnp.int32, every.shape, 0) == head
     return jnp.sum(jnp.where(mine, every, 0.0), axis=0, keepdims=True)
 
 
 def forward_kernel(
-    x_ref, cot_ref, mask_ref, gain_ref, lambdas_ref, sub_ref, wq_ref, wk_ref, wv_ref,
-    dout_ref, q_ref, kv_ref, mixed_ref, parts_ref, log_ref, xnormed_ref, znormed_ref,
+    x_ref, cot_ref, mask_ref, attn_ref, sub_ref, lambdas_ref, wq_ref, wk_ref, wv_ref,
+    dout_ref, normed_ref, q_ref, kv_ref, mixed_ref, parts_ref, log_ref,
     nbuf, obuf, wbuf, kvsrc, qsrc, kv, q, v_t, peaks, kmax, acc, total,
-    wsem, nsend, nrecv, osend, orecv, kvsend, kvrecv, fsend, qsend, qrecv, osem, *sems,
+    wsem, nsend, nrecv, osend, orecv, kvsend, kvrecv, fsend, qsend, qrecv, osem,
 ):
     chip, core, t = place()
     s = 2 * chip + core
-    slot = s % 10
-    served = chip < SERVED
+    parity, place_at, slot, served = worker(chip, core)
     loads = [
         weight_load(ref, wbuf.at[k], wsem.at[k], core, 384)
         for k, ref in enumerate((wk_ref, wv_ref, wq_ref))
@@ -498,15 +529,16 @@
     for load in loads:
         load.start()
     x = x_ref[...]
-    normed = (x * rms_scale(x) * gain_ref[...]).astype(BF)
+    normed = (x * rms_scale(x) * long_row(attn_ref)).astype(BF)
     quad = QuadGather(nbuf, nsend, nrecv, chip, core, t)
     mine = pl.ds(pl.multiple_of(quad.mine, ROWS), ROWS)
     nbuf[mine, :] = normed
     quad_o = QuadGather(obuf, osend, orecv, chip, core, t)
     greet_all(chip, core, t)
     quad.start()
-    obuf[mine, :] = (cot_ref[...] * mask_ref[...]).astype(BF)
-    lam = lambda_of(lambdas_ref, chip, t)
+    obuf[mine, :] = (cot_ref[...] * mask_column(mask_ref)).astype(BF)
+    lam = lambda_of(lambdas_ref, 6 * t + 3 * parity + place_at // PER_HEAD)
+    sub = as_column(sub_ref[...])
     unit = eye(256)
     quad.finish()
     for k in range(2):
@@ -517,9 +549,9 @@
 
     def kv_sends(start):
         def one(o, carry):
-            w = lax.rem(chip + 7 * o, 3 * PER_HEAD)
+            w = lax.rem(chip + 7 * o, WORKERS)
             j = w // PER_HEAD
-            target = 2 * (core * 3 * PER_HEAD + w) + chip % 2
+            target = 2 * worker_chip(core, w) + chip % 2
             if start:
 
                 @pl.when(target == s)
@@ -536,9 +568,10 @@
 
             return carry
 
-        lax.fori_loop(0, 3 * PER_HEAD, one, 0)
+        lax.fori_loop(0, WORKERS, one, 0)
 
     kv_sends(True)
+    saves = pieces_out(nbuf, normed_ref, osem, 5, 4)
     loads[2].wait()
     value = matmul(nbuf[...], wbuf[2]).astype(BF)
     for j in range(3):
@@ -562,15 +595,6 @@
             largest = jnp.sum(square[64 * m : 64 * m + 64], axis=0, keepdims=True)
             peaks[m : m + 1, :] = jnp.maximum(peaks[m : m + 1, :], largest)
 
-    def gathers():
-        def piece(p):
-            return nbuf.at[:, pl.ds(pl.multiple_of(p * 384, 128), 384)]
-
-        return [
-            RingGather(piece, xnormed_ref, *sems[:2], "x", chip, core, t),
-            RingGather(piece, znormed_ref, *sems[2:], "z", chip, core, t),
-        ]
-
     @pl.when(served)
     def _():
         peaks[...] = jnp.zeros_like(peaks)
@@ -596,11 +620,8 @@
             kmax[m] = jnp.max(peaks[m : m + 1, :])
 
     quad_o.finish()
-    saves = pieces_out(obuf, dout_ref, osem, 0, 2)
+    saves += pieces_out(obuf, dout_ref, osem, 0, 2)
     tile_waits(qsrc, q, qsend, qrecv, chip, core, t)
-    for ring in gathers():
-        ring.start()
-
     def keep():
         return [
             pltpu.make_async_copy(kv, kv_ref, osem.at[2]),
@@ -666,11 +687,8 @@
             parts_ref[r] = parts
             log_ref[r] = bound + jnp.log(whole) * LOG2E
             rms, hat = group_norm(parts, lam)
-            mixed_ref[r] = (hat * sub_ref[...] * OUT_SCALE).T.astype(BF)
-
-    for ring in gathers():
-        ring.finish()
-        ring.drain()
+            mixed_ref[r] = (hat * sub * OUT_SCALE).T.astype(BF)
+
     kv_sends(False)
     tile_sends(qsrc, q, qsend, qrecv, chip, core, t, False)
     quad.drain()
@@ -688,22 +706,21 @@
         keep_early().wait()
 
 
-def forward_part(x, cot, mask, gain, lambdas, sub, wq, wk, wv):
+def forward_part(x, cot, mask, attn, sub, lambdas, wq, wk, wv):
     return pl.pallas_call(
         forward_kernel,
         name="forward",
         out_shape=(
             shape(HALVES, BF),
+            shape(QUARTERS, BF),
             shape((SLOTS, TILE, 128), BF),
             shape(KV, BF),
             shape((SLOTS, TILE, 128), BF),
             shape((SLOTS, 128, 2 * TILE), F32),
             shape((SLOTS, 1, 2 * TILE), F32),
-            shape(GATHERED_Q, BF),
-            shape(GATHERED_Q, BF),
         ),
         in_specs=[VM] * 6 + [ANY] * 3,
-        out_specs=(ANY, ANY, ANY, VM, VM, VM, ANY, ANY),
+        out_specs=(ANY, ANY, ANY, ANY, VM, VM, VM),
         scratch_shapes=[
             pltpu.VMEM((BLOCK, D), BF),
             pltpu.VMEM((BLOCK, D), BF),
@@ -724,36 +741,37 @@
             pltpu.SemaphoreType.DMA((CHIPS // 2,)),
             pltpu.SemaphoreType.DMA((6,)),
             pltpu.SemaphoreType.DMA((SLOTS,)),
-            pltpu.SemaphoreType.DMA((5,)),
-            *(RING_SEMS * 2),
+            pltpu.SemaphoreType.DMA((9,)),
         ],
         compiler_params=pltpu.CompilerParams(
             collective_id=0, has_side_effects=True, vmem_limit_bytes=VMEM_LIMIT
         ),
-    )(x, cot, mask, gain, lambdas, sub, wq, wk, wv)
+    )(x, cot, mask, attn, sub, lambdas, wq, wk, wv)
 
 
 SPAN = 1024
 SPANS = CHIPS * BLOCK // SPAN
 PER_SPAN = SPAN // BLOCK // 2
-EARLY_SPANS = 4
+EARLY_SPANS = 3
 
 
 def middle_kernel(
-    x_ref, cot_ref, mask_ref, gain_ref, lambdas_ref, sub_ref, tiles_ref, wo_ref, wg_ref, wu_ref, wd_ref,
-    dout_ref, q_ref, kv_ref, parts_ref, log_ref,
-    out_ref, dres_ref, gainpart_ref, dqkv_ref, small_ref, gate_ref, up_ref, down_ref,
-    lmix_ref, xdres_ref,
-    land, wo, wg, wu, wd, fbuf, rbuf, dms, dout_all, gu, hid, mix,
+    x_ref, cot_ref, mask_ref, attn_ref, ffn_ref, sub_ref, lambdas_ref, tiles_ref,
+    wq_ref, wk_ref, wv_ref, wo_ref, wg_ref, wu_ref, wd_ref,
+    dout_ref, normed_ref, q_ref, kv_ref, parts_ref, log_ref,
+    out_ref, grad_ref, gq_ref, gk_ref, gv_ref, go_ref, gate_ref, up_ref, down_ref, sums_ref,
+    xnormed_ref, znormed_ref,
+    dres, dqkv_ref, rq, rk, rv, xmix, xdres, pqo, pkv, sqo, skv, swap2, swapped2,
+    vec, vecs, quarter, quarters,
+    land, wo, wg, wu, wd, fbuf, rbuf, dms, dout_all, dgate, dup, hid, mix,
     q, kv, parts_all, logs, dmix,
-    lffn, lgu, lhid, ldout, pgu, pdown, sgu, sdown, swap, swapped,
+    lffn, lgate, lup, lhid, ldout, pgate, pup, pdown, sgate, sup, sdown, swap, swapped,
     k_t, acc, q_cols, q_rows, d_cols, d_rows, deltas, dq_acc, dq_out, given, sib, both, home, *rest,
 ):
     chip, core, t = place()
     s = 2 * chip + core
-    slot = s % 10
-    head = chip // PER_HEAD
-    served = chip < SERVED
+    parity, place_at, slot, served = worker(chip, core)
+    head = 3 * parity + place_at // PER_HEAD
     x_at, z_at = chip % 4, chip // 8
     taken = iter(rest)
 
@@ -762,11 +780,12 @@
 
     reduces = [take(9) for _ in range(2)]
     gather_sems = [take(2) for _ in range(2)]
-    ring_sems = [take(2) for _ in range(5)]
+    ring_sems = [take(2) for _ in range(11)]
     once_sems = take(4)
-    scatter = [take(2) for _ in range(2)]
+    scatter = [take(2) for _ in range(5)]
     wsem, osem, hsend, hrecv, tsend, trecv, swap_sem = take(7)
     dsend, drecv, ksend, krecv, gsend, grecv = take(6)
+    w2sem, lsem, swap2_sem, asem, bsem, csem = take(6)
 
     loads = [
         weight_load(wo_ref, wo, wsem.at[0], core, 384),
@@ -789,13 +808,22 @@
     gather_f = QuadGather(fbuf, *gather_sems[0], chip, core, t)
     gather_r = QuadGather(rbuf, *gather_sems[1], chip, core, t)
     ring_dout = RingGather(lambda p: dout_all.at[p // 2], ldout, *ring_sems[0], "x", chip, core, t)
-    ring_mix = RingGather(lambda p: mix, lmix_ref, *ring_sems[1], "x", chip, core, t)
+    ring_mix = RingGather(lambda p: mix, xmix, *ring_sems[1], "x", chip, core, t)
     ring_hid = RingGather(lambda p: hid.at[p % 2], lhid, *ring_sems[2], "x", chip, core, t)
-    ring_gu = RingGather(lambda p: gu.at[p % 2], lgu, *ring_sems[3], "z", chip, core, t)
+    ring_gate = RingGather(lambda p: dgate.at[p % 2], lgate, *ring_sems[3], "z", chip, core, t)
+    ring_up = RingGather(lambda p: dup.at[p % 2], lup, *ring_sems[10], "z", chip, core, t)
     ring_dres = RingGather(
         lambda p: rbuf.at[:, pl.ds(pl.multiple_of(p * 384, 128), 384)],
-        xdres_ref, *ring_sems[4], "x", chip, core, t,
+        xdres, *ring_sems[4], "x", chip, core, t,
     )
+    ring_xn = RingGather(lambda p: normed_ref.at[p], xnormed_ref, *ring_sems[5], "x", chip, core, t)
+    ring_zn = RingGather(lambda p: normed_ref.at[p], znormed_ref, *ring_sems[6], "z", chip, core, t)
+    ring_q = RingGather(lambda p: dqkv_ref.at[0], rq, *ring_sems[7], "x", chip, core, t)
+    ring_k = RingGather(lambda p: dqkv_ref.at[1], rk, *ring_sems[8], "z", chip, core, t)
+    ring_v = RingGather(lambda p: dqkv_ref.at[2], rv, *ring_sems[9], "z", chip, core, t)
+    send_qo = Scatter(pqo, sqo, *scatter[2], 8, 8 * x_at, chip // 4, chip, core, t)
+    send_kv = Scatter(pkv, skv, *scatter[3], 8, 8 * z_at, chip % 8, chip, core, t)
+    members = ((s + 1 - 2 * core, t), (s, 1 - t), (s + 1 - 2 * core, 1 - t))
     ring_ffn = RingGatherOnce(
         lambda p: fbuf.at[:, pl.ds(pl.multiple_of((p // 2) * 768, 128), 768)],
         lffn, *once_sems, "z", chip, core, t,
@@ -803,15 +831,22 @@
     send_down = Scatter(
         pdown, sdown, *scatter[0], 16, 16 * (x_at // 2), 8 * (x_at % 2) + chip // 4, chip, core, t
     )
-    send_gu = Scatter(
-        pgu, sgu, *scatter[1], 16, 16 * (z_at // 2), 8 * (z_at % 2) + chip % 8, chip, core, t
+    send_gate, send_up = (
+        Scatter(
+            part, to, *sems, 16, 16 * (z_at // 2), 8 * (z_at % 2) + chip % 8, chip, core, t
+        )
+        for part, to, sems in ((pgate, sgate, scatter[1]), (pup, sup, scatter[4]))
     )
     mine = pl.ds(pl.multiple_of(gather_f.mine, ROWS), ROWS)
-    dout = cot_ref[...] * mask_ref[...]
-    lam = lambda_of(lambdas_ref, chip, t)
-    small_ref[...] = jnp.zeros_like(small_ref)
+    dout = cot_ref[...] * mask_column(mask_ref)
+    lam = lambda_of(lambdas_ref, 6 * t + head)
+    sub = as_column(sub_ref[...])
+    ffn_gain = long_row(ffn_ref)
+    vec[...] = jnp.zeros_like(vec)
     greet_all(chip, core, t)
     home_sends(tiles_ref, land, hsend, hrecv, chip, core, t, True)
+    ring_zn.start()
+    ring_xn.start()
     loads[0].wait()
     home_waits(tiles_ref, land, hrecv)
     for j in range(3):
@@ -825,7 +860,7 @@
     resid = x_ref[...] + jnp.concatenate([red.result(k) for k in range(NC)], axis=1)
     ffn_rms = rms_scale(resid)
     ffn_hat = resid * ffn_rms
-    fbuf[mine, :] = (ffn_hat * gain_ref[...]).astype(BF)
+    fbuf[mine, :] = (ffn_hat * ffn_gain).astype(BF)
     gather_f.start()
     for load in loads[1:]:
         load.wait()
@@ -842,34 +877,42 @@
         sig = 1.0 / (1.0 + jnp.exp(-gate))
         silu = gate * sig
         to = pl.ds(pl.multiple_of(at * 256, 256), 256)
-        up_to = pl.ds(pl.multiple_of(512 + at * 256, 256), 256)
         hid[b, :, to] = (silu * up).astype(BF)
-        gu[b, :, to] = (d_hidden * up * sig * (1.0 + gate * (1.0 - sig))).astype(BF)
-        gu[b, :, up_to] = (d_hidden * silu).astype(BF)
+        dgate[b, :, to] = (d_hidden * up * sig * (1.0 + gate * (1.0 - sig))).astype(BF)
+        dup[b, :, to] = (d_hidden * silu).astype(BF)
         return carry
 
     lax.fori_loop(0, 4, hidden_step, 0)
+    ring_gate.start()
+    ring_hid.start()
     red2 = QuadReduce(*reduces[0], chip, core, t)
 
     def ffn_term(k):
         rows = slice(k * CW, (k + 1) * CW)
         return (
-            matmul_t(gu[0, :, :512], wg[rows, :512])
-            + matmul_t(gu[1, :, :512], wg[rows, 512:])
-            + matmul_t(gu[0, :, 512:], wu[rows, :512])
-            + matmul_t(gu[1, :, 512:], wu[rows, 512:])
+            matmul_t(dgate[0], wg[rows, :512])
+            + matmul_t(dgate[1], wg[rows, 512:])
+            + matmul_t(dup[0], wu[rows, :512])
+            + matmul_t(dup[1], wu[rows, 512:])
         )
 
     red2.run(ffn_term)
-    ring_hid.start()
-    ring_gu.start()
+    late_loads = [
+        weight_load(ref, buf.at[:, k * 384 : (k + 1) * 384], w2sem.at[i], core, 384)
+        for i, (ref, buf, k) in enumerate(((wq_ref, wg, 0), (wk_ref, wg, 1), (wv_ref, wu, 0)))
+    ]
+    for load in late_loads:
+        load.start()
     red3 = QuadReduce(*reduces[1], chip, core, t)
     d_ffn = jnp.concatenate([red2.result(k) for k in range(NC)], axis=1)
-    gainpart_ref[...] = jnp.sum(d_ffn * ffn_hat, axis=0, keepdims=True)
-    d_resid = dout + norm_back(d_ffn, gain_ref[...], ffn_rms, ffn_hat)
-    dres_ref[...] = d_resid
+    part = jnp.sum(d_ffn * ffn_hat, axis=0, keepdims=True)
+    for k in range(12):
+        vec[12 + k : 13 + k, :] = part[:, k * 128 : (k + 1) * 128]
+    d_resid = dout + norm_back(d_ffn, ffn_gain, ffn_rms, ffn_hat)
+    dres[...] = d_resid
     rbuf[mine, :] = d_resid.astype(BF)
     gather_r.start()
+    ring_ffn.forward()
     red3.run(
         lambda k: matmul_t(hid[0], wd[k * CW : (k + 1) * CW, :512])
         + matmul_t(hid[1], wd[k * CW : (k + 1) * CW, 512:])
@@ -880,7 +923,8 @@
         for u in range(2):
             dms[j, u] = d_mixed[u * 128 : (u + 1) * 128, j * 128 : (j + 1) * 128]
     tile_sends(dms, dmix, tsend, trecv, chip, core, t, True)
-    ring_ffn.forward()
+    ring_up.start()
+    ring_dres.start()
     out_ref[...] = resid + jnp.concatenate([red3.result(k) for k in range(NC)], axis=1)
     for fetch in fetches[1:]:
         fetch.wait()
@@ -890,8 +934,8 @@
         return remote(given.at[at], sib.at[o], dsend.at[at], drecv.at[o], s + 1 - 2 * core, t)
 
     def to_home(o, start):
-        target = 2 * (2 * o + core) + head // 3
-        spot = (head % 3) * PER_HEAD + chip % PER_HEAD
+        target = 2 * (2 * o + core) + parity
+        spot = place_at
         if start:
 
             @pl.when(target == s)
@@ -922,11 +966,22 @@
 
         lax.fori_loop(0, CHIPS * BLOCK // KB, flip, 0)
 
-    tile_waits(dms, dmix, tsend, trecv, chip, core, t)
     ring_dout.finish()
     ring_hid.finish()
     block_grad(pdown, 0, ldout, lhid[...].reshape(4 * BLOCK, 512), 256)
+    ring_xn.finish()
+    ring_zn.finish()
+    lefts = [
+        pltpu.make_async_copy(src, ldout.at[:, :, k * 384 : (k + 1) * 384], lsem.at[k])
+        for k, src in enumerate((xnormed_ref, znormed_ref))
+    ]
+    for left in lefts:
+        left.start()
+    tile_waits(dms, dmix, tsend, trecv, chip, core, t)
     send_down.each(True)
+    ring_ffn.finish()
+    ring_gate.finish()
+    block_grad(pgate, 0, lffn, lgate[...].reshape(4 * BLOCK, 512), 256)
 
     for r in range(SLOTS):
 
@@ -943,16 +998,16 @@
             rms, hat = group_norm(parts, lam)
             e_t = dmix[r].astype(F32).T * OUT_SCALE
             column = jnp.sum(e_t * hat, axis=1, keepdims=True)
-            d_differ = norm_back(e_t, sub_ref[...], rms, hat, 0).astype(BF)
+            d_differ = norm_back(e_t, sub, rms, hat, 0).astype(BF)
             d_wide = d_differ.astype(F32)
             d_cols[r] = d_differ
             d_rows[r] = d_wide.T.astype(BF)
             second_dot = jnp.sum(d_wide * second, axis=0, keepdims=True)
             row = lax.broadcasted_iota(jnp.int32, (128, 128), 0)
             lane = lax.broadcasted_iota(jnp.int32, (128, 128), 1)
-            small_ref[0:1, :] += jnp.sum(jnp.where(row == lane, column, 0.0), axis=0, keepdims=True)
+            vec[24:25, :] += jnp.sum(jnp.where(row == lane, column, 0.0), axis=0, keepdims=True)
             here = lax.broadcasted_iota(jnp.int32, (1, 128), 1) == 6 * t + head
-            small_ref[1:2, :] -= jnp.where(here, jnp.sum(second_dot, axis=1, keepdims=True), 0.0)
+            vec[25:26, :] -= jnp.where(here, jnp.sum(second_dot, axis=1, keepdims=True), 0.0)
             deltas[r, 0:1, :] = jnp.sum(d_wide * first, axis=0, keepdims=True)
             deltas[r, 1:2, :] = -lam * second_dot
             dq_acc[r] = jnp.zeros((128, 2 * TILE), F32)
@@ -1023,19 +1078,43 @@
 
         return carry
 
+    def early(k, carry):
+        span(k, carry)
+
+        @pl.when(k < 2)
+        def _():
+            send_gate.some(8 * k, 8 * k + 8, True)
+
+        return carry
+
+    def late(k, carry):
+        span(k, carry)
+
+        @pl.when(k < EARLY_SPANS + 4)
+        def _():
+            at = 4 * (k - EARLY_SPANS)
+            send_up.some(at, at + 4, True)
+
+        return carry
+
     @pl.when(served)
     def _():
-        lax.fori_loop(0, EARLY_SPANS, span, 0)
-
-    ring_ffn.finish()
-    ring_gu.finish()
-    block_grad(pgu, 0, lffn, lgu[:, :, :512].reshape(4 * BLOCK, 512), 256)
-    block_grad(pgu, 512, lffn, lgu[:, :, 512:].reshape(4 * BLOCK, 512), 256)
-    send_gu.each(True)
+        lax.fori_loop(0, EARLY_SPANS, early, 0)
+
+    @pl.when(jnp.logical_not(served))
+    def _():
+        send_gate.each(True)
+
+    ring_up.finish()
+    block_grad(pup, 0, lffn, lup[...].reshape(4 * BLOCK, 512), 256)
+
+    @pl.when(jnp.logical_not(served))
+    def _():
+        send_up.each(True)
 
     @pl.when(served)
     def _():
-        lax.fori_loop(EARLY_SPANS, SPANS, span, 0)
+        lax.fori_loop(EARLY_SPANS, SPANS, late, 0)
         pass_on(SPANS - 1)
 
     for r in range(SLOTS):
@@ -1046,16 +1125,11 @@
             dq_out[r] = (dq_t * 0.125).T.astype(BF)
 
     home_sends(dq_out, land, gsend, grecv, chip, core, t, True)
-    ring_dres.start()
-    send_down.wait()
-    for b in range(2):
-        total = send_down.total(b, slice(0, 512))
-        for h in range(2):
-            swap[h, :, 2048 + b * 512 : 2560 + b * 512] = total[h * 24 : h * 24 + 24]
     home_waits(dq_out, land, grecv)
     for j in range(3):
         for u in range(2):
             dqkv_ref[0, u * 128 : (u + 1) * 128, j * 128 : (j + 1) * 128] = land[j, u]
+    ring_q.start()
     for j in range(3):
         total = jnp.zeros((BLOCK, 256), F32)
         for p in range(PER_HEAD):
@@ -1064,30 +1138,128 @@
             total = total + home[spot].astype(F32)
         dqkv_ref[1, :, j * 128 : (j + 1) * 128] = total[:, :128].astype(BF)
         dqkv_ref[2, :, j * 128 : (j + 1) * 128] = total[:, 128:].astype(BF)
-    send_gu.wait()
+    ring_k.start()
+    ring_v.start()
+
+    for load in late_loads:
+        load.wait()
+    red2.drain()
+    red4 = QuadReduce(*reduces[0], chip, core, t)
+
+    def normed_term(k):
+        rows = slice(k * CW, (k + 1) * CW)
+        return (
+            matmul_t(dqkv_ref[0], wg[rows, :384])
+            + matmul_t(dqkv_ref[1], wg[rows, 384:768])
+            + matmul_t(dqkv_ref[2], wu[rows, :384])
+        )
+
+    red4.run(normed_term)
+    ring_mix.finish()
+    ring_dres.finish()
+    block_grad(pqo, 384, xdres, xmix[...].reshape(4 * BLOCK, 384), 384, 0, 384)
+    x = x_ref[...]
+    rms = rms_scale(x)
+    hat = x * rms
+    d_normed = jnp.concatenate([red4.result(k) for k in range(NC)], axis=1)
+    part = jnp.sum(d_normed * hat, axis=0, keepdims=True)
+    for k in range(12):
+        vec[k : k + 1, :] = part[:, k * 128 : (k + 1) * 128]
+    first_sum = [
+        remote(vec, vecs.at[k], asem.at[0, k], asem.at[1, k], *member)
+        for k, member in enumerate(members)
+    ]
+    for cp in first_sum:
+        cp.start()
+    grad_ref[...] = dres[...] + norm_back(d_normed, long_row(attn_ref), rms, hat)
+    for left in lefts:
+        left.wait()
+    ring_q.finish()
+    block_grad(pqo, 0, ldout, rq[...].reshape(4 * BLOCK, 384), 384, 0, 384)
+    send_qo.each(True)
+    ring_k.finish()
+    block_grad(pkv, 0, ldout, rk[...].reshape(4 * BLOCK, 384), 384, 384, 384)
+    ring_v.finish()
+    block_grad(pkv, 384, ldout, rv[...].reshape(4 * BLOCK, 384), 384, 384, 384)
+    send_kv.each(True)
+    for cp in first_sum:
+        cp.wait_recv()
+    share = pl.ds(pl.multiple_of((2 * core + t) * 8, 8), 8)
+    quarter[...] = (vec[share, :] + vecs[0, share, :]) + (vecs[1, share, :] + vecs[2, share, :])
+
+    def spread(k, start):
+        to = 2 * lax.rem(chip + k, CHIPS) + core
+        cp = remote(quarter, quarters.at[chip], bsem.at[0, k], bsem.at[1, chip], to, t)
+        if start:
+            cp.start()
+        else:
+            cp.wait_send()
+
+    def spread_start(k, carry):
+        spread(k, True)
+        return carry
+
+    def spread_end(k, carry):
+        spread(k, False)
+        return carry
+
+    own = pltpu.make_async_copy(quarter, quarters.at[chip], bsem.at[1, chip])
+    own.start()
+    lax.fori_loop(1, CHIPS, spread_start, 0)
+
+    send_down.wait()
     for b in range(2):
-        for m in range(2):
-            total = send_gu.total(b, slice(m * 512, m * 512 + 512))
+        total = send_down.total(b, slice(0, 512))
+        for h in range(2):
+            swap[h, :, 2048 + b * 512 : 2560 + b * 512] = total[h * 24 : h * 24 + 24]
+    for m, send in enumerate((send_gate, send_up)):
+        send.wait()
+        for b in range(2):
+            total = send.total(b, slice(0, 512))
             at = m * 1024 + b * 512
             for h in range(2):
                 swap[h, :, at : at + 512] = total[h * 24 : h * 24 + 24]
-    swap_copy = remote(
-        swap.at[1 - core], swapped, swap_sem.at[0], swap_sem.at[1], s + 1 - 2 * core, t
-    )
+    sibling = s + 1 - 2 * core
+    swap_copy = remote(swap.at[1 - core], swapped, swap_sem.at[0], swap_sem.at[1], sibling, t)
     swap_copy.start()
-    ring_mix.finish()
-    ring_dres.finish()
-    for ring in (ring_dout, ring_mix, ring_hid, ring_gu, ring_dres, ring_ffn):
+
+    def collect(k, total):
+        pltpu.make_async_copy(quarter, quarters.at[k], bsem.at[1, k]).wait()
+        return total + quarters[k]
+
+    sums_ref[share, :] = lax.fori_loop(0, CHIPS, collect, jnp.zeros((8, 128), F32))
+    last_sum = [
+        remote(sums_ref.at[share], sums_ref.at[share], csem.at[0, k], csem.at[1, k], *member)
+        for k, member in enumerate(members)
+    ]
+    for cp in last_sum:
+        cp.start()
+    for send, first in ((send_qo, (0, 3)), (send_kv, (1, 2))):
+        send.wait()
+        for m in range(2):
+            total = send.total(0, slice(m * 384, m * 384 + 384))
+            at = first[m] * 384
+            for h in range(2):
+                swap2[h, :, at : at + 384] = total[h * 24 : h * 24 + 24]
+    swap2_copy = remote(swap2.at[1 - core], swapped2, swap2_sem.at[0], swap2_sem.at[1], sibling, t)
+    swap2_copy.start()
+    swap_copy.wait()
+    swap_out(swap, swapped, ((gate_ref, 0), (up_ref, 1024), (down_ref, 2048)), 1024, core)
+
+    for ring in (
+        ring_dout, ring_mix, ring_hid, ring_gate, ring_up, ring_dres, ring_ffn, ring_xn, ring_zn, ring_q, ring_k,
+        ring_v,
+    ):
         ring.drain()
-    send_gu.each(False)
-    send_down.each(False)
+    for send in (send_gate, send_up, send_down, send_qo, send_kv):
+        send.each(False)
     home_sends(tiles_ref, land, hsend, hrecv, chip, core, t, False)
     home_sends(dq_out, land, gsend, grecv, chip, core, t, False)
     tile_sends(dms, dmix, tsend, trecv, chip, core, t, False)
     for gather in (gather_f, gather_r):
         gather.drain()
-    red2.drain()
     red3.drain()
+    red4.drain()
 
     @pl.when(served)
     def _():
@@ -1101,8 +1273,14 @@
 
         lax.fori_loop(0, CHIPS // 2, last, 0)
 
-    swap_copy.wait()
-    swap_out(swap, swapped, ((gate_ref, 0), (up_ref, 1024), (down_ref, 2048)), 1024, core)
+    for cp in last_sum:
+        cp.wait()
+    for cp in first_sum:
+        cp.wait_send()
+    lax.fori_loop(1, CHIPS, spread_end, 0)
+    swap2_copy.wait()
+    outs = ((gq_ref, 0), (gk_ref, 384), (gv_ref, 768), (go_ref, 1152))
+    swap_out(swap2, swapped2, outs, 384, core)
 
 
 def swap_out(swap, swapped, outs, width, core):
@@ -1118,7 +1296,8 @@
 
 
 def middle_part(
-    x, cot, mask, gain, lambdas, sub, tiles, wo, wg, wu, wd, dout_all, q, kv, parts, logs
+    x, cot, mask, attn, ffn, sub, lambdas, tiles, wq, wk, wv, wo, wg, wu, wd,
+    dout_all, normed, q, kv, parts, logs,
 ):
     half = (CHIPS // 2, BLOCK, 256)
     vm = pltpu.VMEM
@@ -1129,18 +1308,28 @@
         out_shape=(
             shape((ROWS, D), F32),
             shape((ROWS, D), F32),
-            shape((1, D), F32),
-            shape((3, BLOCK, 384), BF),
-            shape((2, 128), F32),
-            shape((24, 2048), F32),
-            shape((24, 2048), F32),
-            shape((24, 2048), F32),
+            *([shape((24, 768), F32)] * 4),
+            *([shape((24, 2048), F32)] * 3),
+            shape((32, 128), F32),
             shape(GATHERED_Q, BF),
             shape(GATHERED_Q, BF),
         ),
-        in_specs=[VM] * 6 + [ANY] * 10,
-        out_specs=(VM,) * 8 + (ANY,) * 2,
+        in_specs=[VM] * 7 + [ANY] * 14,
+        out_specs=(VM,) * 10 + (ANY,) * 2,
         scratch_shapes=[
+            vm((ROWS, D), F32),
+            vm((3, BLOCK, 384), BF),
+            *([vm(GATHERED_Q, BF)] * 5),
+            vm((384, 768), BF),
+            vm((384, 768), BF),
+            vm((8, CHUNK, 768), BF),
+            vm((8, CHUNK, 768), BF),
+            vm((2, 24, 1536), F32),
+            vm((24, 1536), F32),
+            vm((32, 128), F32),
+            vm((3, 32, 128), F32),
+            vm((8, 128), F32),
+            vm((CHIPS, 8, 128), F32),
             vm((3, 2, TILE, 128), BF),
             vm((D, 384), BF),
             vm((D, 1024), BF),
@@ -1150,7 +1339,8 @@
             vm((BLOCK, D), BF),
             vm((3, 2, TILE, 128), BF),
             vm(HALVES, BF),
-            vm((2, BLOCK, 1024), BF),
+            vm((2, BLOCK, 512), BF),
+            vm((2, BLOCK, 512), BF),
             vm((2, BLOCK, 512), BF),
             vm((BLOCK, 384), BF),
             vm((SLOTS, TILE, 128), BF),
@@ -1159,13 +1349,10 @@
             vm((SLOTS, 1, 2 * TILE), F32),
             vm((SLOTS, TILE, 128), BF),
             vm(GATHERED, BF),
-            vm((4, BLOCK, 1024), BF),
-            vm((4, BLOCK, 512), BF),
+            *([vm((4, BLOCK, 512), BF)] * 3),
             vm(GATHERED, BF),
-            vm((768, 1024), BF),
-            vm((768, 512), BF),
-            vm((16, CHUNK, 1024), BF),
-            vm((16, CHUNK, 512), BF),
+            *([vm((768, 512), BF)] * 3),
+            *([vm((16, CHUNK, 512), BF)] * 3),
             vm((2, 24, 3072), F32),
             vm((24, 3072), F32),
             vm((128, CHIPS * BLOCK), BF),
@@ -1183,9 +1370,10 @@
             vm((3 * PER_HEAD, BLOCK, 256), BF),
             *(REDUCE_SCRATCH * 2),
             *(GATHER_SEMS * 2),
-            *(RING_SEMS * 5),
+            *(RING_SEMS * 11),
             *ONCE_SEMS,
-            *scatter_sems(16),
+            *(scatter_sems(16) * 2),
+            *(scatter_sems(8) * 2),
             *scatter_sems(16),
             sem((4,)),
             sem((9,)),
@@ -1200,247 +1388,71 @@
             sem((3 * PER_HEAD,)),
             sem((SLOTS,)),
             sem((3, 2)),
+            sem((3,)),
+            sem((2,)),
+            sem((2,)),
+            sem((2, 3)),
+            sem((2, CHIPS)),
+            sem((2, 3)),
         ],
         compiler_params=pltpu.CompilerParams(
             collective_id=1, has_side_effects=True, vmem_limit_bytes=VMEM_LIMIT
         ),
-    )(x, cot, mask, gain, lambdas, sub, tiles, wo, wg, wu, wd, dout_all, q, kv, parts, logs)
-
-
-def finish_kernel(
-    x_ref, gain_ref, dres_ref, dqkv_ref, wq_ref, wk_ref, wv_ref,
-    xnormed_ref, znormed_ref, xdres_ref, xmix_ref, ffnpart_ref, small_ref,
-    grad_ref, gq_ref, gk_ref, gv_ref, go_ref, sums_ref,
-    wbuf, xnormed, znormed, xdres, xmix, rq, rk, rv, pqo, pkv, sqo, skv, swap, swapped,
-    vec, vecs, quarter, quarters, *rest,
-):
-    chip, core, t = place()
-    s = 2 * chip + core
-    x, z = chip % 4, chip // 8
-    reduce = rest[:9]
-    wsem, lsem = rest[9:11]
-    rings = [
-        RingGather(lambda p, k=k: dqkv_ref.at[k], land, *sems, axis, chip, core, t)
-        for k, land, sems, axis in (
-            (1, rk, rest[11:13], "z"), (0, rq, rest[13:15], "x"), (2, rv, rest[15:17], "z")
-        )
-    ]
-    send_qo = Scatter(pqo, sqo, *rest[17:19], 8, 8 * x, chip // 4, chip, core, t)
-    send_kv = Scatter(pkv, skv, *rest[19:21], 8, 8 * z, chip % 8, chip, core, t)
-    swap_sem, asem, bsem, csem = rest[21:]
-    loads = [
-        weight_load(ref, wbuf.at[k], wsem.at[k], core, 384)
-        for k, ref in enumerate((wq_ref, wk_ref, wv_ref))
-    ]
-    lefts = [
-        pltpu.make_async_copy(src, dst, lsem.at[k])
-        for k, (src, dst) in enumerate(
-            ((xdres_ref, xdres), (xmix_ref, xmix), (xnormed_ref, xnormed), (znormed_ref, znormed))
-        )
-    ]
-    for load in loads + lefts:
-        load.start()
-    greet_all(chip, core, t)
-    for ring in rings:
-        ring.start()
-    for load in loads:
-        load.wait()
-    red = QuadReduce(*reduce, chip, core, t)
-
-    def term(k):
-        rows = slice(k * CW, (k + 1) * CW)
-        return (
-            matmul_t(dqkv_ref[0], wbuf[0, rows, :])
-            + matmul_t(dqkv_ref[1], wbuf[1, rows, :])
-            + matmul_t(dqkv_ref[2], wbuf[2, rows, :])
-        )
-
-    red.run(term)
-    for left in lefts:
-        left.wait()
-    block_grad(pqo, 384, xdres, xmix[...].reshape(4 * BLOCK, 384), 384)
-    x = x_ref[...]
-    rms = rms_scale(x)
-    hat = x * rms
-    d_normed = jnp.concatenate([red.result(k) for k in range(NC)], axis=1)
-    part = jnp.sum(d_normed * hat, axis=0, keepdims=True)
-    vec[...] = jnp.zeros_like(vec)
-    for k in range(12):
-        vec[k : k + 1, :] = part[:, k * 128 : (k + 1) * 128]
-        vec[12 + k : 13 + k, :] = ffnpart_ref[:, k * 128 : (k + 1) * 128]
-    vec[24:26, :] = small_ref[...]
-    members = ((s + 1 - 2 * core, t), (s, 1 - t), (s + 1 - 2 * core, 1 - t))
-    first_sum = [
-        remote(vec, vecs.at[k], asem.at[0, k], asem.at[1, k], *member)
-        for k, member in enumerate(members)
-    ]
-    for cp in first_sum:
-        cp.start()
-    grad_ref[...] = dres_ref[...] + norm_back(d_normed, gain_ref[...], rms, hat)
-    for cp in first_sum:
-        cp.wait_recv()
-    share = pl.ds(pl.multiple_of((2 * core + t) * 8, 8), 8)
-    quarter[...] = (vec[share, :] + vecs[0, share, :]) + (vecs[1, share, :] + vecs[2, share, :])
-
-    def spread(k, start):
-        to = 2 * lax.rem(chip + k, CHIPS) + core
-        cp = remote(quarter, quarters.at[chip], bsem.at[0, k], bsem.at[1, chip], to, t)
-        if start:
-            cp.start()
-        else:
-            cp.wait_send()
-
-    def spread_start(k, carry):
-        spread(k, True)
-        return carry
-
-    def spread_end(k, carry):
-        spread(k, False)
-        return carry
-
-    own = pltpu.make_async_copy(quarter, quarters.at[chip], bsem.at[1, chip])
-    own.start()
-    lax.fori_loop(1, CHIPS, spread_start, 0)
-    rings[1].finish()
-    block_grad(pqo, 0, xnormed, rq[...].reshape(4 * BLOCK, 384), 384)
-    send_qo.each(True)
-    rings[0].finish()
-    block_grad(pkv, 0, znormed, rk[...].reshape(4 * BLOCK, 384), 384)
-    rings[2].finish()
-    block_grad(pkv, 384, znormed, rv[...].reshape(4 * BLOCK, 384), 384)
-    send_kv.each(True)
-
-    def collect(k, total):
-        pltpu.make_async_copy(quarter, quarters.at[k], bsem.at[1, k]).wait()
-        return total + quarters[k]
-
-    sums_ref[share, :] = lax.fori_loop(0, CHIPS, collect, jnp.zeros((8, 128), F32))
-    last_sum = [
-        remote(sums_ref.at[share], sums_ref.at[share], csem.at[0, k], csem.at[1, k], *member)
-        for k, member in enumerate(members)
-    ]
-    for cp in last_sum:
-        cp.start()
-    for send, first in ((send_qo, (0, 3)), (send_kv, (1, 2))):
-        send.wait()
-        for m in range(2):
-            total = send.total(0, slice(m * 384, m * 384 + 384))
-            at = first[m] * 384
-            for h in range(2):
-                swap[h, :, at : at + 384] = total[h * 24 : h * 24 + 24]
-    swap_copy = remote(
-        swap.at[1 - core], swapped, swap_sem.at[0], swap_sem.at[1], s + 1 - 2 * core, t
+    )(
+        x, cot, mask, attn, ffn, sub, lambdas, tiles, wq, wk, wv, wo, wg, wu, wd,
+        dout_all, normed, q, kv, parts, logs,
     )
-    swap_copy.start()
-    for cp in last_sum:
-        cp.wait()
-    for cp in first_sum:
-        cp.wait_send()
-    lax.fori_loop(1, CHIPS, spread_end, 0)
-    send_qo.each(False)
-    send_kv.each(False)
-    for ring in rings:
-        ring.drain()
-    red.drain()
-    swap_copy.wait()
-    outs = ((gq_ref, 0), (gk_ref, 384), (gv_ref, 768), (go_ref, 1152))
-    swap_out(swap, swapped, outs, 384, core)
-
-
-def finish(x, gain, dres, dqkv, wq, wk, wv, xnormed, znormed, xdres, xmix, ffn_part, small):
-    return pl.pallas_call(
-        finish_kernel,
-        name="finish",
-        out_shape=(shape((ROWS, D), F32),) + (shape((24, 768), F32),) * 4 + (shape((32, 128), F32),),
-        in_specs=[VM] * 4 + [ANY] * 7 + [VM] * 2,
-        out_specs=(VM,) * 6,
-        scratch_shapes=[
-            pltpu.VMEM((3, D, 384), BF),
-            *([pltpu.VMEM(GATHERED_Q, BF)] * 7),
-            pltpu.VMEM((384, 768), BF),
-            pltpu.VMEM((384, 768), BF),
-            pltpu.VMEM((8, CHUNK, 768), BF),
-            pltpu.VMEM((8, CHUNK, 768), BF),
-            pltpu.VMEM((2, 24, 1536), F32),
-            pltpu.VMEM((24, 1536), F32),
-            pltpu.VMEM((32, 128), F32),
-            pltpu.VMEM((3, 32, 128), F32),
-            pltpu.VMEM((8, 128), F32),
-            pltpu.VMEM((CHIPS, 8, 128), F32),
-            *REDUCE_SCRATCH,
-            pltpu.SemaphoreType.DMA((3,)),
-            pltpu.SemaphoreType.DMA((4,)),
-            *(RING_SEMS * 3),
-            *scatter_sems(8),
-            *scatter_sems(8),
-            pltpu.SemaphoreType.DMA((2,)),
-            pltpu.SemaphoreType.DMA((2, 3)),
-            pltpu.SemaphoreType.DMA((2, CHIPS)),
-            pltpu.SemaphoreType.DMA((2, 3)),
-        ],
-        compiler_params=pltpu.CompilerParams(
-            collective_id=2, has_side_effects=True, vmem_limit_bytes=VMEM_LIMIT
-        ),
-    )(x, gain, dres, dqkv, wq, wk, wv, xnormed, znormed, xdres, xmix, ffn_part, small)
-
-
-def publish(*arrays):
+
+
+def publish(lambdas, sums, arrays):
     count = len(arrays)
 
-    def kernel(*refs):
+    def kernel(lambdas_ref, sums_ref, *refs):
         for k in range(count):
             refs[count + k][...] = refs[k][...]
+        attn_ref, ffn_ref, sub_ref, grad_ref = refs[2 * count :]
+        attn_ref[...] = sums_ref[0:12, :]
+        ffn_ref[...] = sums_ref[12:24, :]
+        sub_ref[...] = sums_ref[24:25, :]
+        vectors, first, second = lambda_parts(lambdas_ref)
+        d_lam = as_column(sums_ref[25:26, :])[:12, :1]
+        factors = (d_lam * first, d_lam * first, -d_lam * second, -d_lam * second)
+        for k, other in enumerate((1, 0, 3, 2)):
+            grad_ref[:, k, :] = factors[k] * vectors[other]
 
     return pl.pallas_call(
         kernel,
         name="publish",
-        out_shape=tuple(shape(a.shape, a.dtype) for a in arrays),
-        in_specs=[VM] * count,
-        out_specs=(VM,) * count,
-    )(*arrays)
+        out_shape=tuple(shape(a.shape, a.dtype) for a in arrays)
+        + (shape((12, 128), F32), shape((12, 128), F32), shape((1, 128), F32), shape((12, 4, 64), F32)),
+        in_specs=[VM] * (count + 2),
+        out_specs=(VM,) * (count + 4),
+    )(lambdas, sums, *arrays)
 
 
 def on_device(
     hidden_in, cotangent, needle_mask, attn_gain, lambdas, subln_gain, ffn_gain,
     weight_query, weight_key, weight_value, weight_out, weight_gate, weight_up, weight_down,
 ):
-    attn_row = attn_gain.reshape(1, D)
-    ffn_row = ffn_gain.reshape(1, D)
-    sub_col = subln_gain.reshape(128, 1)
-    mask = needle_mask.astype(F32).reshape(ROWS, 1)
-
-    dout, q, kv, mixed, parts, logs, xnormed, znormed = forward_part(
-        hidden_in, cotangent, mask, attn_row, lambdas, sub_col, weight_query, weight_key, weight_value
+    mask = needle_mask.reshape(1, ROWS)
+    attn = attn_gain.reshape(12, 128)
+    sub = subln_gain.reshape(1, 128)
+    by_head = jnp.transpose(lambdas, (1, 0, 2))
+    dout, normed, q, kv, mixed, parts, logs = forward_part(
+        hidden_in, cotangent, mask, attn, sub, by_head, weight_query, weight_key, weight_value
     )
-    output, d_resid, ffn_part, dqkv, small, grad_gate, grad_up, grad_down, xmix, xdres = middle_part(
-        hidden_in, cotangent, mask, ffn_row, lambdas, sub_col, mixed,
-        weight_out, weight_gate, weight_up, weight_down, dout, q, kv, parts, logs,
+    *results, sums, _, _ = middle_part(
+        hidden_in, cotangent, mask, attn, ffn_gain.reshape(12, 128), sub, by_head, mixed,
+        weight_query, weight_key, weight_value, weight_out, weight_gate, weight_up, weight_down,
+        dout, normed, q, kv, parts, logs,
     )
-    grad_input, grad_query, grad_key, grad_value, grad_out, sums = finish(
-        hidden_in, attn_row, d_resid, dqkv, weight_query, weight_key, weight_value,
-        xnormed, znormed, xdres, xmix, ffn_part, small,
-    )
-    first_exp = jnp.exp(jnp.sum(lambdas[0] * lambdas[1], axis=-1))
-    second_exp = jnp.exp(jnp.sum(lambdas[2] * lambdas[3], axis=-1))
-    d_first = sums[25, :12] * first_exp
-    d_second = -sums[25, :12] * second_exp
-    grad_lambdas = jnp.stack(
-        [
-            d_first[:, None] * lambdas[1],
-            d_first[:, None] * lambdas[0],
-            d_second[:, None] * lambdas[3],
-            d_second[:, None] * lambdas[2],
-        ]
-    )
-    results = publish(
-        output, grad_input, grad_query, grad_key, grad_value, grad_out, grad_gate, grad_up, grad_down
-    )
+    *results, attn_grad, ffn_grad, sub_grad, lambda_grad = publish(by_head, sums, results)
     return (
         *results,
-        sums[:12].reshape(D),
-        grad_lambdas,
-        sums[24],
-        sums[12:24].reshape(D),
+        attn_grad.reshape(D),
+        jnp.transpose(lambda_grad, (1, 0, 2)),
+        sub_grad.reshape(128),
+        ffn_grad.reshape(D),
     )
 
 

time: 285 us -> 246 us (0.86)
  Pallas kernels: 270 us -> 241 us
  local copies, waits for them, and re-layouts: 7.92 us -> 0 us
    pallas_call x1 -> x0, Pallas kernels: 47.5 us -> none  [finish(): pl.pallas_call(finish_kernel, name='finish', out_shape=(shape((ROWS, D),...]
    pallas_call x1, Pallas kernels: 148 us -> 172 us  [middle_part(): pl.pallas_call(middle_kernel, name='middle', out_shape=(shape((ROWS, D),...]
    pallas_call x1, Pallas kernels: 72.5 us -> 66.7 us  [forward_part(): pl.pallas_call(forward_kernel, name='forward', out_shape=(shape(HALVES, B...]
    reshape x5 -> x0, local copies, waits for them, and re-layouts: 5.38 us -> none  [the longest x1 1.4 us: on_device(): sub_col = subln_gain.reshape(128, 1)]
where the time goes in v4:
time: 246 us; the launch traced here: 242 us
  Pallas kernels  241 us (98%)
    pallas_call x1, Pallas kernels, middle_part(): pl.pallas_call(middle_kernel, name='middle', out_shape=(shape((ROWS, D),...  172 us
    pallas_call x1, Pallas kernels, forward_part(): pl.pallas_call(forward_kernel, name='forward', out_shape=(shape(HALVES, B...  66.7 us

profile of v4, /device:TPU:31, one launch (start us, length us, event | category | flops | bytes accessed | tf_op | source)
XLA Modules:
  0.0 242.0 jit_solution(10003036825841731832)
XLA Ops:
  0.6 66.7 %forward.1 = (bf16[2,256,768]{2,1,0:T(8,128)(2,1)}, bf16[4,256,384]{2,1,0:T(8,128)(2,1)}, bf16[7,128,128]{2,1,0:T(8,128)(2,1)}, bf16[32,256,256]{2,1,0:T(8,128)(...) custom-call(f32[64,1536]{1,0:T(8,128)} %x_ref.3, f32[64,1536]{1,0:T(8,128)} %cot_ref.3, ...), custom_call_target="tpu_custom_call" | custom-call | tf_op jit(solution)/shard_map/forward/pallas_call | solution.py:710
  67.3 171.8 %middle.1 = (f32[64,1536]{1,0:T(8,128)}, f32[64,1536]{1,0:T(8,128)}, f32[24,768]{1,0:T(8,128)}, f32[24,768]{1,0:T(8,128)}, f32[24,768]{1,0:T(8,128)}, /*index=5*...) custom-call(f32[64,1536]{1,0:T(8,128)} %x_ref.3, ...), custom_call_target="tpu_custom_call" | custom-call | tf_op jit(solution)/shard_map/middle/pallas_call | solution.py:1305
  239.1 2.7 %publish.1 = (f32[64,1536]{1,0:T(8,128)}, f32[64,1536]{1,0:T(8,128)}, f32[24,768]{1,0:T(8,128)}, f32[24,768]{1,0:T(8,128)}, f32[24,768]{1,0:T(8,128)}, /*index=5...) custom-call(f32[12,4,64]{2,1,0:T(4,128)} %bitcast.11, ...), custom_call_target="tpu_custom_call" | custom-call | tf_op jit(solution)/shard_map/publish/pallas_call | solution.py:1423

commit v5 on v4

--- a/solution.py
+++ b/solution.py
@@ -433,19 +433,6 @@
     )
 
 
-def pieces_out(buf, ref, sem, first, count):
-    width = D // count
-    copies = [
-        pltpu.make_async_copy(
-            buf.at[:, a * width : (a + 1) * width], ref.at[a], sem.at[first + a]
-        )
-        for a in range(count)
-    ]
-    for cp in copies:
-        cp.start()
-    return copies
-
-
 VM = pl.BlockSpec(memory_space=pltpu.VMEM)
 ANY = pl.BlockSpec(memory_space=pl.ANY)
 
@@ -513,39 +500,120 @@
     return jnp.sum(jnp.where(mine, every, 0.0), axis=0, keepdims=True)
 
 
-def forward_kernel(
-    x_ref, cot_ref, mask_ref, attn_ref, sub_ref, lambdas_ref, wq_ref, wk_ref, wv_ref,
-    dout_ref, normed_ref, q_ref, kv_ref, mixed_ref, parts_ref, log_ref,
-    nbuf, obuf, wbuf, kvsrc, qsrc, kv, q, v_t, peaks, kmax, acc, total,
-    wsem, nsend, nrecv, osend, orecv, kvsend, kvrecv, fsend, qsend, qrecv, osem,
+SPAN = 1024
+SPANS = CHIPS * BLOCK // SPAN
+PER_SPAN = SPAN // BLOCK // 2
+EARLY_SPANS = 3
+
+
+def layer_kernel(
+    x_ref, cot_ref, mask_ref, attn_ref, ffn_ref, sub_ref, lambdas_ref,
+    wq_ref, wk_ref, wv_ref, wo_ref, wg_ref, wu_ref, wd_ref,
+    out_ref, grad_ref, gq_ref, gk_ref, gv_ref, go_ref, gate_ref, up_ref, down_ref, sums_ref,
+    xnormed_ref, znormed_ref,
+    dres, dqkv_ref, rq, rk, rv, xmix, xdres, pqo, pkv, sqo, skv, swap2, swapped2,
+    vec, vecs, quarter, quarters,
+    land, wo, wg, wu, wd, fbuf, nbuf, dms, obuf, dgate, dup, hid, mix,
+    q, kv, parts_all, logs, dmix,
+    lffn, lgate, lup, lhid, ldout, pgate, pup, pdown, sgate, sup, sdown, swap, swapped,
+    turned, acc, q_cols, q_rows, d_cols, d_rows, deltas, dq_acc, dq_out, given, sib, both, home,
+    peaks, kmax, total, *rest,
 ):
     chip, core, t = place()
     s = 2 * chip + core
     parity, place_at, slot, served = worker(chip, core)
+    head = 3 * parity + place_at // PER_HEAD
+    x_at, z_at = chip % 4, chip // 8
+    taken = iter(rest)
+
+    def take(count):
+        return [next(taken) for _ in range(count)]
+
+    reduces = [take(9) for _ in range(2)]
+    gather_sems = [take(2) for _ in range(4)]
+    ring_sems = [take(2) for _ in range(11)]
+    once_sems = take(4)
+    scatter = [take(2) for _ in range(5)]
+    wsem, hsend, hrecv, tsend, trecv, swap_sem = take(6)
+    dsend, drecv, ksend, krecv, gsend, grecv = take(6)
+    w2sem, lsem, swap2_sem, asem, bsem, csem = take(6)
+    kvsend, kvrecv, fsend, qsend, qrecv = take(5)
+    rbuf = nbuf
+    front = dq_acc.at[0]
+
+
+    def halves(ref):
+        return lambda p: ref.at[:, pl.ds(pl.multiple_of(p // 2 * 768, 128), 768)]
+
+    def quarters_of(ref):
+        return lambda p: ref.at[:, pl.ds(pl.multiple_of(p * 384, 128), 384)]
+
+    gather_f = QuadGather(fbuf, *gather_sems[0], chip, core, t)
+    gather_r = QuadGather(rbuf, *gather_sems[1], chip, core, t)
+    ring_dout = RingGather(halves(obuf), ldout, *ring_sems[0], "x", chip, core, t)
+    ring_mix = RingGather(lambda p: mix, xmix, *ring_sems[1], "x", chip, core, t)
+    ring_hid = RingGather(lambda p: hid.at[p % 2], lhid, *ring_sems[2], "x", chip, core, t)
+    ring_gate = RingGather(lambda p: dgate.at[p % 2], lgate, *ring_sems[3], "z", chip, core, t)
+    ring_up = RingGather(lambda p: dup.at[p % 2], lup, *ring_sems[10], "z", chip, core, t)
+    ring_dres = RingGather(
+        quarters_of(rbuf), xdres, *ring_sems[4], "x", chip, core, t,
+    )
+    ring_xn = RingGather(quarters_of(nbuf), xnormed_ref, *ring_sems[5], "x", chip, core, t)
+    ring_zn = RingGather(quarters_of(nbuf), znormed_ref, *ring_sems[6], "z", chip, core, t)
+    ring_q = RingGather(lambda p: dqkv_ref.at[0], rq, *ring_sems[7], "x", chip, core, t)
+    ring_k = RingGather(lambda p: dqkv_ref.at[1], rk, *ring_sems[8], "z", chip, core, t)
+    ring_v = RingGather(lambda p: dqkv_ref.at[2], rv, *ring_sems[9], "z", chip, core, t)
+    send_qo = Scatter(pqo, sqo, *scatter[2], 8, 8 * x_at, chip // 4, chip, core, t)
+    send_kv = Scatter(pkv, skv, *scatter[3], 8, 8 * z_at, chip % 8, chip, core, t)
+    members = ((s + 1 - 2 * core, t), (s, 1 - t), (s + 1 - 2 * core, 1 - t))
+    ring_ffn = RingGatherOnce(
+        halves(fbuf), lffn, *once_sems, "z", chip, core, t,
+    )
+    send_down = Scatter(
+        pdown, sdown, *scatter[0], 16, 16 * (x_at // 2), 8 * (x_at % 2) + chip // 4, chip, core, t
+    )
+    send_gate, send_up = (
+        Scatter(
+            part, to, *sems, 16, 16 * (z_at // 2), 8 * (z_at % 2) + chip % 8, chip, core, t
+        )
+        for part, to, sems in ((pgate, sgate, scatter[1]), (pup, sup, scatter[4]))
+    )
+    first_loads = [
+        weight_load(ref, buf.at[:, k * 384 : (k + 1) * 384], w2sem.at[i], core, 384)
+        for i, (ref, buf, k) in enumerate(((wk_ref, wg, 0), (wv_ref, wg, 1), (wq_ref, wu, 0)))
+    ]
     loads = [
-        weight_load(ref, wbuf.at[k], wsem.at[k], core, 384)
-        for k, ref in enumerate((wk_ref, wv_ref, wq_ref))
+        weight_load(wo_ref, wo, wsem.at[0], core, 384),
+        weight_load(wg_ref, wg, wsem.at[1], core, 1024),
+        weight_load(wu_ref, wu, wsem.at[2], core, 1024),
+        weight_load(wd_ref, wd, wsem.at[3], core, 1024),
     ]
-    for load in loads:
+    for load in first_loads + loads[:1]:
         load.start()
+    quad = QuadGather(nbuf, *gather_sems[2], chip, core, t)
+    quad_o = QuadGather(obuf, *gather_sems[3], chip, core, t)
+    mine = pl.ds(pl.multiple_of(quad.mine, ROWS), ROWS)
     x = x_ref[...]
     normed = (x * rms_scale(x) * long_row(attn_ref)).astype(BF)
-    quad = QuadGather(nbuf, nsend, nrecv, chip, core, t)
-    mine = pl.ds(pl.multiple_of(quad.mine, ROWS), ROWS)
     nbuf[mine, :] = normed
-    quad_o = QuadGather(obuf, osend, orecv, chip, core, t)
     greet_all(chip, core, t)
     quad.start()
-    obuf[mine, :] = (cot_ref[...] * mask_column(mask_ref)).astype(BF)
-    lam = lambda_of(lambdas_ref, 6 * t + 3 * parity + place_at // PER_HEAD)
+    dout = cot_ref[...] * mask_column(mask_ref)
+    obuf[mine, :] = dout.astype(BF)
+    lam = lambda_of(lambdas_ref, 6 * t + head)
     sub = as_column(sub_ref[...])
+    ffn_gain = long_row(ffn_ref)
+    vec[...] = jnp.zeros_like(vec)
     unit = eye(256)
     quad.finish()
     for k in range(2):
-        loads[k].wait()
-        value = matmul(nbuf[...], wbuf[k]).astype(BF)
+        first_loads[k].wait()
+        value = matmul(nbuf[...], wg[:, k * 384 : (k + 1) * 384]).astype(BF)
         for j in range(3):
-            kvsrc[j, :, k * 128 : (k + 1) * 128] = value[:, j * 128 : (j + 1) * 128]
+            dqkv_ref[j, :, k * 128 : (k + 1) * 128] = value[:, j * 128 : (j + 1) * 128]
+
+    def kv_piece(j):
+        return dqkv_ref.at[j, :, :256]
 
     def kv_sends(start):
         def one(o, carry):
@@ -556,11 +624,11 @@
 
                 @pl.when(target == s)
                 def _():
-                    pltpu.make_async_copy(kvsrc.at[j], kv.at[chip], kvrecv.at[chip]).start()
+                    pltpu.make_async_copy(kv_piece(j), kv.at[chip], kvrecv.at[chip]).start()
 
             @pl.when(target != s)
             def _():
-                cp = remote(kvsrc.at[j], kv.at[chip], kvsend.at[w], kvrecv.at[chip], target, t)
+                cp = remote(kv_piece(j), kv.at[chip], kvsend.at[w], kvrecv.at[chip], target, t)
                 if start:
                     cp.start()
                 else:
@@ -571,14 +639,15 @@
         lax.fori_loop(0, WORKERS, one, 0)
 
     kv_sends(True)
-    saves = pieces_out(nbuf, normed_ref, osem, 5, 4)
-    loads[2].wait()
-    value = matmul(nbuf[...], wbuf[2]).astype(BF)
+    first_loads[2].wait()
+    value = matmul(nbuf[...], wu[:, :384]).astype(BF)
     for j in range(3):
         for u in range(2):
-            qsrc[j, u] = value[u * 128 : (u + 1) * 128, j * 128 : (j + 1) * 128]
-    tile_sends(qsrc, q, qsend, qrecv, chip, core, t, True)
+            dms[j, u] = value[u * 128 : (u + 1) * 128, j * 128 : (j + 1) * 128]
+    tile_sends(dms, q, qsend, qrecv, chip, core, t, True)
     quad_o.start()
+    for load in loads[1:]:
+        load.start()
 
     def forward(o):
         source = lax.rem((chip // 2 + o) * 2 + core, CHIPS)
@@ -588,9 +657,9 @@
     def turn(source):
         block = kv[source]
         at = pl.ds(pl.multiple_of(source * BLOCK, BLOCK), BLOCK)
-        turned = matmul_t(unit, block)
-        v_t[:, at] = turned[128:].astype(BF)
-        square = turned[:128] * turned[:128]
+        both_t = matmul_t(unit, block)
+        turned[:, at] = both_t[128:].astype(BF)
+        square = both_t[:128] * both_t[:128]
         for m in range(2):
             largest = jnp.sum(square[64 * m : 64 * m + 64], axis=0, keepdims=True)
             peaks[m : m + 1, :] = jnp.maximum(peaks[m : m + 1, :], largest)
@@ -601,7 +670,7 @@
 
         def take(o, carry):
             source, cp = forward(o)
-            pltpu.make_async_copy(kvsrc.at[0], kv.at[source], kvrecv.at[source]).wait()
+            pltpu.make_async_copy(kv_piece(0), kv.at[source], kvrecv.at[source]).wait()
             cp.start()
             turn(source)
             return carry
@@ -610,7 +679,7 @@
 
         def finish(o, carry):
             source = lax.rem((chip // 2 + o) * 2 + 1 - core, CHIPS)
-            pltpu.make_async_copy(kvsrc.at[0], kv.at[source], kvrecv.at[source]).wait()
+            pltpu.make_async_copy(kv_piece(0), kv.at[source], kvrecv.at[source]).wait()
             forward(o)[1].wait_send()
             turn(source)
             return carry
@@ -620,25 +689,9 @@
             kmax[m] = jnp.max(peaks[m : m + 1, :])
 
     quad_o.finish()
-    saves += pieces_out(obuf, dout_ref, osem, 0, 2)
-    tile_waits(qsrc, q, qsend, qrecv, chip, core, t)
-    def keep():
-        return [
-            pltpu.make_async_copy(kv, kv_ref, osem.at[2]),
-            pltpu.make_async_copy(q.at[pl.ds(1, SLOTS - 1)], q_ref.at[pl.ds(1, SLOTS - 1)], osem.at[3]),
-        ]
-
-    def keep_early():
-        return pltpu.make_async_copy(q.at[0], q_ref.at[0], osem.at[4])
-
-    @pl.when(served)
-    def _():
-        for cp in keep():
-            cp.start()
-
-    @pl.when(jnp.logical_and(served, slot < 4))
-    def _():
-        keep_early().start()
+    tile_waits(dms, q, qsend, qrecv, chip, core, t)
+    ring_zn.start()
+    ring_dout.start()
 
     for r in range(SLOTS):
         tile = tile_of(slot, r)
@@ -655,7 +708,7 @@
                 axis=1,
             )
             q_both = both_maps(q_t).astype(BF)
-            acc[...] = jnp.zeros_like(acc)
+            front[...] = jnp.zeros_like(front)
             total[...] = jnp.zeros_like(total)
 
             def step(b, masked):
@@ -668,11 +721,11 @@
                     if masked:
                         prob = jnp.where(key_mask(start, KB, tile, 2 * TILE), prob, 0.0)
                     part = jnp.sum(prob.reshape(KB // 8, 8, 2 * TILE), axis=0)
-                    term = matmul(v_t[:, pl.ds(start, KB)], prob.astype(BF))
+                    term = matmul(turned[:, pl.ds(start, KB)], prob.astype(BF))
                     sums = part if sums is None else sums + part
                     out = term if out is None else out + term
                 total[...] += sums
-                acc[...] += out
+                front[...] += out
 
             full = tile * TILE // STEP
 
@@ -683,180 +736,26 @@
             lax.fori_loop(0, full, body, 0)
             step(full, True)
             whole = jnp.sum(total[...], axis=0, keepdims=True)
-            parts = acc[...] / whole
-            parts_ref[r] = parts
-            log_ref[r] = bound + jnp.log(whole) * LOG2E
+            parts = front[...] / whole
+            parts_all[r] = parts
+            logs[r] = bound + jnp.log(whole) * LOG2E
             rms, hat = group_norm(parts, lam)
-            mixed_ref[r] = (hat * sub * OUT_SCALE).T.astype(BF)
-
-    kv_sends(False)
-    tile_sends(qsrc, q, qsend, qrecv, chip, core, t, False)
-    quad.drain()
-    quad_o.drain()
-    for save in saves:
-        save.wait()
-
-    @pl.when(served)
-    def _():
-        for cp in keep():
-            cp.wait()
-
-    @pl.when(jnp.logical_and(served, slot < 4))
-    def _():
-        keep_early().wait()
-
-
-def forward_part(x, cot, mask, attn, sub, lambdas, wq, wk, wv):
-    return pl.pallas_call(
-        forward_kernel,
-        name="forward",
-        out_shape=(
-            shape(HALVES, BF),
-            shape(QUARTERS, BF),
-            shape((SLOTS, TILE, 128), BF),
-            shape(KV, BF),
-            shape((SLOTS, TILE, 128), BF),
-            shape((SLOTS, 128, 2 * TILE), F32),
-            shape((SLOTS, 1, 2 * TILE), F32),
-        ),
-        in_specs=[VM] * 6 + [ANY] * 3,
-        out_specs=(ANY, ANY, ANY, ANY, VM, VM, VM),
-        scratch_shapes=[
-            pltpu.VMEM((BLOCK, D), BF),
-            pltpu.VMEM((BLOCK, D), BF),
-            pltpu.VMEM((3, D, 384), BF),
-            pltpu.VMEM((3, BLOCK, 256), BF),
-            pltpu.VMEM((3, 2, TILE, 128), BF),
-            pltpu.VMEM(KV, BF),
-            pltpu.VMEM((SLOTS, TILE, 128), BF),
-            pltpu.VMEM((128, CHIPS * BLOCK), BF),
-            pltpu.VMEM((8, BLOCK), F32),
-            pltpu.SMEM((2,), F32),
-            pltpu.VMEM((128, 2 * TILE), F32),
-            pltpu.VMEM((8, 2 * TILE), F32),
-            pltpu.SemaphoreType.DMA((3,)),
-            *(GATHER_SEMS * 2),
-            pltpu.SemaphoreType.DMA((15,)),
-            pltpu.SemaphoreType.DMA((CHIPS,)),
-            pltpu.SemaphoreType.DMA((CHIPS // 2,)),
-            pltpu.SemaphoreType.DMA((6,)),
-            pltpu.SemaphoreType.DMA((SLOTS,)),
-            pltpu.SemaphoreType.DMA((9,)),
-        ],
-        compiler_params=pltpu.CompilerParams(
-            collective_id=0, has_side_effects=True, vmem_limit_bytes=VMEM_LIMIT
-        ),
-    )(x, cot, mask, attn, sub, lambdas, wq, wk, wv)
-
-
-SPAN = 1024
-SPANS = CHIPS * BLOCK // SPAN
-PER_SPAN = SPAN // BLOCK // 2
-EARLY_SPANS = 3
-
-
-def middle_kernel(
-    x_ref, cot_ref, mask_ref, attn_ref, ffn_ref, sub_ref, lambdas_ref, tiles_ref,
-    wq_ref, wk_ref, wv_ref, wo_ref, wg_ref, wu_ref, wd_ref,
-    dout_ref, normed_ref, q_ref, kv_ref, parts_ref, log_ref,
-    out_ref, grad_ref, gq_ref, gk_ref, gv_ref, go_ref, gate_ref, up_ref, down_ref, sums_ref,
-    xnormed_ref, znormed_ref,
-    dres, dqkv_ref, rq, rk, rv, xmix, xdres, pqo, pkv, sqo, skv, swap2, swapped2,
-    vec, vecs, quarter, quarters,
-    land, wo, wg, wu, wd, fbuf, rbuf, dms, dout_all, dgate, dup, hid, mix,
-    q, kv, parts_all, logs, dmix,
-    lffn, lgate, lup, lhid, ldout, pgate, pup, pdown, sgate, sup, sdown, swap, swapped,
-    k_t, acc, q_cols, q_rows, d_cols, d_rows, deltas, dq_acc, dq_out, given, sib, both, home, *rest,
-):
-    chip, core, t = place()
-    s = 2 * chip + core
-    parity, place_at, slot, served = worker(chip, core)
-    head = 3 * parity + place_at // PER_HEAD
-    x_at, z_at = chip % 4, chip // 8
-    taken = iter(rest)
-
-    def take(count):
-        return [next(taken) for _ in range(count)]
-
-    reduces = [take(9) for _ in range(2)]
-    gather_sems = [take(2) for _ in range(2)]
-    ring_sems = [take(2) for _ in range(11)]
-    once_sems = take(4)
-    scatter = [take(2) for _ in range(5)]
-    wsem, osem, hsend, hrecv, tsend, trecv, swap_sem = take(7)
-    dsend, drecv, ksend, krecv, gsend, grecv = take(6)
-    w2sem, lsem, swap2_sem, asem, bsem, csem = take(6)
-
-    loads = [
-        weight_load(wo_ref, wo, wsem.at[0], core, 384),
-        weight_load(wg_ref, wg, wsem.at[1], core, 1024),
-        weight_load(wu_ref, wu, wsem.at[2], core, 1024),
-        weight_load(wd_ref, wd, wsem.at[3], core, 1024),
-    ]
-    fetches = [
-        pltpu.make_async_copy(src, dst, osem.at[4 + k])
-        for k, (src, dst) in enumerate(
-            ((dout_ref, dout_all), (q_ref, q), (kv_ref, kv), (parts_ref, parts_all), (log_ref, logs))
-        )
-    ]
-    loads[0].start()
-    fetches[0].start()
-    for load in loads[1:]:
-        load.start()
-    for fetch in fetches[1:]:
-        fetch.start()
-    gather_f = QuadGather(fbuf, *gather_sems[0], chip, core, t)
-    gather_r = QuadGather(rbuf, *gather_sems[1], chip, core, t)
-    ring_dout = RingGather(lambda p: dout_all.at[p // 2], ldout, *ring_sems[0], "x", chip, core, t)
-    ring_mix = RingGather(lambda p: mix, xmix, *ring_sems[1], "x", chip, core, t)
-    ring_hid = RingGather(lambda p: hid.at[p % 2], lhid, *ring_sems[2], "x", chip, core, t)
-    ring_gate = RingGather(lambda p: dgate.at[p % 2], lgate, *ring_sems[3], "z", chip, core, t)
-    ring_up = RingGather(lambda p: dup.at[p % 2], lup, *ring_sems[10], "z", chip, core, t)
-    ring_dres = RingGather(
-        lambda p: rbuf.at[:, pl.ds(pl.multiple_of(p * 384, 128), 384)],
-        xdres, *ring_sems[4], "x", chip, core, t,
-    )
-    ring_xn = RingGather(lambda p: normed_ref.at[p], xnormed_ref, *ring_sems[5], "x", chip, core, t)
-    ring_zn = RingGather(lambda p: normed_ref.at[p], znormed_ref, *ring_sems[6], "z", chip, core, t)
-    ring_q = RingGather(lambda p: dqkv_ref.at[0], rq, *ring_sems[7], "x", chip, core, t)
-    ring_k = RingGather(lambda p: dqkv_ref.at[1], rk, *ring_sems[8], "z", chip, core, t)
-    ring_v = RingGather(lambda p: dqkv_ref.at[2], rv, *ring_sems[9], "z", chip, core, t)
-    send_qo = Scatter(pqo, sqo, *scatter[2], 8, 8 * x_at, chip // 4, chip, core, t)
-    send_kv = Scatter(pkv, skv, *scatter[3], 8, 8 * z_at, chip % 8, chip, core, t)
-    members = ((s + 1 - 2 * core, t), (s, 1 - t), (s + 1 - 2 * core, 1 - t))
-    ring_ffn = RingGatherOnce(
-        lambda p: fbuf.at[:, pl.ds(pl.multiple_of((p // 2) * 768, 128), 768)],
-        lffn, *once_sems, "z", chip, core, t,
-    )
-    send_down = Scatter(
-        pdown, sdown, *scatter[0], 16, 16 * (x_at // 2), 8 * (x_at % 2) + chip // 4, chip, core, t
-    )
-    send_gate, send_up = (
-        Scatter(
-            part, to, *sems, 16, 16 * (z_at // 2), 8 * (z_at % 2) + chip % 8, chip, core, t
-        )
-        for part, to, sems in ((pgate, sgate, scatter[1]), (pup, sup, scatter[4]))
-    )
-    mine = pl.ds(pl.multiple_of(gather_f.mine, ROWS), ROWS)
-    dout = cot_ref[...] * mask_column(mask_ref)
-    lam = lambda_of(lambdas_ref, 6 * t + head)
-    sub = as_column(sub_ref[...])
-    ffn_gain = long_row(ffn_ref)
-    vec[...] = jnp.zeros_like(vec)
-    greet_all(chip, core, t)
-    home_sends(tiles_ref, land, hsend, hrecv, chip, core, t, True)
-    ring_zn.start()
-    ring_xn.start()
+            dq_out[r] = (hat * sub * OUT_SCALE).T.astype(BF)
+
+
+    home_sends(dq_out, land, hsend, hrecv, chip, core, t, True)
     loads[0].wait()
-    home_waits(tiles_ref, land, hrecv)
+    home_waits(dq_out, land, hrecv)
     for j in range(3):
         for u in range(2):
             mix[u * 128 : (u + 1) * 128, j * 128 : (j + 1) * 128] = land[j, u]
     red = QuadReduce(*reduces[0], chip, core, t)
     red.run(lambda k: matmul_t(mix[...], wo[k * CW : (k + 1) * CW, :]))
-    fetches[0].wait()
-    ring_dout.start()
+    ring_xn.start()
     ring_mix.start()
+    home_sends(dq_out, land, hsend, hrecv, chip, core, t, False)
+    kv_sends(False)
+    tile_sends(dms, q, qsend, qrecv, chip, core, t, False)
     resid = x_ref[...] + jnp.concatenate([red.result(k) for k in range(NC)], axis=1)
     ffn_rms = rms_scale(resid)
     ffn_hat = resid * ffn_rms
@@ -873,7 +772,7 @@
         b, at = n // 2, n % 2
         gate = matmul(fbuf[...], wg[:, cols])
         up = matmul(fbuf[...], wu[:, cols])
-        d_hidden = matmul(dout_all[0], wd[:768, cols]) + matmul(dout_all[1], wd[768:, cols])
+        d_hidden = matmul(obuf[...], wd[:, cols])
         sig = 1.0 / (1.0 + jnp.exp(-gate))
         silu = gate * sig
         to = pl.ds(pl.multiple_of(at * 256, 256), 256)
@@ -896,6 +795,11 @@
             + matmul_t(dup[1], wu[rows, 512:])
         )
 
+    quad.drain()
+    quad_o.drain()
+    for ring in (ring_zn, ring_xn):
+        ring.finish()
+        ring.drain()
     red2.run(ffn_term)
     late_loads = [
         weight_load(ref, buf.at[:, k * 384 : (k + 1) * 384], w2sem.at[i], core, 384)
@@ -926,8 +830,6 @@
     ring_up.start()
     ring_dres.start()
     out_ref[...] = resid + jnp.concatenate([red3.result(k) for k in range(NC)], axis=1)
-    for fetch in fetches[1:]:
-        fetch.wait()
 
     def to_sibling(o):
         at = o % (2 * PER_SPAN)
@@ -961,7 +863,7 @@
         def flip(b, carry):
             rows = pl.ds(pl.multiple_of(b * KB, KB), KB)
             block = kv[pl.ds(2 * b, 2), :, :128].reshape(KB, 128)
-            k_t[:, rows] = matmul_t(unit, block).astype(BF)
+            turned[:, rows] = matmul_t(unit, block).astype(BF)
             return carry
 
         lax.fori_loop(0, CHIPS * BLOCK // KB, flip, 0)
@@ -969,8 +871,6 @@
     ring_dout.finish()
     ring_hid.finish()
     block_grad(pdown, 0, ldout, lhid[...].reshape(4 * BLOCK, 512), 256)
-    ring_xn.finish()
-    ring_zn.finish()
     lefts = [
         pltpu.make_async_copy(src, ldout.at[:, :, k * 384 : (k + 1) * 384], lsem.at[k])
         for k, src in enumerate((xnormed_ref, znormed_ref))
@@ -1040,7 +940,7 @@
             mixed = (p1 - lam * p2).astype(BF)
             acc[:, :128] += matmul(ds, q_rows[r])
             acc[:, 128:] += matmul(mixed, d_rows[r])
-            dq_acc[r] += matmul(k_t[:, rows], ds)
+            dq_acc[r] += matmul(turned[:, rows], ds)
 
         def masked_step(r, carry):
             step(r, True)
@@ -1078,43 +978,16 @@
 
         return carry
 
-    def early(k, carry):
-        span(k, carry)
-
-        @pl.when(k < 2)
-        def _():
-            send_gate.some(8 * k, 8 * k + 8, True)
-
-        return carry
-
-    def late(k, carry):
-        span(k, carry)
-
-        @pl.when(k < EARLY_SPANS + 4)
-        def _():
-            at = 4 * (k - EARLY_SPANS)
-            send_up.some(at, at + 4, True)
-
-        return carry
-
     @pl.when(served)
     def _():
-        lax.fori_loop(0, EARLY_SPANS, early, 0)
-
-    @pl.when(jnp.logical_not(served))
-    def _():
-        send_gate.each(True)
+        lax.fori_loop(0, EARLY_SPANS, span, 0)
 
     ring_up.finish()
     block_grad(pup, 0, lffn, lup[...].reshape(4 * BLOCK, 512), 256)
 
-    @pl.when(jnp.logical_not(served))
-    def _():
-        send_up.each(True)
-
     @pl.when(served)
     def _():
-        lax.fori_loop(EARLY_SPANS, SPANS, late, 0)
+        lax.fori_loop(EARLY_SPANS, SPANS, span, 0)
         pass_on(SPANS - 1)
 
     for r in range(SLOTS):
@@ -1140,6 +1013,8 @@
         dqkv_ref[2, :, j * 128 : (j + 1) * 128] = total[:, 128:].astype(BF)
     ring_k.start()
     ring_v.start()
+    send_gate.each(True)
+    send_up.each(True)
 
     for load in late_loads:
         load.wait()
@@ -1179,9 +1054,6 @@
     send_qo.each(True)
     ring_k.finish()
     block_grad(pkv, 0, ldout, rk[...].reshape(4 * BLOCK, 384), 384, 384, 384)
-    ring_v.finish()
-    block_grad(pkv, 384, ldout, rv[...].reshape(4 * BLOCK, 384), 384, 384, 384)
-    send_kv.each(True)
     for cp in first_sum:
         cp.wait_recv()
     share = pl.ds(pl.multiple_of((2 * core + t) * 8, 8), 8)
@@ -1206,6 +1078,9 @@
     own = pltpu.make_async_copy(quarter, quarters.at[chip], bsem.at[1, chip])
     own.start()
     lax.fori_loop(1, CHIPS, spread_start, 0)
+    ring_v.finish()
+    block_grad(pkv, 384, ldout, rv[...].reshape(4 * BLOCK, 384), 384, 384, 384)
+    send_kv.each(True)
 
     send_down.wait()
     for b in range(2):
@@ -1247,13 +1122,11 @@
     swap_out(swap, swapped, ((gate_ref, 0), (up_ref, 1024), (down_ref, 2048)), 1024, core)
 
     for ring in (
-        ring_dout, ring_mix, ring_hid, ring_gate, ring_up, ring_dres, ring_ffn, ring_xn, ring_zn, ring_q, ring_k,
-        ring_v,
+        ring_dout, ring_mix, ring_hid, ring_gate, ring_up, ring_dres, ring_ffn, ring_q, ring_k, ring_v,
     ):
         ring.drain()
     for send in (send_gate, send_up, send_down, send_qo, send_kv):
         send.each(False)
-    home_sends(tiles_ref, land, hsend, hrecv, chip, core, t, False)
     home_sends(dq_out, land, gsend, grecv, chip, core, t, False)
     tile_sends(dms, dmix, tsend, trecv, chip, core, t, False)
     for gather in (gather_f, gather_r):
@@ -1295,16 +1168,13 @@
                 ref[:, other : other + width] = swapped[:, at : at + width]
 
 
-def middle_part(
-    x, cot, mask, attn, ffn, sub, lambdas, tiles, wq, wk, wv, wo, wg, wu, wd,
-    dout_all, normed, q, kv, parts, logs,
-):
+def layer(x, cot, mask, attn, ffn, sub, lambdas, wq, wk, wv, wo, wg, wu, wd):
     half = (CHIPS // 2, BLOCK, 256)
     vm = pltpu.VMEM
     sem = pltpu.SemaphoreType.DMA
     return pl.pallas_call(
-        middle_kernel,
-        name="middle",
+        layer_kernel,
+        name="layer",
         out_shape=(
             shape((ROWS, D), F32),
             shape((ROWS, D), F32),
@@ -1314,7 +1184,7 @@
             shape(GATHERED_Q, BF),
             shape(GATHERED_Q, BF),
         ),
-        in_specs=[VM] * 7 + [ANY] * 14,
+        in_specs=[VM] * 7 + [ANY] * 7,
         out_specs=(VM,) * 10 + (ANY,) * 2,
         scratch_shapes=[
             vm((ROWS, D), F32),
@@ -1338,7 +1208,7 @@
             vm((BLOCK, D), BF),
             vm((BLOCK, D), BF),
             vm((3, 2, TILE, 128), BF),
-            vm(HALVES, BF),
+            vm((BLOCK, D), BF),
             vm((2, BLOCK, 512), BF),
             vm((2, BLOCK, 512), BF),
             vm((2, BLOCK, 512), BF),
@@ -1368,15 +1238,17 @@
             vm(half, BF),
             vm(half, BF),
             vm((3 * PER_HEAD, BLOCK, 256), BF),
+            vm((8, BLOCK), F32),
+            pltpu.SMEM((2,), F32),
+            vm((8, 2 * TILE), F32),
             *(REDUCE_SCRATCH * 2),
-            *(GATHER_SEMS * 2),
+            *(GATHER_SEMS * 4),
             *(RING_SEMS * 11),
             *ONCE_SEMS,
             *(scatter_sems(16) * 2),
             *(scatter_sems(8) * 2),
             *scatter_sems(16),
             sem((4,)),
-            sem((9,)),
             sem((SLOTS,)),
             sem((3, 2)),
             sem((6,)),
@@ -1394,14 +1266,16 @@
             sem((2, 3)),
             sem((2, CHIPS)),
             sem((2, 3)),
+            sem((WORKERS,)),
+            sem((CHIPS,)),
+            sem((CHIPS // 2,)),
+            sem((6,)),
+            sem((SLOTS,)),
         ],
         compiler_params=pltpu.CompilerParams(
-            collective_id=1, has_side_effects=True, vmem_limit_bytes=VMEM_LIMIT
+            collective_id=0, has_side_effects=True, vmem_limit_bytes=VMEM_LIMIT
         ),
-    )(
-        x, cot, mask, attn, ffn, sub, lambdas, tiles, wq, wk, wv, wo, wg, wu, wd,
-        dout_all, normed, q, kv, parts, logs,
-    )
+    )(x, cot, mask, attn, ffn, sub, lambdas, wq, wk, wv, wo, wg, wu, wd)
 
 
 def publish(lambdas, sums, arrays):
@@ -1438,13 +1312,9 @@
     attn = attn_gain.reshape(12, 128)
     sub = subln_gain.reshape(1, 128)
     by_head = jnp.transpose(lambdas, (1, 0, 2))
-    dout, normed, q, kv, mixed, parts, logs = forward_part(
-        hidden_in, cotangent, mask, attn, sub, by_head, weight_query, weight_key, weight_value
-    )
-    *results, sums, _, _ = middle_part(
-        hidden_in, cotangent, mask, attn, ffn_gain.reshape(12, 128), sub, by_head, mixed,
+    *results, sums, _, _ = layer(
+        hidden_in, cotangent, mask, attn, ffn_gain.reshape(12, 128), sub, by_head,
         weight_query, weight_key, weight_value, weight_out, weight_gate, weight_up, weight_down,
-        dout, normed, q, kv, parts, logs,
     )
     *results, attn_grad, ffn_grad, sub_grad, lambda_grad = publish(by_head, sums, results)
     return (

time: 246 us -> 241 us (0.980)
  Pallas kernels: 241 us -> 236 us
    pallas_call x2 -> x1, Pallas kernels: 238 us -> 233 us  [layer(): pl.pallas_call(layer_kernel, name='layer', out_shape=(shape((ROWS, D), F3...]
where the time goes in v5:
time: 241 us; the launch traced here: 237 us
  Pallas kernels  236 us (98%)
    pallas_call x1, Pallas kernels, layer(): pl.pallas_call(layer_kernel, name='layer', out_shape=(shape((ROWS, D), F3...  233 us

profile of v5, /device:TPU:31, one launch (start us, length us, event | category | flops | bytes accessed | tf_op | source)
XLA Modules:
  0.0 236.9 jit_solution(13237421118699989047)
XLA Ops:
  0.6 233.3 %layer.1 = (f32[64,1536]{1,0:T(8,128)}, f32[64,1536]{1,0:T(8,128)}, f32[24,768]{1,0:T(8,128)}, f32[24,768]{1,0:T(8,128)}, f32[24,768]{1,0:T(8,128)}, /*index=5*/...) custom-call(f32[64,1536]{1,0:T(8,128)} %x_ref.1, ...), custom_call_target="tpu_custom_call" | custom-call | tf_op jit(solution)/shard_map/layer/pallas_call | solution.py:1175
  233.9 2.7 %publish.1 = (f32[64,1536]{1,0:T(8,128)}, f32[64,1536]{1,0:T(8,128)}, f32[24,768]{1,0:T(8,128)}, f32[24,768]{1,0:T(8,128)}, f32[24,768]{1,0:T(8,128)}, /*index=5...) custom-call(f32[12,4,64]{2,1,0:T(4,128)} %bitcast.10, ...), custom_call_target="tpu_custom_call" | custom-call | tf_op jit(solution)/shard_map/publish/pallas_call | solution.py:1297

commit v6 on v5

--- a/solution.py
+++ b/solution.py
@@ -509,9 +509,10 @@
 def layer_kernel(
     x_ref, cot_ref, mask_ref, attn_ref, ffn_ref, sub_ref, lambdas_ref,
     wq_ref, wk_ref, wv_ref, wo_ref, wg_ref, wu_ref, wd_ref,
-    out_ref, grad_ref, gq_ref, gk_ref, gv_ref, go_ref, gate_ref, up_ref, down_ref, sums_ref,
+    out_to, grad_to, gq_to, gk_to, gv_to, go_to, gate_to, up_to, down_to, sums_ref,
     xnormed_ref, znormed_ref,
-    dres, dqkv_ref, rq, rk, rv, xmix, xdres, pqo, pkv, sqo, skv, swap2, swapped2,
+    out_ref, grad_ref, gq_ref, gk_ref, gv_ref, go_ref, gate_ref, up_ref, down_ref,
+    dres, dqkv_ref, rq, rk, rvx, rvz, xmix, xdres, pqo, pkv, sqo, skv, swap2, swapped2,
     vec, vecs, quarter, quarters,
     land, wo, wg, wu, wd, fbuf, nbuf, dms, obuf, dgate, dup, hid, mix,
     q, kv, parts_all, logs, dmix,
@@ -531,12 +532,23 @@
 
     reduces = [take(9) for _ in range(2)]
     gather_sems = [take(2) for _ in range(4)]
-    ring_sems = [take(2) for _ in range(11)]
+    ring_sems = [take(2) for _ in range(12)]
     once_sems = take(4)
     scatter = [take(2) for _ in range(5)]
     wsem, hsend, hrecv, tsend, trecv, swap_sem = take(6)
     dsend, drecv, ksend, krecv, gsend, grecv = take(6)
     w2sem, lsem, swap2_sem, asem, bsem, csem = take(6)
+    (osem,) = take(1)
+    results = [
+        pltpu.make_async_copy(src, dst, osem.at[k])
+        for k, (src, dst) in enumerate(
+            (
+                (out_ref, out_to), (grad_ref, grad_to), (gq_ref, gq_to), (gk_ref, gk_to),
+                (gv_ref, gv_to), (go_ref, go_to), (gate_ref, gate_to), (up_ref, up_to),
+                (down_ref, down_to),
+            )
+        )
+    ]
     kvsend, kvrecv, fsend, qsend, qrecv = take(5)
     rbuf = nbuf
     front = dq_acc.at[0]
@@ -562,7 +574,12 @@
     ring_zn = RingGather(quarters_of(nbuf), znormed_ref, *ring_sems[6], "z", chip, core, t)
     ring_q = RingGather(lambda p: dqkv_ref.at[0], rq, *ring_sems[7], "x", chip, core, t)
     ring_k = RingGather(lambda p: dqkv_ref.at[1], rk, *ring_sems[8], "z", chip, core, t)
-    ring_v = RingGather(lambda p: dqkv_ref.at[2], rv, *ring_sems[9], "z", chip, core, t)
+    ring_vx = RingGather(
+        lambda p: dqkv_ref.at[2, :, :128], rvx, *ring_sems[9], "x", chip, core, t
+    )
+    ring_vz = RingGather(
+        lambda p: dqkv_ref.at[2, :, 128:], rvz, *ring_sems[11], "z", chip, core, t
+    )
     send_qo = Scatter(pqo, sqo, *scatter[2], 8, 8 * x_at, chip // 4, chip, core, t)
     send_kv = Scatter(pkv, skv, *scatter[3], 8, 8 * z_at, chip % 8, chip, core, t)
     members = ((s + 1 - 2 * core, t), (s, 1 - t), (s + 1 - 2 * core, 1 - t))
@@ -830,6 +847,7 @@
     ring_up.start()
     ring_dres.start()
     out_ref[...] = resid + jnp.concatenate([red3.result(k) for k in range(NC)], axis=1)
+    results[0].start()
 
     def to_sibling(o):
         at = o % (2 * PER_SPAN)
@@ -978,16 +996,43 @@
 
         return carry
 
+    def early(k, carry):
+        span(k, carry)
+
+        @pl.when(k < 2)
+        def _():
+            send_gate.some(8 * k, 8 * k + 8, True)
+
+        return carry
+
+    def late(k, carry):
+        span(k, carry)
+
+        @pl.when(k < EARLY_SPANS + 4)
+        def _():
+            at = 4 * (k - EARLY_SPANS)
+            send_up.some(at, at + 4, True)
+
+        return carry
+
     @pl.when(served)
     def _():
-        lax.fori_loop(0, EARLY_SPANS, span, 0)
+        lax.fori_loop(0, EARLY_SPANS, early, 0)
+
+    @pl.when(jnp.logical_not(served))
+    def _():
+        send_gate.each(True)
 
     ring_up.finish()
     block_grad(pup, 0, lffn, lup[...].reshape(4 * BLOCK, 512), 256)
 
+    @pl.when(jnp.logical_not(served))
+    def _():
+        send_up.each(True)
+
     @pl.when(served)
     def _():
-        lax.fori_loop(EARLY_SPANS, SPANS, span, 0)
+        lax.fori_loop(EARLY_SPANS, SPANS, late, 0)
         pass_on(SPANS - 1)
 
     for r in range(SLOTS):
@@ -1012,9 +1057,8 @@
         dqkv_ref[1, :, j * 128 : (j + 1) * 128] = total[:, :128].astype(BF)
         dqkv_ref[2, :, j * 128 : (j + 1) * 128] = total[:, 128:].astype(BF)
     ring_k.start()
-    ring_v.start()
-    send_gate.each(True)
-    send_up.each(True)
+    ring_vx.start()
+    ring_vz.start()
 
     for load in late_loads:
         load.wait()
@@ -1047,10 +1091,13 @@
     for cp in first_sum:
         cp.start()
     grad_ref[...] = dres[...] + norm_back(d_normed, long_row(attn_ref), rms, hat)
+    results[1].start()
     for left in lefts:
         left.wait()
     ring_q.finish()
     block_grad(pqo, 0, ldout, rq[...].reshape(4 * BLOCK, 384), 384, 0, 384)
+    ring_vx.finish()
+    block_grad(pqo, 768, ldout, rvx[...].reshape(4 * BLOCK, 128), 384, 0, 384)
     send_qo.each(True)
     ring_k.finish()
     block_grad(pkv, 0, ldout, rk[...].reshape(4 * BLOCK, 384), 384, 384, 384)
@@ -1078,8 +1125,8 @@
     own = pltpu.make_async_copy(quarter, quarters.at[chip], bsem.at[1, chip])
     own.start()
     lax.fori_loop(1, CHIPS, spread_start, 0)
-    ring_v.finish()
-    block_grad(pkv, 384, ldout, rv[...].reshape(4 * BLOCK, 384), 384, 384, 384)
+    ring_vz.finish()
+    block_grad(pkv, 384, ldout, rvz[...].reshape(4 * BLOCK, 256), 384, 384, 384)
     send_kv.each(True)
 
     send_down.wait()
@@ -1109,20 +1156,25 @@
     ]
     for cp in last_sum:
         cp.start()
-    for send, first in ((send_qo, (0, 3)), (send_kv, (1, 2))):
+    for send, spots in (
+        (send_qo, ((0, 384, 0), (384, 384, 1152), (768, 128, 768))),
+        (send_kv, ((0, 384, 384), (384, 256, 896))),
+    ):
         send.wait()
-        for m in range(2):
-            total = send.total(0, slice(m * 384, m * 384 + 384))
-            at = first[m] * 384
+        for first, width, at in spots:
+            total = send.total(0, slice(first, first + width))
             for h in range(2):
-                swap2[h, :, at : at + 384] = total[h * 24 : h * 24 + 24]
+                swap2[h, :, at : at + width] = total[h * 24 : h * 24 + 24]
     swap2_copy = remote(swap2.at[1 - core], swapped2, swap2_sem.at[0], swap2_sem.at[1], sibling, t)
     swap2_copy.start()
     swap_copy.wait()
     swap_out(swap, swapped, ((gate_ref, 0), (up_ref, 1024), (down_ref, 2048)), 1024, core)
+    for cp in results[6:]:
+        cp.start()
 
     for ring in (
-        ring_dout, ring_mix, ring_hid, ring_gate, ring_up, ring_dres, ring_ffn, ring_q, ring_k, ring_v,
+        ring_dout, ring_mix, ring_hid, ring_gate, ring_up, ring_dres, ring_ffn, ring_q, ring_k, ring_vx,
+        ring_vz,
     ):
         ring.drain()
     for send in (send_gate, send_up, send_down, send_qo, send_kv):
@@ -1154,6 +1206,10 @@
     swap2_copy.wait()
     outs = ((gq_ref, 0), (gk_ref, 384), (gv_ref, 768), (go_ref, 1152))
     swap_out(swap2, swapped2, outs, 384, core)
+    for cp in results[2:6]:
+        cp.start()
+    for cp in results:
+        cp.wait()
 
 
 def swap_out(swap, swapped, outs, width, core):
@@ -1185,15 +1241,22 @@
             shape(GATHERED_Q, BF),
         ),
         in_specs=[VM] * 7 + [ANY] * 7,
-        out_specs=(VM,) * 10 + (ANY,) * 2,
+        out_specs=(ANY,) * 9 + (VM,) + (ANY,) * 2,
         scratch_shapes=[
             vm((ROWS, D), F32),
+            vm((ROWS, D), F32),
+            *([vm((24, 768), F32)] * 4),
+            *([vm((24, 2048), F32)] * 3),
+            vm((ROWS, D), F32),
             vm((3, BLOCK, 384), BF),
-            *([vm(GATHERED_Q, BF)] * 5),
-            vm((384, 768), BF),
-            vm((384, 768), BF),
-            vm((8, CHUNK, 768), BF),
-            vm((8, CHUNK, 768), BF),
+            *([vm(GATHERED_Q, BF)] * 2),
+            vm((4, BLOCK, 128), BF),
+            vm((4, BLOCK, 256), BF),
+            *([vm(GATHERED_Q, BF)] * 2),
+            vm((384, 896), BF),
+            vm((384, 640), BF),
+            vm((8, CHUNK, 896), BF),
+            vm((8, CHUNK, 640), BF),
             vm((2, 24, 1536), F32),
             vm((24, 1536), F32),
             vm((32, 128), F32),
@@ -1243,7 +1306,7 @@
             vm((8, 2 * TILE), F32),
             *(REDUCE_SCRATCH * 2),
             *(GATHER_SEMS * 4),
-            *(RING_SEMS * 11),
+            *(RING_SEMS * 12),
             *ONCE_SEMS,
             *(scatter_sems(16) * 2),
             *(scatter_sems(8) * 2),
@@ -1266,6 +1329,7 @@
             sem((2, 3)),
             sem((2, CHIPS)),
             sem((2, 3)),
+            sem((9,)),
             sem((WORKERS,)),
             sem((CHIPS,)),
             sem((CHIPS // 2,)),

time: 241 us -> 245 us (1.017)
  Pallas kernels: 236 us -> 239 us
    pallas_call x1, Pallas kernels: 233 us -> 236 us  [layer(): pl.pallas_call(layer_kernel, name='layer', out_shape=(shape((ROWS, D), F3...]
where the time goes in v6:
time: 245 us; the launch traced here: 240 us
  Pallas kernels  239 us (98%)
    pallas_call x1, Pallas kernels, layer(): pl.pallas_call(layer_kernel, name='layer', out_shape=(shape((ROWS, D), F3...  236 us

profile of v6, /device:TPU:31, one launch (start us, length us, event | category | flops | bytes accessed | tf_op | source)
XLA Modules:
  0.0 239.7 jit_solution(13339801610217612370)
XLA Ops:
  0.6 236.2 %layer.1 = (f32[64,1536]{1,0:T(8,128)}, f32[64,1536]{1,0:T(8,128)}, f32[24,768]{1,0:T(8,128)}, f32[24,768]{1,0:T(8,128)}, f32[24,768]{1,0:T(8,128)}, /*index=5*/...) custom-call(f32[64,1536]{1,0:T(8,128)} %x_ref.1, ...), custom_call_target="tpu_custom_call" | custom-call | tf_op jit(solution)/shard_map/layer/pallas_call | solution.py:1231
  236.8 2.7 %publish.1 = (f32[64,1536]{1,0:T(8,128)}, f32[64,1536]{1,0:T(8,128)}, f32[24,768]{1,0:T(8,128)}, f32[24,768]{1,0:T(8,128)}, f32[24,768]{1,0:T(8,128)}, /*index=5...) custom-call(f32[12,4,64]{2,1,0:T(4,128)} %bitcast.10, ...), custom_call_target="tpu_custom_call" | custom-call | tf_op jit(solution)/shard_map/publish/pallas_call | solution.py:1361

commit v7 on v6

--- a/solution.py
+++ b/solution.py
@@ -24,6 +24,7 @@
 KB = 512
 LOG2E = 1.4426950408889634
 SCORE = 0.125 * LOG2E
+LOWEST = -1e30
 VMEM_LIMIT = 63 * 2**20
 
 
@@ -139,7 +140,8 @@
 class RingGather:
     def __init__(self, pieces, land, send, recv, axis, chip, core, t):
         at = chip % 4 if axis == "x" else chip // 8
-        self.local = pltpu.make_async_copy(pieces(at), land.at[at], recv.at[at])
+        self.local = pltpu.make_async_copy(pieces(at), land.at[at], recv.at[0])
+        self.land, self.send, self.recv = land, send, recv
         self.copies = []
         for k in (1, 3, 2):
             if axis == "x":
@@ -147,11 +149,8 @@
             else:
                 peer, chip_to = (at + k) % 4, (chip + 8 * k) % CHIPS
             self.copies.append(
-                remote(pieces(peer), land.at[at], send.at[k - 1], recv.at[at], 2 * chip_to + core, t)
+                remote(pieces(peer), land.at[at], send.at[0], recv.at[0], 2 * chip_to + core, t)
             )
-        self.waits = [
-            pltpu.make_async_copy(pieces(at), land.at[k], recv.at[k]) for k in range(4)
-        ]
 
     def start(self):
         self.local.start()
@@ -159,12 +158,11 @@
             cp.start()
 
     def finish(self):
-        for cp in self.waits:
-            cp.wait()
+        pltpu.make_async_copy(self.land, self.land, self.recv.at[0]).wait()
 
     def drain(self):
-        for cp in self.copies:
-            cp.wait_send()
+        three = self.land.at[pl.ds(0, 3)]
+        pltpu.make_async_copy(three, three, self.send.at[0]).wait()
 
 
 class RingGatherOnce:
@@ -219,7 +217,7 @@
     pltpu.SemaphoreType.DMA((3,)),
     pltpu.SemaphoreType.DMA((3,)),
 ]
-RING_SEMS = [pltpu.SemaphoreType.DMA((3,)), pltpu.SemaphoreType.DMA((4,))]
+RING_SEMS = [pltpu.SemaphoreType.DMA((1,)), pltpu.SemaphoreType.DMA((1,))]
 
 
 def block_grad(dst, start, left, right, step, at=0, total=768):
@@ -248,52 +246,46 @@
     def source(self, i):
         return self.part.at[pl.ds(pl.multiple_of(i * CHUNK, 16), CHUNK)]
 
-    def each(self, start):
-        self.some(0, self.count, start)
-
-    def some(self, first, end, start):
+    def each(self):
+        self.some(0, self.count)
+
+    def some(self, first, end):
         def one(o, carry):
             i = lax.rem(self.chip + 1 + 3 * o, self.count)
             owner = self.first + i
-            cp = remote(
-                self.source(i), self.land.at[self.spot], self.send.at[i], self.recv.at[self.spot],
-                2 * owner + self.core, self.t,
-            )
-            if start:
-
-                @pl.when(owner == self.chip)
-                def _():
-                    pltpu.make_async_copy(
-                        self.source(i), self.land.at[self.spot], self.recv.at[self.spot]
-                    ).start()
+            to = self.land.at[self.spot]
+
+            @pl.when(owner == self.chip)
+            def _():
+                pltpu.make_async_copy(self.source(i), to, self.recv.at[0]).start()
 
             @pl.when(owner != self.chip)
             def _():
-                if start:
-                    cp.start()
-                else:
-                    cp.wait_send()
+                remote(
+                    self.source(i), to, self.send.at[0], self.recv.at[0], 2 * owner + self.core, self.t
+                ).start()
 
             return carry
 
         lax.fori_loop(first, end, one, 0)
 
     def wait(self):
-        def one(k, carry):
-            pltpu.make_async_copy(self.source(0), self.land.at[k], self.recv.at[k]).wait()
-            return carry
-
-        lax.fori_loop(0, self.count, one, 0)
+        pltpu.make_async_copy(self.land, self.land, self.recv.at[0]).wait()
+
+    def drain(self):
+        own = jnp.logical_and(self.chip >= self.first, self.chip < self.first + self.count)
+        for count, case in ((self.count - 1, own), (self.count, jnp.logical_not(own))):
+
+            @pl.when(case)
+            def _():
+                sent = self.part.at[pl.ds(0, count * CHUNK)]
+                pltpu.make_async_copy(sent, sent, self.send.at[0]).wait()
 
     def total(self, b, cols):
         def one(k, carry):
             return carry + self.land[8 * b + k, :, cols].astype(F32)
 
         return lax.fori_loop(0, 8, one, jnp.zeros((CHUNK, cols.stop - cols.start), F32))
-
-
-def scatter_sems(count):
-    return [pltpu.SemaphoreType.DMA((count,)), pltpu.SemaphoreType.DMA((count,))]
 
 
 GATHER_SEMS = [pltpu.SemaphoreType.DMA((3,)), pltpu.SemaphoreType.DMA((3,))]
@@ -306,12 +298,13 @@
         self.part, self.dsend, self.drecv = part, dsend, drecv
         self.ysend, self.yrecv = ysend, yrecv
         self.core, self.t = core, t
+        self.ds, self.ys = ds, ys
         self.d = [
-            remote(dsend.at[k], drecv.at[k], ds.at[k], dr.at[k], 2 * chip + 1 - core, t)
+            remote(dsend.at[k], drecv.at[k], ds.at[0], dr.at[k], 2 * chip + 1 - core, t)
             for k in range(NC)
         ]
         self.y = [
-            remote(ysend.at[k], yrecv.at[k], ys.at[k], yr.at[k], 2 * chip + core, 1 - t)
+            remote(ysend.at[k], yrecv.at[k], ys.at[0], yr.at[k], 2 * chip + core, 1 - t)
             for k in range(NC)
         ]
 
@@ -346,9 +339,8 @@
         self.middle(NC - 1)
 
     def drain(self):
-        for k in range(NC):
-            self.d[k].wait_send()
-            self.y[k].wait_send()
+        pltpu.make_async_copy(self.dsend, self.dsend, self.ds.at[0]).wait()
+        pltpu.make_async_copy(self.ysend, self.ysend, self.ys.at[0]).wait()
 
 
 REDUCE_SCRATCH = [
@@ -357,7 +349,7 @@
     pltpu.VMEM((NC, 128, CW), BF),
     pltpu.VMEM((NC, ROWS, CW), BF),
     pltpu.VMEM((NC, ROWS, CW), BF),
-] + [pltpu.SemaphoreType.DMA((NC,))] * 4
+] + [pltpu.SemaphoreType.DMA((n,)) for n in (1, NC, 1, NC)]
 
 
 def tile_sends(tiles, land, send, recv, chip, core, t, start):
@@ -518,7 +510,7 @@
     q, kv, parts_all, logs, dmix,
     lffn, lgate, lup, lhid, ldout, pgate, pup, pdown, sgate, sup, sdown, swap, swapped,
     turned, acc, q_cols, q_rows, d_cols, d_rows, deltas, dq_acc, dq_out, given, sib, both, home,
-    peaks, kmax, total, *rest,
+    peaks, *rest,
 ):
     chip, core, t = place()
     s = 2 * chip + core
@@ -551,7 +543,6 @@
     ]
     kvsend, kvrecv, fsend, qsend, qrecv = take(5)
     rbuf = nbuf
-    front = dq_acc.at[0]
 
 
     def halves(ref):
@@ -605,7 +596,7 @@
         weight_load(wu_ref, wu, wsem.at[2], core, 1024),
         weight_load(wd_ref, wd, wsem.at[3], core, 1024),
     ]
-    for load in first_loads + loads[:1]:
+    for load in (first_loads[2], *first_loads[:2], loads[0]):
         load.start()
     quad = QuadGather(nbuf, *gather_sems[2], chip, core, t)
     quad_o = QuadGather(obuf, *gather_sems[3], chip, core, t)
@@ -621,144 +612,148 @@
     sub = as_column(sub_ref[...])
     ffn_gain = long_row(ffn_ref)
     vec[...] = jnp.zeros_like(vec)
-    unit = eye(256)
+    unit = eye(128)
     quad.finish()
-    for k in range(2):
-        first_loads[k].wait()
-        value = matmul(nbuf[...], wg[:, k * 384 : (k + 1) * 384]).astype(BF)
-        for j in range(3):
-            dqkv_ref[j, :, k * 128 : (k + 1) * 128] = value[:, j * 128 : (j + 1) * 128]
-
     def kv_piece(j):
         return dqkv_ref.at[j, :, :256]
 
-    def kv_sends(start):
+    self_served = jnp.logical_and(parity == core, chip % 2 == core)
+
+    def kv_sends():
         def one(o, carry):
             w = lax.rem(chip + 7 * o, WORKERS)
             j = w // PER_HEAD
             target = 2 * worker_chip(core, w) + chip % 2
-            if start:
-
-                @pl.when(target == s)
-                def _():
-                    pltpu.make_async_copy(kv_piece(j), kv.at[chip], kvrecv.at[chip]).start()
+
+            @pl.when(target == s)
+            def _():
+                pltpu.make_async_copy(kv_piece(j), kv.at[chip], kvrecv.at[chip]).start()
 
             @pl.when(target != s)
             def _():
-                cp = remote(kv_piece(j), kv.at[chip], kvsend.at[w], kvrecv.at[chip], target, t)
-                if start:
-                    cp.start()
-                else:
-                    cp.wait_send()
+                remote(kv_piece(j), kv.at[chip], kvsend.at[0], kvrecv.at[chip], target, t).start()
 
             return carry
 
         lax.fori_loop(0, WORKERS, one, 0)
 
-    kv_sends(True)
     first_loads[2].wait()
     value = matmul(nbuf[...], wu[:, :384]).astype(BF)
     for j in range(3):
         for u in range(2):
             dms[j, u] = value[u * 128 : (u + 1) * 128, j * 128 : (j + 1) * 128]
     tile_sends(dms, q, qsend, qrecv, chip, core, t, True)
+    for k in range(2):
+        first_loads[k].wait()
+        value = matmul(nbuf[...], wg[:, k * 384 : (k + 1) * 384]).astype(BF)
+        for j in range(3):
+            dqkv_ref[j, :, k * 128 : (k + 1) * 128] = value[:, j * 128 : (j + 1) * 128]
+
+    kv_sends()
     quad_o.start()
     for load in loads[1:]:
         load.start()
 
-    def forward(o):
-        source = lax.rem((chip // 2 + o) * 2 + core, CHIPS)
-        view = kv.at[source]
-        return source, remote(view, view, fsend.at[o], kvrecv.at[source], s + 1 - 2 * core, t)
-
-    def turn(source):
-        block = kv[source]
-        at = pl.ds(pl.multiple_of(source * BLOCK, BLOCK), BLOCK)
-        both_t = matmul_t(unit, block)
-        turned[:, at] = both_t[128:].astype(BF)
-        square = both_t[:128] * both_t[:128]
-        for m in range(2):
-            largest = jnp.sum(square[64 * m : 64 * m + 64], axis=0, keepdims=True)
-            peaks[m : m + 1, :] = jnp.maximum(peaks[m : m + 1, :], largest)
+    def tile_at(r):
+        late = 4 + 10 * (r - 1) + jnp.where((r - 1) % 2 == 0, slot, 9 - slot)
+        return jnp.where(r == 0, slot, late)
+
+    def tiles_from(first, span):
+        reach, past = 0, 0
+        for r in range(SLOTS):
+            last = tile_of(slot, r) * TILE // span
+            counts = (slot < 4) if r == 0 else True
+            reach += jnp.where(jnp.logical_and(counts, last >= first), 1, 0)
+            past += jnp.where(jnp.logical_and(counts, last > first), 1, 0)
+        return SLOTS - reach, SLOTS - past
+
+    def each_tile(first, span, step):
+        reach, past = tiles_from(first, span)
+
+        def masked_step(r, carry):
+            step(r, True)
+            return carry
+
+        def full_step(r, carry):
+            step(r, False)
+            return carry
+
+        lax.fori_loop(reach, past, masked_step, 0)
+        lax.fori_loop(past, SLOTS, full_step, 0)
+
+    tile_waits(dms, q, qsend, qrecv, chip, core, t)
+    for r in range(SLOTS):
+
+        @pl.when(served if r else jnp.logical_and(served, slot < 4))
+        def _():
+            q_cols[r] = both_maps(q[r].astype(F32).T).astype(BF)
+            dq_acc[r] = jnp.zeros((128, 2 * TILE), F32)
+            peaks[r, 0:1, :] = jnp.full((1, 2 * TILE), LOWEST, F32)
+            peaks[r, 1:2, :] = jnp.zeros((1, 2 * TILE), F32)
+
+    def pair_of(o):
+        return lax.rem(chip // 2 + o, CHIPS // 2)
+
+    def arrive(source):
+        pltpu.make_async_copy(kv_piece(0), kv.at[source], kvrecv.at[source]).wait()
+
+    def use(o):
+        pair = pair_of(o)
+        arrive(2 * pair + 1 - core)
+        start = pl.multiple_of(pair * KB, KB)
+        rows, blocks = pl.ds(start, KB), pl.ds(2 * pair, 2)
+        turned[:, rows] = matmul_t(unit, kv[blocks, :, 128:].reshape(KB, 128)).astype(BF)
+
+        def step(r, masked):
+            score = matmul(kv[blocks, :, :128].reshape(KB, 128), q_cols[r])
+            if masked:
+                score = jnp.where(key_mask(start, KB, tile_at(r), 2 * TILE), score, LOWEST)
+            old = peaks[r, 0:1, :]
+            peak = jnp.maximum(old, jnp.max(score, axis=0, keepdims=True))
+            shrink = jnp.exp2((old - peak) * SCORE)
+            prob = jnp.exp2((score - peak) * SCORE)
+            peaks[r, 0:1, :] = peak
+            peaks[r, 1:2, :] = peaks[r, 1:2, :] * shrink + jnp.sum(prob, axis=0, keepdims=True)
+            dq_acc[r] = dq_acc[r] * shrink + matmul(turned[:, rows], prob.astype(BF))
+
+        each_tile(pair, KB, step)
 
     @pl.when(served)
     def _():
-        peaks[...] = jnp.zeros_like(peaks)
-
         def take(o, carry):
-            source, cp = forward(o)
-            pltpu.make_async_copy(kv_piece(0), kv.at[source], kvrecv.at[source]).wait()
-            cp.start()
-            turn(source)
+            source = 2 * pair_of(o) + core
+            arrive(source)
+            view = kv.at[source]
+            remote(view, view, fsend.at[0], kvrecv.at[source], s + 1 - 2 * core, t).start()
+
+            @pl.when(o > 0)
+            def _():
+                use(o - 1)
+
             return carry
 
         lax.fori_loop(0, CHIPS // 2, take, 0)
 
-        def finish(o, carry):
-            source = lax.rem((chip // 2 + o) * 2 + 1 - core, CHIPS)
-            pltpu.make_async_copy(kv_piece(0), kv.at[source], kvrecv.at[source]).wait()
-            forward(o)[1].wait_send()
-            turn(source)
-            return carry
-
-        lax.fori_loop(0, CHIPS // 2, finish, 0)
-        for m in range(2):
-            kmax[m] = jnp.max(peaks[m : m + 1, :])
-
     quad_o.finish()
-    tile_waits(dms, q, qsend, qrecv, chip, core, t)
     ring_zn.start()
     ring_dout.start()
 
+    @pl.when(served)
+    def _():
+        use(CHIPS // 2 - 1)
+        passed = kv.at[pl.ds(0, CHIPS // 2)]
+        pltpu.make_async_copy(passed, passed, fsend.at[0]).wait()
+
     for r in range(SLOTS):
-        tile = tile_of(slot, r)
 
         @pl.when(served if r else jnp.logical_and(served, slot < 4))
         def _():
-            q_t = q[r].astype(F32).T
-            square = q_t * q_t
-            bound = SCORE * jnp.concatenate(
-                [
-                    jnp.sqrt(jnp.sum(square[:64], axis=0, keepdims=True) * kmax[0]),
-                    jnp.sqrt(jnp.sum(square[64:], axis=0, keepdims=True) * kmax[1]),
-                ],
-                axis=1,
-            )
-            q_both = both_maps(q_t).astype(BF)
-            front[...] = jnp.zeros_like(front)
-            total[...] = jnp.zeros_like(total)
-
-            def step(b, masked):
-                sums, out = None, None
-                for u in range(STEP // KB):
-                    start = pl.multiple_of(b * STEP + u * KB, KB)
-                    pair = pl.ds(b * (STEP // BLOCK) + u * (KB // BLOCK), KB // BLOCK)
-                    score = matmul(kv[pair, :, :128].reshape(KB, 128), q_both)
-                    prob = jnp.exp2(score * SCORE - bound)
-                    if masked:
-                        prob = jnp.where(key_mask(start, KB, tile, 2 * TILE), prob, 0.0)
-                    part = jnp.sum(prob.reshape(KB // 8, 8, 2 * TILE), axis=0)
-                    term = matmul(turned[:, pl.ds(start, KB)], prob.astype(BF))
-                    sums = part if sums is None else sums + part
-                    out = term if out is None else out + term
-                total[...] += sums
-                front[...] += out
-
-            full = tile * TILE // STEP
-
-            def body(b, carry):
-                step(b, False)
-                return carry
-
-            lax.fori_loop(0, full, body, 0)
-            step(full, True)
-            whole = jnp.sum(total[...], axis=0, keepdims=True)
-            parts = front[...] / whole
+            whole = peaks[r, 1:2, :]
+            parts = dq_acc[r] / whole
             parts_all[r] = parts
-            logs[r] = bound + jnp.log(whole) * LOG2E
+            logs[r] = peaks[r, 0:1, :] * SCORE + jnp.log(whole) * LOG2E
             rms, hat = group_norm(parts, lam)
             dq_out[r] = (hat * sub * OUT_SCALE).T.astype(BF)
-
 
     home_sends(dq_out, land, hsend, hrecv, chip, core, t, True)
     loads[0].wait()
@@ -771,7 +766,14 @@
     ring_xn.start()
     ring_mix.start()
     home_sends(dq_out, land, hsend, hrecv, chip, core, t, False)
-    kv_sends(False)
+    own_kv = jnp.logical_and(self_served, served)
+    for count, case in ((WORKERS - 1, own_kv), (WORKERS, jnp.logical_not(own_kv))):
+
+        @pl.when(case)
+        def _():
+            sent = kv.at[pl.ds(0, count)]
+            pltpu.make_async_copy(sent, sent, kvsend.at[0]).wait()
+
     tile_sends(dms, q, qsend, qrecv, chip, core, t, False)
     resid = x_ref[...] + jnp.concatenate([red.result(k) for k in range(NC)], axis=1)
     ffn_rms = rms_scale(resid)
@@ -853,31 +855,20 @@
         at = o % (2 * PER_SPAN)
         return remote(given.at[at], sib.at[o], dsend.at[at], drecv.at[o], s + 1 - 2 * core, t)
 
-    def to_home(o, start):
+    def to_home(o):
         target = 2 * (2 * o + core) + parity
-        spot = place_at
-        if start:
-
-            @pl.when(target == s)
-            def _():
-                pltpu.make_async_copy(both.at[o], home.at[spot], krecv.at[spot]).start()
+        spot = home.at[place_at]
+
+        @pl.when(target == s)
+        def _():
+            pltpu.make_async_copy(both.at[o], spot, krecv.at[0]).start()
 
         @pl.when(target != s)
         def _():
-            cp = remote(both.at[o], home.at[spot], ksend.at[o], krecv.at[spot], target, t)
-            if start:
-                cp.start()
-            else:
-                cp.wait_send()
-
-    def tile_at(r):
-        late = 4 + 10 * (r - 1) + jnp.where((r - 1) % 2 == 0, slot, 9 - slot)
-        return jnp.where(r == 0, slot, late)
+            remote(both.at[o], spot, ksend.at[0], krecv.at[0], target, t).start()
 
     @pl.when(served)
     def _():
-        unit = eye(128)
-
         def flip(b, carry):
             rows = pl.ds(pl.multiple_of(b * KB, KB), KB)
             block = kv[pl.ds(2 * b, 2), :, :128].reshape(KB, 128)
@@ -896,7 +887,7 @@
     for left in lefts:
         left.start()
     tile_waits(dms, dmix, tsend, trecv, chip, core, t)
-    send_down.each(True)
+    send_down.each()
     ring_ffn.finish()
     ring_gate.finish()
     block_grad(pgate, 0, lffn, lgate[...].reshape(4 * BLOCK, 512), 256)
@@ -906,7 +897,6 @@
         @pl.when(served if r else jnp.logical_and(served, slot < 4))
         def _():
             q_wide = q[r].astype(F32)
-            q_cols[r] = both_maps(q_wide.T).astype(BF)
             left = lax.broadcasted_iota(jnp.int32, q_wide.shape, 1) < 64
             q_rows[r] = jnp.concatenate(
                 [jnp.where(left, q_wide, 0.0), jnp.where(left, 0.0, q_wide)], axis=0
@@ -935,7 +925,7 @@
             o = PER_SPAN * lax.rem(chip + k, SPANS) + u
             to_sibling(o).wait_recv()
             both[o] = (both[o].astype(F32) + sib[o].astype(F32)).astype(BF)
-            to_home(o, True)
+            to_home(o)
 
     def span(k, carry):
         b = lax.rem(chip + k, SPANS)
@@ -960,22 +950,7 @@
             acc[:, 128:] += matmul(mixed, d_rows[r])
             dq_acc[r] += matmul(turned[:, rows], ds)
 
-        def masked_step(r, carry):
-            step(r, True)
-            return carry
-
-        def full_step(r, carry):
-            step(r, False)
-            return carry
-
-        reach, past = 0, 0
-        for r in range(SLOTS):
-            last = tile_of(slot, r) * TILE // SPAN
-            counts = (slot < 4) if r == 0 else True
-            reach += jnp.where(jnp.logical_and(counts, last >= b), 1, 0)
-            past += jnp.where(jnp.logical_and(counts, last > b), 1, 0)
-        lax.fori_loop(SLOTS - reach, SLOTS - past, masked_step, 0)
-        lax.fori_loop(SLOTS - past, SLOTS, full_step, 0)
+        each_tile(b, SPAN, step)
 
         @pl.when(k >= 2)
         def _():
@@ -1001,7 +976,7 @@
 
         @pl.when(k < 2)
         def _():
-            send_gate.some(8 * k, 8 * k + 8, True)
+            send_gate.some(8 * k, 8 * k + 8)
 
         return carry
 
@@ -1011,7 +986,7 @@
         @pl.when(k < EARLY_SPANS + 4)
         def _():
             at = 4 * (k - EARLY_SPANS)
-            send_up.some(at, at + 4, True)
+            send_up.some(at, at + 4)
 
         return carry
 
@@ -1021,14 +996,14 @@
 
     @pl.when(jnp.logical_not(served))
     def _():
-        send_gate.each(True)
+        send_gate.each()
 
     ring_up.finish()
     block_grad(pup, 0, lffn, lup[...].reshape(4 * BLOCK, 512), 256)
 
     @pl.when(jnp.logical_not(served))
     def _():
-        send_up.each(True)
+        send_up.each()
 
     @pl.when(served)
     def _():
@@ -1048,11 +1023,11 @@
         for u in range(2):
             dqkv_ref[0, u * 128 : (u + 1) * 128, j * 128 : (j + 1) * 128] = land[j, u]
     ring_q.start()
+    pltpu.make_async_copy(home, home, krecv.at[0]).wait()
     for j in range(3):
         total = jnp.zeros((BLOCK, 256), F32)
         for p in range(PER_HEAD):
             spot = j * PER_HEAD + p
-            pltpu.make_async_copy(both.at[0], home.at[spot], krecv.at[spot]).wait()
             total = total + home[spot].astype(F32)
         dqkv_ref[1, :, j * 128 : (j + 1) * 128] = total[:, :128].astype(BF)
         dqkv_ref[2, :, j * 128 : (j + 1) * 128] = total[:, 128:].astype(BF)
@@ -1098,7 +1073,7 @@
     block_grad(pqo, 0, ldout, rq[...].reshape(4 * BLOCK, 384), 384, 0, 384)
     ring_vx.finish()
     block_grad(pqo, 768, ldout, rvx[...].reshape(4 * BLOCK, 128), 384, 0, 384)
-    send_qo.each(True)
+    send_qo.each()
     ring_k.finish()
     block_grad(pkv, 0, ldout, rk[...].reshape(4 * BLOCK, 384), 384, 384, 384)
     for cp in first_sum:
@@ -1106,28 +1081,17 @@
     share = pl.ds(pl.multiple_of((2 * core + t) * 8, 8), 8)
     quarter[...] = (vec[share, :] + vecs[0, share, :]) + (vecs[1, share, :] + vecs[2, share, :])
 
-    def spread(k, start):
+    def spread(k, carry):
         to = 2 * lax.rem(chip + k, CHIPS) + core
-        cp = remote(quarter, quarters.at[chip], bsem.at[0, k], bsem.at[1, chip], to, t)
-        if start:
-            cp.start()
-        else:
-            cp.wait_send()
-
-    def spread_start(k, carry):
-        spread(k, True)
+        remote(quarter, quarters.at[chip], bsem.at[0], bsem.at[1], to, t).start()
         return carry
 
-    def spread_end(k, carry):
-        spread(k, False)
-        return carry
-
-    own = pltpu.make_async_copy(quarter, quarters.at[chip], bsem.at[1, chip])
+    own = pltpu.make_async_copy(quarter, quarters.at[chip], bsem.at[1])
     own.start()
-    lax.fori_loop(1, CHIPS, spread_start, 0)
+    lax.fori_loop(1, CHIPS, spread, 0)
     ring_vz.finish()
     block_grad(pkv, 384, ldout, rvz[...].reshape(4 * BLOCK, 256), 384, 384, 384)
-    send_kv.each(True)
+    send_kv.each()
 
     send_down.wait()
     for b in range(2):
@@ -1145,8 +1109,9 @@
     swap_copy = remote(swap.at[1 - core], swapped, swap_sem.at[0], swap_sem.at[1], sibling, t)
     swap_copy.start()
 
+    pltpu.make_async_copy(quarters, quarters, bsem.at[1]).wait()
+
     def collect(k, total):
-        pltpu.make_async_copy(quarter, quarters.at[k], bsem.at[1, k]).wait()
         return total + quarters[k]
 
     sums_ref[share, :] = lax.fori_loop(0, CHIPS, collect, jnp.zeros((8, 128), F32))
@@ -1178,7 +1143,7 @@
     ):
         ring.drain()
     for send in (send_gate, send_up, send_down, send_qo, send_kv):
-        send.each(False)
+        send.drain()
     home_sends(dq_out, land, gsend, grecv, chip, core, t, False)
     tile_sends(dms, dmix, tsend, trecv, chip, core, t, False)
     for gather in (gather_f, gather_r):
@@ -1192,17 +1157,19 @@
             for u in range(PER_SPAN):
                 to_sibling(PER_SPAN * lax.rem(chip + k, SPANS) + u).wait_send()
 
-        def last(o, carry):
-            to_home(o, False)
-            return carry
-
-        lax.fori_loop(0, CHIPS // 2, last, 0)
+    for count, case in ((CHIPS // 2 - 1, self_served), (CHIPS // 2, jnp.logical_not(self_served))):
+
+        @pl.when(jnp.logical_and(served, case))
+        def _():
+            sent = both.at[pl.ds(0, count)]
+            pltpu.make_async_copy(sent, sent, ksend.at[0]).wait()
 
     for cp in last_sum:
         cp.wait()
     for cp in first_sum:
         cp.wait_send()
-    lax.fori_loop(1, CHIPS, spread_end, 0)
+    others = quarters.at[pl.ds(0, CHIPS - 1)]
+    pltpu.make_async_copy(others, others, bsem.at[0]).wait()
     swap2_copy.wait()
     outs = ((gq_ref, 0), (gk_ref, 384), (gv_ref, 768), (go_ref, 1152))
     swap_out(swap2, swapped2, outs, 384, core)
@@ -1301,16 +1268,12 @@
             vm(half, BF),
             vm(half, BF),
             vm((3 * PER_HEAD, BLOCK, 256), BF),
-            vm((8, BLOCK), F32),
-            pltpu.SMEM((2,), F32),
-            vm((8, 2 * TILE), F32),
+            vm((SLOTS, 2, 2 * TILE), F32),
             *(REDUCE_SCRATCH * 2),
             *(GATHER_SEMS * 4),
             *(RING_SEMS * 12),
             *ONCE_SEMS,
-            *(scatter_sems(16) * 2),
-            *(scatter_sems(8) * 2),
-            *scatter_sems(16),
+            *(RING_SEMS * 5),
             sem((4,)),
             sem((SLOTS,)),
             sem((3, 2)),
@@ -1319,20 +1282,20 @@
             sem((2,)),
             sem((2 * PER_SPAN,)),
             sem((CHIPS // 2,)),
-            sem((CHIPS // 2,)),
-            sem((3 * PER_HEAD,)),
+            sem((1,)),
+            sem((1,)),
             sem((SLOTS,)),
             sem((3, 2)),
             sem((3,)),
             sem((2,)),
             sem((2,)),
             sem((2, 3)),
-            sem((2, CHIPS)),
+            sem((2,)),
             sem((2, 3)),
             sem((9,)),
-            sem((WORKERS,)),
+            sem((1,)),
             sem((CHIPS,)),
-            sem((CHIPS // 2,)),
+            sem((1,)),
             sem((6,)),
             sem((SLOTS,)),
         ],

time: 245 us -> 262 us (1.069)
  Pallas kernels: 239 us -> 257 us
    pallas_call x1, Pallas kernels: 236 us -> 254 us  [layer(): pl.pallas_call(layer_kernel, name='layer', out_shape=(shape((ROWS, D), F3...]
where the time goes in v7:
time: 262 us; the launch traced here: 258 us
  Pallas kernels  257 us (98%)
    pallas_call x1, Pallas kernels, layer(): pl.pallas_call(layer_kernel, name='layer', out_shape=(shape((ROWS, D), F3...  254 us

profile of v7, /device:TPU:31, one launch (start us, length us, event | category | flops | bytes accessed | tf_op | source)
XLA Modules:
  0.0 257.8 jit_solution(9153431847551464509)
XLA Ops:
  0.6 254.2 %layer.1 = (f32[64,1536]{1,0:T(8,128)}, f32[64,1536]{1,0:T(8,128)}, f32[24,768]{1,0:T(8,128)}, f32[24,768]{1,0:T(8,128)}, f32[24,768]{1,0:T(8,128)}, /*index=5*/...) custom-call(f32[64,1536]{1,0:T(8,128)} %x_ref.1, ...), custom_call_target="tpu_custom_call" | custom-call | tf_op jit(solution)/shard_map/layer/pallas_call | solution.py:1198
  254.9 2.7 %publish.1 = (f32[64,1536]{1,0:T(8,128)}, f32[64,1536]{1,0:T(8,128)}, f32[24,768]{1,0:T(8,128)}, f32[24,768]{1,0:T(8,128)}, f32[24,768]{1,0:T(8,128)}, /*index=5...) custom-call(f32[12,4,64]{2,1,0:T(4,128)} %bitcast.10, ...), custom_call_target="tpu_custom_call" | custom-call | tf_op jit(solution)/shard_map/publish/pallas_call | solution.py:1324

commit v8 on v7

--- a/solution.py
+++ b/solution.py
@@ -24,7 +24,6 @@
 KB = 512
 LOG2E = 1.4426950408889634
 SCORE = 0.125 * LOG2E
-LOWEST = -1e30
 VMEM_LIMIT = 63 * 2**20
 
 
@@ -510,7 +509,7 @@
     q, kv, parts_all, logs, dmix,
     lffn, lgate, lup, lhid, ldout, pgate, pup, pdown, sgate, sup, sdown, swap, swapped,
     turned, acc, q_cols, q_rows, d_cols, d_rows, deltas, dq_acc, dq_out, given, sib, both, home,
-    peaks, *rest,
+    crest, kmax, weights, *rest,
 ):
     chip, core, t = place()
     s = 2 * chip + core
@@ -681,79 +680,104 @@
         lax.fori_loop(reach, past, masked_step, 0)
         lax.fori_loop(past, SLOTS, full_step, 0)
 
-    tile_waits(dms, q, qsend, qrecv, chip, core, t)
-    for r in range(SLOTS):
-
-        @pl.when(served if r else jnp.logical_and(served, slot < 4))
-        def _():
-            q_cols[r] = both_maps(q[r].astype(F32).T).astype(BF)
-            dq_acc[r] = jnp.zeros((128, 2 * TILE), F32)
-            peaks[r, 0:1, :] = jnp.full((1, 2 * TILE), LOWEST, F32)
-            peaks[r, 1:2, :] = jnp.zeros((1, 2 * TILE), F32)
-
-    def pair_of(o):
-        return lax.rem(chip // 2 + o, CHIPS // 2)
+    def source_of(o, half):
+        return lax.rem((chip // 2 + o) * 2 + half, CHIPS)
 
     def arrive(source):
         pltpu.make_async_copy(kv_piece(0), kv.at[source], kvrecv.at[source]).wait()
 
-    def use(o):
-        pair = pair_of(o)
-        arrive(2 * pair + 1 - core)
-        start = pl.multiple_of(pair * KB, KB)
-        rows, blocks = pl.ds(start, KB), pl.ds(2 * pair, 2)
-        turned[:, rows] = matmul_t(unit, kv[blocks, :, 128:].reshape(KB, 128)).astype(BF)
-
-        def step(r, masked):
-            score = matmul(kv[blocks, :, :128].reshape(KB, 128), q_cols[r])
-            if masked:
-                score = jnp.where(key_mask(start, KB, tile_at(r), 2 * TILE), score, LOWEST)
-            old = peaks[r, 0:1, :]
-            peak = jnp.maximum(old, jnp.max(score, axis=0, keepdims=True))
-            shrink = jnp.exp2((old - peak) * SCORE)
-            prob = jnp.exp2((score - peak) * SCORE)
-            peaks[r, 0:1, :] = peak
-            peaks[r, 1:2, :] = peaks[r, 1:2, :] * shrink + jnp.sum(prob, axis=0, keepdims=True)
-            dq_acc[r] = dq_acc[r] * shrink + matmul(turned[:, rows], prob.astype(BF))
-
-        each_tile(pair, KB, step)
+    def turn(source):
+        both_t = matmul_t(eye(256), kv[source])
+        turned[:, pl.ds(pl.multiple_of(source * BLOCK, BLOCK), BLOCK)] = both_t[128:].astype(BF)
+        square = both_t[:128] * both_t[:128]
+        for m in range(2):
+            largest = jnp.sum(square[64 * m : 64 * m + 64], axis=0, keepdims=True)
+            crest[m : m + 1, :] = jnp.maximum(crest[m : m + 1, :], largest)
 
     @pl.when(served)
     def _():
+        crest[...] = jnp.zeros_like(crest)
+
         def take(o, carry):
-            source = 2 * pair_of(o) + core
+            source = source_of(o, core)
             arrive(source)
             view = kv.at[source]
             remote(view, view, fsend.at[0], kvrecv.at[source], s + 1 - 2 * core, t).start()
-
-            @pl.when(o > 0)
-            def _():
-                use(o - 1)
-
+            turn(source)
             return carry
 
         lax.fori_loop(0, CHIPS // 2, take, 0)
 
+        def take_passed(o, carry):
+            source = source_of(o, 1 - core)
+            arrive(source)
+            turn(source)
+            return carry
+
+        lax.fori_loop(0, CHIPS // 2, take_passed, 0)
+        for m in range(2):
+            kmax[m] = jnp.max(crest[m : m + 1, :])
+
     quad_o.finish()
+    tile_waits(dms, q, qsend, qrecv, chip, core, t)
     ring_zn.start()
     ring_dout.start()
+    front = dq_acc.at[0]
+
+    for r in range(SLOTS):
+        tile = tile_of(slot, r)
+
+        @pl.when(served if r else jnp.logical_and(served, slot < 4))
+        def _():
+            q_t = q[r].astype(F32).T
+            square = q_t * q_t
+            bound = SCORE * jnp.concatenate(
+                [
+                    jnp.sqrt(jnp.sum(square[:64], axis=0, keepdims=True) * kmax[0]),
+                    jnp.sqrt(jnp.sum(square[64:], axis=0, keepdims=True) * kmax[1]),
+                ],
+                axis=1,
+            )
+            q_both = both_maps(q_t).astype(BF)
+            q_cols[r] = q_both
+            front[...] = jnp.zeros((128, 2 * TILE), F32)
+            weights[...] = jnp.zeros_like(weights)
+
+            def step(b, masked):
+                sums, out = None, None
+                for u in range(STEP // KB):
+                    start = pl.multiple_of(b * STEP + u * KB, KB)
+                    pair = pl.ds(b * (STEP // BLOCK) + u * (KB // BLOCK), KB // BLOCK)
+                    score = matmul(kv[pair, :, :128].reshape(KB, 128), q_both)
+                    prob = jnp.exp2(score * SCORE - bound)
+                    if masked:
+                        prob = jnp.where(key_mask(start, KB, tile, 2 * TILE), prob, 0.0)
+                    part = jnp.sum(prob.reshape(KB // 8, 8, 2 * TILE), axis=0)
+                    term = matmul(turned[:, pl.ds(start, KB)], prob.astype(BF))
+                    sums = part if sums is None else sums + part
+                    out = term if out is None else out + term
+                weights[...] += sums
+                front[...] += out
+
+            full = tile * TILE // STEP
+
+            def body(b, carry):
+                step(b, False)
+                return carry
+
+            lax.fori_loop(0, full, body, 0)
+            step(full, True)
+            whole = jnp.sum(weights[...], axis=0, keepdims=True)
+            parts = front[...] / whole
+            parts_all[r] = parts
+            logs[r] = bound + jnp.log(whole) * LOG2E
+            rms, hat = group_norm(parts, lam)
+            dq_out[r] = (hat * sub * OUT_SCALE).T.astype(BF)
 
     @pl.when(served)
     def _():
-        use(CHIPS // 2 - 1)
         passed = kv.at[pl.ds(0, CHIPS // 2)]
         pltpu.make_async_copy(passed, passed, fsend.at[0]).wait()
-
-    for r in range(SLOTS):
-
-        @pl.when(served if r else jnp.logical_and(served, slot < 4))
-        def _():
-            whole = peaks[r, 1:2, :]
-            parts = dq_acc[r] / whole
-            parts_all[r] = parts
-            logs[r] = peaks[r, 0:1, :] * SCORE + jnp.log(whole) * LOG2E
-            rms, hat = group_norm(parts, lam)
-            dq_out[r] = (hat * sub * OUT_SCALE).T.astype(BF)
 
     home_sends(dq_out, land, hsend, hrecv, chip, core, t, True)
     loads[0].wait()
@@ -1067,6 +1091,19 @@
         cp.start()
     grad_ref[...] = dres[...] + norm_back(d_normed, long_row(attn_ref), rms, hat)
     results[1].start()
+    for cp in first_sum:
+        cp.wait_recv()
+    share = pl.ds(pl.multiple_of((2 * core + t) * 8, 8), 8)
+    quarter[...] = (vec[share, :] + vecs[0, share, :]) + (vecs[1, share, :] + vecs[2, share, :])
+
+    def spread(k, carry):
+        to = 2 * lax.rem(chip + k, CHIPS) + core
+        remote(quarter, quarters.at[chip], bsem.at[0], bsem.at[1], to, t).start()
+        return carry
+
+    own = pltpu.make_async_copy(quarter, quarters.at[chip], bsem.at[1])
+    own.start()
+    lax.fori_loop(1, CHIPS, spread, 0)
     for left in lefts:
         left.wait()
     ring_q.finish()
@@ -1076,19 +1113,6 @@
     send_qo.each()
     ring_k.finish()
     block_grad(pkv, 0, ldout, rk[...].reshape(4 * BLOCK, 384), 384, 384, 384)
-    for cp in first_sum:
-        cp.wait_recv()
-    share = pl.ds(pl.multiple_of((2 * core + t) * 8, 8), 8)
-    quarter[...] = (vec[share, :] + vecs[0, share, :]) + (vecs[1, share, :] + vecs[2, share, :])
-
-    def spread(k, carry):
-        to = 2 * lax.rem(chip + k, CHIPS) + core
-        remote(quarter, quarters.at[chip], bsem.at[0], bsem.at[1], to, t).start()
-        return carry
-
-    own = pltpu.make_async_copy(quarter, quarters.at[chip], bsem.at[1])
-    own.start()
-    lax.fori_loop(1, CHIPS, spread, 0)
     ring_vz.finish()
     block_grad(pkv, 384, ldout, rvz[...].reshape(4 * BLOCK, 256), 384, 384, 384)
     send_kv.each()
@@ -1268,7 +1292,9 @@
             vm(half, BF),
             vm(half, BF),
             vm((3 * PER_HEAD, BLOCK, 256), BF),
-            vm((SLOTS, 2, 2 * TILE), F32),
+            vm((8, BLOCK), F32),
+            pltpu.SMEM((2,), F32),
+            vm((8, 2 * TILE), F32),
             *(REDUCE_SCRATCH * 2),
             *(GATHER_SEMS * 4),
             *(RING_SEMS * 12),

time: 262 us -> 241 us (0.920); the launches traced: 258 us -> 241 us
  Pallas kernels: 257 us -> 240 us
    pallas_call x1, Pallas kernels: 254 us -> 237 us  [layer(): pl.pallas_call(layer_kernel, name='layer', out_shape=(shape((ROWS, D), F3...]
where the time goes in v8:
time: 241 us
  Pallas kernels  240 us (100%)
    pallas_call x1, Pallas kernels, layer(): pl.pallas_call(layer_kernel, name='layer', out_shape=(shape((ROWS, D), F3...  237 us

profile of v8, /device:TPU:31, one launch (start us, length us, event | category | flops | bytes accessed | tf_op | source)
XLA Modules:
  0.0 240.5 jit_solution(7215111249638398521)
XLA Ops:
  0.6 237.0 %layer.1 = (f32[64,1536]{1,0:T(8,128)}, f32[64,1536]{1,0:T(8,128)}, f32[24,768]{1,0:T(8,128)}, f32[24,768]{1,0:T(8,128)}, f32[24,768]{1,0:T(8,128)}, /*index=5*/...) custom-call(f32[64,1536]{1,0:T(8,128)} %x_ref.1, ...), custom_call_target="tpu_custom_call" | custom-call | tf_op jit(solution)/shard_map/layer/pallas_call | solution.py:1222
  237.6 2.7 %publish.1 = (f32[64,1536]{1,0:T(8,128)}, f32[64,1536]{1,0:T(8,128)}, f32[24,768]{1,0:T(8,128)}, f32[24,768]{1,0:T(8,128)}, f32[24,768]{1,0:T(8,128)}, /*index=5...) custom-call(f32[12,4,64]{2,1,0:T(4,128)} %bitcast.10, ...), custom_call_target="tpu_custom_call" | custom-call | tf_op jit(solution)/shard_map/publish/pallas_call | solution.py:1350

commit v9 on v8

--- a/solution.py
+++ b/solution.py
@@ -494,7 +494,7 @@
 SPAN = 1024
 SPANS = CHIPS * BLOCK // SPAN
 PER_SPAN = SPAN // BLOCK // 2
-EARLY_SPANS = 3
+EARLY_SPANS = 5
 
 
 def layer_kernel(
@@ -649,7 +649,6 @@
             dqkv_ref[j, :, k * 128 : (k + 1) * 128] = value[:, j * 128 : (j + 1) * 128]
 
     kv_sends()
-    quad_o.start()
     for load in loads[1:]:
         load.start()
 
@@ -718,14 +717,16 @@
         for m in range(2):
             kmax[m] = jnp.max(crest[m : m + 1, :])
 
-    quad_o.finish()
+    quad_o.start()
     tile_waits(dms, q, qsend, qrecv, chip, core, t)
     ring_zn.start()
-    ring_dout.start()
     front = dq_acc.at[0]
 
     for r in range(SLOTS):
         tile = tile_of(slot, r)
+        if r == 4:
+            quad_o.finish()
+            ring_dout.start()
 
         @pl.when(served if r else jnp.logical_and(served, slot < 4))
         def _():
@@ -804,6 +805,17 @@
     ffn_hat = resid * ffn_rms
     fbuf[mine, :] = (ffn_hat * ffn_gain).astype(BF)
     gather_f.start()
+
+    @pl.when(served)
+    def _():
+        def flip(b, carry):
+            rows = pl.ds(pl.multiple_of(b * KB, KB), KB)
+            block = kv[pl.ds(2 * b, 2), :, :128].reshape(KB, 128)
+            turned[:, rows] = matmul_t(unit, block).astype(BF)
+            return carry
+
+        lax.fori_loop(0, CHIPS * BLOCK // KB, flip, 0)
+
     for load in loads[1:]:
         load.wait()
     red.drain()
@@ -870,8 +882,6 @@
         for u in range(2):
             dms[j, u] = d_mixed[u * 128 : (u + 1) * 128, j * 128 : (j + 1) * 128]
     tile_sends(dms, dmix, tsend, trecv, chip, core, t, True)
-    ring_up.start()
-    ring_dres.start()
     out_ref[...] = resid + jnp.concatenate([red3.result(k) for k in range(NC)], axis=1)
     results[0].start()
 
@@ -890,16 +900,6 @@
         @pl.when(target != s)
         def _():
             remote(both.at[o], spot, ksend.at[0], krecv.at[0], target, t).start()
-
-    @pl.when(served)
-    def _():
-        def flip(b, carry):
-            rows = pl.ds(pl.multiple_of(b * KB, KB), KB)
-            block = kv[pl.ds(2 * b, 2), :, :128].reshape(KB, 128)
-            turned[:, rows] = matmul_t(unit, block).astype(BF)
-            return carry
-
-        lax.fori_loop(0, CHIPS * BLOCK // KB, flip, 0)
 
     ring_dout.finish()
     ring_hid.finish()
@@ -911,6 +911,8 @@
     for left in lefts:
         left.start()
     tile_waits(dms, dmix, tsend, trecv, chip, core, t)
+    ring_up.start()
+    ring_dres.start()
     send_down.each()
     ring_ffn.finish()
     ring_gate.finish()
@@ -1007,11 +1009,8 @@
     def late(k, carry):
         span(k, carry)
 
-        @pl.when(k < EARLY_SPANS + 4)
-        def _():
-            at = 4 * (k - EARLY_SPANS)
-            send_up.some(at, at + 4)
-
+        at = 6 * (k - EARLY_SPANS)
+        send_up.some(at, jnp.minimum(at + 6, 16))
         return carry
 
     @pl.when(served)

time: 241 us -> 260 us (1.079)
  the two profiles are of different devices: /device:TPU:31 before, /device:TPU:101 now
where the time goes in v9:
time: 260 us
  Pallas kernels  259 us (100%)
    pallas_call x1, Pallas kernels, layer(): pl.pallas_call(layer_kernel, name='layer', out_shape=(shape((ROWS, D), F3...  256 us

profile of v9, /device:TPU:101, one launch (start us, length us, event | category | flops | bytes accessed | tf_op | source)
XLA Modules:
  0.0 259.5 jit_solution(9955665974444895796)
XLA Ops:
  0.6 256.0 %layer.1 = (f32[64,1536]{1,0:T(8,128)}, f32[64,1536]{1,0:T(8,128)}, f32[24,768]{1,0:T(8,128)}, f32[24,768]{1,0:T(8,128)}, f32[24,768]{1,0:T(8,128)}, /*index=5*/...) custom-call(f32[64,1536]{1,0:T(8,128)} %x_ref.1, ...), custom_call_target="tpu_custom_call" | custom-call | tf_op jit(solution)/shard_map/layer/pallas_call | solution.py:1221
  256.6 2.7 %publish.1 = (f32[64,1536]{1,0:T(8,128)}, f32[64,1536]{1,0:T(8,128)}, f32[24,768]{1,0:T(8,128)}, f32[24,768]{1,0:T(8,128)}, f32[24,768]{1,0:T(8,128)}, /*index=5...) custom-call(f32[12,4,64]{2,1,0:T(4,128)} %bitcast.10, ...), custom_call_target="tpu_custom_call" | custom-call | tf_op jit(solution)/shard_map/publish/pallas_call | solution.py:1349
